TPU v7x, 32 devices: a whole 2x2x4 slice. The times are simulated.
32 devices in a mesh: samples: 4 (over z), rows: 8 (over y, x, core).
Axes of the slice: x: 2, y: 2, z: 4, core: 2. Of those that a mesh axis runs over, the one named last changes fastest.
Arguments:
- x_big: bfloat16 [112, 4, 48, 16384], P('samples', None, None, 'rows'), may hold values from -6 to 6
- x_small: bfloat16 [8, 4, 48, 4096], P('samples', None, None, 'rows'), may hold values from -6 to 6
- spec_weight: bfloat16 [256, 4, 48, 48], P('rows'), may hold values from -0.4375 to 0.4375
- lin_weight: bfloat16 [4, 48, 48], replicated, may hold values from -0.4375 to 0.4375
- lin_bias: bfloat16 [4, 48], replicated, may hold values from -3 to 3
- grad_big: bfloat16 [112, 4, 48, 16384], P('samples', None, None, 'rows'), may hold values from -6 to 6
- grad_small: bfloat16 [8, 4, 48, 4096], P('samples', None, None, 'rows'), may hold values from -6 to 6
Outputs:
- out_big: bfloat16 [112, 4, 48, 16384], P('samples', None, None, 'rows')
- out_small: bfloat16 [8, 4, 48, 4096], P('samples', None, None, 'rows')
- dx_big: float32 [112, 4, 48, 16384], P('samples', None, None, 'rows')
- dx_small: float32 [8, 4, 48, 4096], P('samples', None, None, 'rows')
- d_spec_weight: float32 [256, 4, 48, 48], P('rows')
- d_lin_weight: float32 [4, 48, 48], replicated
- d_lin_bias: float32 [4, 48], replicated
All inputs are finite; a program needn't handle non-finite values.
Results may differ from a plain program's by a relative error of at most 0.014.
Values may be sent and summed in bfloat16 or wider, within the bound.
A program may use at most 384 MiB of HBM per device.

v0:
```python
import math

import jax
import jax.numpy as jnp
from jax import lax
from jax.sharding import PartitionSpec as P

C = 48
MX = 16
N1 = 128
N2 = 64


def kept_freqs(mode_ids, grid_side):
    return jnp.where(mode_ids < MX // 2, mode_ids, grid_side - MX + mode_ids)


def trig_pair(phases, grid_side):
    angles = phases.astype(jnp.float32) * (2.0 * math.pi / grid_side)
    return (jnp.cos(angles).astype(jnp.bfloat16), jnp.sin(angles).astype(jnp.bfloat16))


def combine(leading, second, sign_flip, axis_at):
    left_parts = [
        lax.index_in_dim(leading, blade_id, axis_at, keepdims=False) for blade_id in range(4)
    ]
    right_parts = [
        lax.index_in_dim(second, blade_id, axis_at, keepdims=False) for blade_id in range(4)
    ]
    return jnp.stack(
        [
            left_parts[0] + sign_flip * right_parts[3],
            left_parts[1] + sign_flip * right_parts[2],
            left_parts[2] - sign_flip * right_parts[1],
            left_parts[3] - sign_flip * right_parts[0],
        ],
        axis=axis_at,
    )


def build_kernel(weights):
    rows_list = []
    for source in range(4):
        blocks = []
        for target in range(4):
            blade_id = source ^ target
            block_part = weights[..., blade_id, :, :]
            if blade_id >> 1 & source & 1:
                block_part = -block_part
            blocks.append(block_part)
        rows_list.append(jnp.concatenate(blocks, axis=-1))
    return jnp.concatenate(rows_list, axis=-2)


def fold_kernel(kernel_grad):
    blades = []
    for blade_id in range(4):
        summed = None
        for source in range(4):
            target = source ^ blade_id
            block_part = kernel_grad[
                ..., source * C : (source + 1) * C, target * C : (target + 1) * C
            ]
            if blade_id >> 1 & source & 1:
                block_part = -block_part
            summed = block_part if summed is None else summed + block_part
        blades.append(summed)
    return jnp.stack(blades, axis=-3)


def dual_einsum(pattern, operand, tables):
    return (
        jnp.einsum(pattern, operand, tables[0], preferred_element_type=jnp.float32),
        jnp.einsum(pattern, operand, tables[1], preferred_element_type=jnp.float32),
    )


def on_device(x_big, x_small, spec_weight, lin_weight, lin_bias, grad_big, grad_small):
    comp_width = 4 * C
    row_index = lax.axis_index("rows")
    own_count = spec_weight.shape[0]
    mode_ids = jnp.arange(MX, dtype=jnp.int32)
    own_modes = row_index * own_count + jnp.arange(own_count, dtype=jnp.int32)
    own_onehot = (mode_ids[:, None] == (own_modes % MX)[None, :]).astype(jnp.bfloat16)
    bundles = []
    for grid_field, cotangent, grid_side in ((x_big, grad_big, N1), (x_small, grad_small, N2)):
        samples = grid_field.shape[0]
        rows_local = grid_field.shape[3] // grid_side
        frequencies = kept_freqs(mode_ids, grid_side)
        cell_ids = jnp.arange(grid_side, dtype=jnp.int32)
        row_ids = row_index * rows_local + jnp.arange(rows_local, dtype=jnp.int32)
        bundles.append(
            {
                "field": grid_field.reshape(samples, comp_width, rows_local * grid_side),
                "cotangent": cotangent.astype(jnp.float32).reshape(
                    samples, comp_width, rows_local * grid_side
                ),
                "initial": grid_field.shape,
                "side": grid_side,
                "rows": rows_local,
                "samples": samples,
                "columns": trig_pair(
                    cell_ids[:, None] * frequencies[None, :] % grid_side, grid_side
                ),
                "local": trig_pair(row_ids[:, None] * frequencies[None, :] % grid_side, grid_side),
            }
        )
    total_samples = sum((bundle["samples"] for bundle in bundles))
    columns = []
    for bundle in bundles:
        shaped = bundle["field"].reshape(bundle["samples"], 4, C, bundle["rows"], bundle["side"])
        column = combine(*dual_einsum("sbchw,wk->shkbc", shaped, bundle["columns"]), 1.0, 3)
        columns.append((column * (1.0 / bundle["side"])).astype(jnp.bfloat16))

    def owner_fold(totals, pieces):
        results = []
        for shard_piece, bundle in zip(pieces, bundles):
            grid_side, rows_local = (bundle["side"], bundle["rows"])
            frequency = kept_freqs(own_modes // MX, grid_side)
            row_ids = (
                jnp.arange(shard_piece.shape[0], dtype=jnp.int32)[:, None] * rows_local
                + jnp.arange(rows_local, dtype=jnp.int32)[None, :]
            )
            cos_part, sin_part = trig_pair(
                row_ids[:, :, None] * frequency[None, None, :] % grid_side, grid_side
            )
            tables = (
                cos_part[:, :, None, :] * own_onehot[None, None],
                sin_part[:, :, None, :] * own_onehot[None, None],
            )
            results.append(combine(*dual_einsum("jsrkbc,jrki->isbc", shard_piece, tables), 1.0, 2))
        return jnp.concatenate(results, axis=1).reshape(totals.shape)

    owner_zero = jnp.zeros((own_count, total_samples, comp_width), jnp.float32)
    spectrum = owner_fold(
        owner_zero,
        (
            lax.all_gather(columns[0][None], "rows", axis=0, tiled=True),
            lax.all_gather(columns[1][None], "rows", axis=0, tiled=True),
        ),
    )
    spectrum = spectrum.astype(jnp.bfloat16)
    kernel = build_kernel(spec_weight)
    mixed_modes = jnp.einsum(
        "msi,mio->mso", spectrum, kernel, preferred_element_type=jnp.float32
    ).astype(jnp.bfloat16)

    def mode_fold(totals, shard_piece):
        piece_modes = jnp.arange(shard_piece.shape[0], dtype=jnp.int32)
        onehot = ((piece_modes % MX)[:, None] == mode_ids[None, :]).astype(jnp.bfloat16)
        updated = []
        first_sample = 0
        for summed, bundle in zip(totals, bundles):
            grid_side, rows_local, samples = (bundle["side"], bundle["rows"], bundle["samples"])
            sample_part = shard_piece[:, first_sample : first_sample + samples]
            first_sample += samples
            frequency = kept_freqs(piece_modes // MX, grid_side)
            row_ids = row_index * rows_local + jnp.arange(rows_local, dtype=jnp.int32)
            cos_part, sin_part = trig_pair(
                frequency[:, None] * row_ids[None, :] % grid_side, grid_side
            )
            tables = (
                cos_part[:, :, None] * onehot[:, None, :],
                sin_part[:, :, None] * onehot[:, None, :],
            )
            leading, second = dual_einsum("msx,mhk->shkx", sample_part, tables)
            block_shape = (samples, rows_local, MX, 4, C)
            updated.append(
                combine(leading.reshape(block_shape), second.reshape(block_shape), -1.0, 3)
            )
        return tuple(updated)

    zero_rows = tuple(
        (
            jnp.zeros((bundle["samples"], bundle["rows"], MX, 4, C), jnp.float32)
            for bundle in bundles
        )
    )
    rows_back = mode_fold(zero_rows, lax.all_gather(mixed_modes, "rows", axis=0, tiled=True))
    lin_kernel = build_kernel(lin_weight)
    bias_row = lin_bias.astype(jnp.float32).reshape(comp_width)
    lin_total = jnp.zeros((comp_width, comp_width), jnp.float32)
    bias_total = jnp.zeros((comp_width,), jnp.float32)
    outputs = []
    linear_backs = []
    row_grads = []
    for bundle, back_summed in zip(bundles, rows_back):
        samples, cell_count = (bundle["samples"], bundle["rows"] * bundle["side"])
        back_rounded = (back_summed * (1.0 / MX)).astype(jnp.bfloat16)
        spectral = combine(
            *dual_einsum("shkbc,wk->sbchw", back_rounded, bundle["columns"]), -1.0, 1
        ).reshape(samples, comp_width, cell_count)
        linear = jnp.einsum(
            "sin,io->son", bundle["field"], lin_kernel, preferred_element_type=jnp.float32
        )
        before = spectral + linear + bias_row[None, :, None]
        activated, gelu_back = jax.vjp(jax.nn.gelu, before)
        outputs.append(
            (bundle["field"].astype(jnp.float32) + activated)
            .astype(jnp.bfloat16)
            .reshape(bundle["initial"])
        )
        pre_grad = gelu_back(bundle["cotangent"])[0].astype(jnp.bfloat16)
        bias_total = bias_total + jnp.sum(pre_grad, axis=(0, 2), dtype=jnp.float32)
        lin_total = lin_total + jnp.einsum(
            "sin,son->io", bundle["field"], pre_grad, preferred_element_type=jnp.float32
        )
        linear_backs.append(
            jnp.einsum("son,io->sin", pre_grad, lin_kernel, preferred_element_type=jnp.float32)
        )
        shaped = pre_grad.reshape(samples, 4, C, bundle["rows"], bundle["side"])
        row_grads.append(
            combine(*dual_einsum("sbchw,wk->shkbc", shaped, bundle["columns"]), 1.0, 3).astype(
                jnp.bfloat16
            )
        )
    owned_sum = owner_fold(
        owner_zero,
        (
            lax.all_gather(row_grads[0][None], "rows", axis=0, tiled=True),
            lax.all_gather(row_grads[1][None], "rows", axis=0, tiled=True),
        ),
    )
    mode_grad = (owned_sum * (1.0 / MX)).astype(jnp.bfloat16)
    kernel_grad = jnp.einsum(
        "msi,mso->mio", spectrum, mode_grad, preferred_element_type=jnp.float32
    )
    spec_grad = lax.psum(fold_kernel(kernel_grad).astype(jnp.bfloat16), "samples").astype(
        jnp.float32
    )
    spectrum_grad = jnp.einsum(
        "mso,mio->msi", mode_grad, kernel, preferred_element_type=jnp.float32
    ).astype(jnp.bfloat16)
    column_grads = mode_fold(zero_rows, lax.all_gather(spectrum_grad, "rows", axis=0, tiled=True))
    input_grads = []
    for bundle, column_grad, linear_back in zip(bundles, column_grads, linear_backs):
        samples, cell_count = (bundle["samples"], bundle["rows"] * bundle["side"])
        spec_back = combine(
            *dual_einsum("shkbc,wk->sbchw", column_grad.astype(jnp.bfloat16), bundle["columns"]),
            -1.0,
            1
        )
        spec_back = spec_back.reshape(samples, comp_width, cell_count) * (1.0 / bundle["side"])
        input_grad = bundle["cotangent"] + spec_back + linear_back
        input_grads.append(input_grad.reshape(bundle["initial"]))
    lin_grads = lax.psum((fold_kernel(lin_total), bias_total.reshape(4, C)), ("samples", "rows"))
    return (
        outputs[0],
        outputs[1],
        input_grads[0],
        input_grads[1],
        spec_grad,
        lin_grads[0],
        lin_grads[1],
    )


def solution(mesh):
    placed = (
        P("samples", None, None, "rows"),
        P("samples", None, None, "rows"),
        P("rows", None, None, None),
        P(),
        P(),
        P("samples", None, None, "rows"),
        P("samples", None, None, "rows"),
    )
    return jax.shard_map(
        on_device,
        mesh=mesh,
        in_specs=placed,
        out_specs=(
            P("samples", None, None, "rows"),
            P("samples", None, None, "rows"),
            P("samples", None, None, "rows"),
            P("samples", None, None, "rows"),
            P("rows", None, None, None),
            P(),
            P(),
        ),
        check_vma=False,
    )
```

profile of v0, /device:TPU:0, one launch (start us, length us, event | category | flops | bytes accessed | tf_op | source)
XLA Modules:
  0.0 1869.7 jit_solution(5129793340586270434)
XLA Ops:
  56.6 28.7 %fusion.45 = f32[28,16,16,4,48]{4,2,1,0,3:T(8,128)} fusion(bf16[28,4,48,16,128]{4,3,2,1,0:T(8,128)(2,1)} %bitcast.523, s32[16]{0:T(128)S(1)} %compare_select_fusion.5), kind=kOutput, calls=%fused_computation.65 | convolution fusion | flops 352352256 | bytes 27525184 | tf_op jit(solution)/shard_map/sbchw,wk->shkbc/dot_general | solution.py:74
  133.4 241.2 %all-gather.5.cloned.1.call-done = bf16[8,28,16,16,4,48]{5,3,4,2,1,0:T(8,128)(2,1)} async-done(((bf16[1,28,16,16,4,48]{5,3,4,2,1,0:T(8,128)(2,1)}), bf16[8,28,16,16,4,48]{5,3,4,2,1,0:T(8,128)(2,1)}) %all-gather.5.cloned.1.call-update) | async-done | bytes 22020112 | tf_op jit(solution)/shard_map/all_gather | solution.py:138
  374.6 52.7 %fusion.81 = f32[32,28,4,48]{3,0,2,1:T(8,128)S(1)} fusion(bf16[8,28,16,16,4,48]{5,3,4,2,1,0:T(8,128)(2,1)} %all-gather.5.cloned.1.call-done, bf16[8,16,32]{2,1,0:T(8,128)(2,1)S(1)} %get-tuple-element.129, bf16[16,32]{1,0:T(8,128)(2,1)S(1)} %fusion.262), kind=kOutput, calls=%fused_computation.130 | convolution fusion | flops 704905216 | bytes 22717440 | tf_op jit(solution)/shard_map/jsrkbc,jrki->isbc/dot_general | solution.py:74
  427.4 52.7 %fusion.78 = f32[32,28,4,48]{3,0,2,1:T(8,128)S(1)} fusion(bf16[8,28,16,16,4,48]{5,3,4,2,1,0:T(8,128)(2,1)} %all-gather.5.cloned.1.call-done, bf16[16,32]{1,0:T(8,128)(2,1)S(1)} %fusion.262, bf16[8,16,32]{2,1,0:T(8,128)(2,1)S(1)} %get-tuple-element.128), kind=kOutput, calls=%fused_computation.129 | convolution fusion | flops 704905216 | bytes 22717440 | tf_op jit(solution)/shard_map/jsrkbc,jrki->isbc/dot_general | solution.py:73
  490.9 32.7 %all-gather.7.cloned.1.call-done = bf16[256,30,192]{2,0,1:T(8,128)(2,1)} async-done(((bf16[32,30,192]{2,0,1:T(8,128)(2,1)}), bf16[256,30,192]{2,0,1:T(8,128)(2,1)}) %all-gather.7.cloned.1.call-update) | async-done | bytes 2949136 | tf_op jit(solution)/shard_map/all_gather | solution.py:179
  543.6 29.5 %fusion.359 = (f32[28,16,16,1,48]{4,3,2,0,1:T(1,128)}, f32[28,16,16,1,48]{4,3,2,0,1:T(1,128)}, f32[28,16,16,1,48]{4,3,2,0,1:T(1,128)}, f32[28,16,16,1,48]{4,3,2,0,1:T(1,128)}) fusion(f32[28,16,16,4,48]{4,3,2,0,1:T(4,128)} %reshape.690), kind=kLoop, calls=%fused_computation.568 | loop fusion | bytes 11010048 | tf_op jit(solution)/shard_map/slice | solution.py:25
  593.3 29.6 %fusion.360 = (f32[28,16,16,1,48]{4,3,2,0,1:T(1,128)}, f32[28,16,16,1,48]{4,3,2,0,1:T(1,128)}, f32[28,16,16,1,48]{4,3,2,0,1:T(1,128)}, f32[28,16,16,1,48]{4,3,2,0,1:T(1,128)}) fusion(f32[28,16,16,4,48]{4,3,2,0,1:T(4,128)} %reshape.691), kind=kLoop, calls=%fused_computation.569 | loop fusion | bytes 11010048 | tf_op jit(solution)/shard_map/slice | solution.py:28
  666.5 45.2 %fusion.38 = (f32[28,1,48,16,128]{4,2,1,3,0:T(8,128)}, f32[28,1,48,16,128]{4,2,1,3,0:T(8,128)}, f32[28,1,48,16,128]{4,2,1,3,0:T(8,128)}, f32[28,1,48,16,128]{4,2,1,3,0:T(8,128)}) fusion(f32[28,4,48,16,128]{4,2,1,3,0:T(8,128)} %convolution_bitcast_fusion.2, f32[28,4,48,16,128]{4,2,1,3,0:T(8,128)} %convolution_bitcast_fusion.3), kind=kLoop, calls=%fused_computation.62 | loop fusion | flops 22020096 | bytes 132120576 | tf_op jit(solution)/shard_map/add | solution.py:32
  711.7 31.6 %pad_maximum_fusion = f32[28,4,48,16,128]{4,2,1,3,0:T(8,128)} fusion(f32[28,1,48,16,128]{4,2,1,3,0:T(8,128)} %get-tuple-element.35, f32[28,1,48,16,128]{4,2,1,3,0:T(8,128)} %get-tuple-element.36, f32[28,1,48,16,128]{4,2,1,3,0:T(8,128)} %get-tuple-element.37, f32[28,1,48,16,128]{4,2,1,3,0:T(8,128)} %get-tuple-element.34), kind=kLoop, calls=%fused_computation.24 | loop fusion | flops 33030144 | bytes 88080384 | tf_op jit(solution)/shard_map/stack | solution.py:30
  743.2 43.3 %copy.224 = f32[28,4,48,16,128]{4,3,2,1,0:T(8,128)} copy(f32[28,4,48,16,128]{4,2,1,3,0:T(8,128)} %pad_maximum_fusion) | data formatting | bytes 88080384 | tf_op jit(solution)/shard_map/stack | solution.py:30
  786.5 46.4 %reshape.692 = f32[28,192,2048]{2,1,0:T(8,128)} reshape(f32[28,4,48,16,128]{4,3,2,1,0:T(8,128)} %copy.224) | data formatting | bytes 88080384 | tf_op jit(solution)/shard_map/reshape | solution.py:192
  833.0 66.3 %fusion.14 = (bf16[28,192,2048]{2,1,0:T(8,128)(2,1)}, bf16[28,192,2048]{2,1,0:T(8,128)(2,1)}) fusion(bf16[28,4,48,2048]{3,2,1,0:T(8,128)(2,1)} %param.12, bf16[28,4,48,2048]{3,2,1,0:T(8,128)(2,1)} %param.7, f32[192]{0:T(256)S(1)} %copy-done.61, f32[28,192,2048]{2,1,0:T(8,128)} %reshape.692, bf16[28,192,2048]{2,1,0:T(8,128)(2,1)} %bitcast.521, ...), kind=kOutput, calls=%fused_computation.19 | convolution fusion | flops 4526309376 | bytes 154169088 | tf_op jit(solution)/shard_map/sin,io->son/dot_general | solution.py:193
  1035.0 235.8 %all-gather.9.cloned.1.call-done = bf16[8,28,16,16,4,48]{5,3,4,2,1,0:T(8,128)(2,1)} async-done(((bf16[1,28,16,16,4,48]{5,3,4,2,1,0:T(8,128)(2,1)}), bf16[8,28,16,16,4,48]{5,3,4,2,1,0:T(8,128)(2,1)}) %all-gather.9.cloned.1.call-update) | async-done | bytes 22020112 | tf_op jit(solution)/shard_map/all_gather | solution.py:220
  1270.9 52.4 %fusion.87 = f32[32,28,4,48]{3,0,2,1:T(8,128)S(1)} fusion(bf16[8,28,16,16,4,48]{5,3,4,2,1,0:T(8,128)(2,1)} %all-gather.9.cloned.1.call-done, bf16[8,16,32]{2,1,0:T(8,128)(2,1)S(1)} %copy-done.34, bf16[16,32]{1,0:T(8,128)(2,1)S(1)} %copy-done.21), kind=kOutput, calls=%fused_computation.132 | convolution fusion | flops 704905216 | bytes 22717440 | tf_op jit(solution)/shard_map/jsrkbc,jrki->isbc/dot_general | solution.py:74
  1323.3 52.9 %fusion.84 = f32[32,28,4,48]{3,0,2,1:T(8,128)S(1)} fusion(bf16[8,28,16,16,4,48]{5,3,4,2,1,0:T(8,128)(2,1)} %all-gather.9.cloned.1.call-done, bf16[16,32]{1,0:T(8,128)(2,1)S(1)} %copy-done.21, bf16[8,16,32]{2,1,0:T(8,128)(2,1)S(1)} %copy-done.32), kind=kOutput, calls=%fused_computation.131 | convolution fusion | flops 704905216 | bytes 22717440 | tf_op jit(solution)/shard_map/jsrkbc,jrki->isbc/dot_general | solution.py:73
  1413.8 42.4 %all-reduce = (f32[4,48,48]{1,2,0:T(8,128)S(1)}, f32[4,48]{1,0:T(4,128)}) all-reduce(f32[4,48,48]{1,2,0:T(8,128)S(1)} %pad_maximum_fusion.9, f32[4,48]{1,0:T(4,128)S(1)} %add.688), channel_id=1, replica_groups=mesh['samples'=4,'rows'=8] {'samples','rows'}, use_global_device_ids=true, to_apply=%region_1.2 | all-reduce | flops 9408 | bytes 75264 | tf_op jit(solution)/shard_map/psum | solution.py:246
  1460.4 30.9 %all-gather.11.cloned.1.call-done = bf16[256,30,192]{2,0,1:T(8,128)(2,1)} async-done(((bf16[32,30,192]{2,0,1:T(8,128)(2,1)}), bf16[256,30,192]{2,0,1:T(8,128)(2,1)}) %all-gather.11.cloned.1.call-update) | async-done | bytes 2949136 | tf_op jit(solution)/shard_map/all_gather | solution.py:234
  1515.5 29.4 %fusion.357 = (f32[28,16,16,1,48]{4,3,2,0,1:T(1,128)}, f32[28,16,16,1,48]{4,3,2,0,1:T(1,128)}, f32[28,16,16,1,48]{4,3,2,0,1:T(1,128)}, f32[28,16,16,1,48]{4,3,2,0,1:T(1,128)}) fusion(f32[28,16,16,4,48]{4,3,2,0,1:T(4,128)} %reshape.747), kind=kLoop, calls=%fused_computation.566 | loop fusion | bytes 11010048 | tf_op jit(solution)/shard_map/slice | solution.py:25
  1565.0 29.7 %fusion.358 = (f32[28,16,16,1,48]{4,3,2,0,1:T(1,128)}, f32[28,16,16,1,48]{4,3,2,0,1:T(1,128)}, f32[28,16,16,1,48]{4,3,2,0,1:T(1,128)}, f32[28,16,16,1,48]{4,3,2,0,1:T(1,128)}) fusion(f32[28,16,16,4,48]{4,3,2,0,1:T(4,128)} %reshape.748), kind=kLoop, calls=%fused_computation.567 | loop fusion | bytes 11010048 | tf_op jit(solution)/shard_map/slice | solution.py:28
  1651.8 45.1 %fusion.34 = (f32[28,1,48,16,128]{4,2,1,3,0:T(8,128)}, f32[28,1,48,16,128]{4,2,1,3,0:T(8,128)}, f32[28,1,48,16,128]{4,2,1,3,0:T(8,128)}, f32[28,1,48,16,128]{4,2,1,3,0:T(8,128)}) fusion(f32[28,4,48,16,128]{4,2,1,3,0:T(8,128)} %convolution_bitcast_fusion, f32[28,4,48,16,128]{4,2,1,3,0:T(8,128)} %convolution_bitcast_fusion.1), kind=kLoop, calls=%fused_computation.54 | loop fusion | flops 22020096 | bytes 132120576 | tf_op jit(solution)/shard_map/add | solution.py:32
  1697.0 31.7 %maximum_multiply_fusion = f32[28,4,48,16,128]{4,2,1,3,0:T(8,128)} fusion(f32[28,1,48,16,128]{4,2,1,3,0:T(8,128)} %get-tuple-element.31, f32[28,1,48,16,128]{4,2,1,3,0:T(8,128)} %get-tuple-element.32, f32[28,1,48,16,128]{4,2,1,3,0:T(8,128)} %get-tuple-element.33, f32[28,1,48,16,128]{4,2,1,3,0:T(8,128)} %get-tuple-element.30), kind=kLoop, calls=%fused_computation.25 | loop fusion | flops 44040192 | bytes 88080384 | tf_op jit(solution)/shard_map/mul | solution.py:243
  1728.7 43.3 %copy.273 = f32[28,4,48,16,128]{4,3,2,1,0:T(8,128)} copy(f32[28,4,48,16,128]{4,2,1,3,0:T(8,128)} %maximum_multiply_fusion) | data formatting | bytes 88080384 | tf_op jit(solution)/shard_map/mul | solution.py:243
  1772.0 46.4 %mul.883 = f32[28,192,2048]{2,1,0:T(8,128)} reshape(f32[28,4,48,16,128]{4,3,2,1,0:T(8,128)} %copy.273) | data formatting | bytes 88080384 | tf_op jit(solution)/shard_map/mul | solution.py:243
  1819.7 43.0 %fusion.18 = f32[28,192,2048]{2,1,0:T(8,128)} fusion(f32[28,192,2048]{2,1,0:T(8,128)} %mul.883, bf16[28,192,2048]{2,1,0:T(8,128)(2,1)} %bitcast.524, bf16[28,192,2048]{2,1,0:T(8,128)(2,1)} %get-tuple-element.38, bf16[48,48]{0,1:T(8,128)(2,1)S(1)} %bitcast.542, bf16[48,48]{0,1:T(8,128)(2,1)S(1)} %bitcast.538, bf16[48,48]{0,1:T(8,128)(2,1)S(1)} %copy-done.52, ...), kind=kOutput, calls=%fused_computation.23 | convolution fusion | flops 4262068224 | bytes 132148224 | tf_op jit(solution)/shard_map/son,io->sin/dot_general | solution.py:209
  (280 shorter events, 471.5 us)
Async XLA Ops:
  7.2 367.5 %all-gather.5.cloned.1.call-start = ((), (), s32[]{:S(2)}) async-start(), calls=%async_computation | async-start | bytes 66060288 | tf_op jit(solution)/shard_map/all_gather | solution.py:138
  7.2 642.7 %copy-start.54 = (s32[16]{0:T(128)}, s32[16]{0:T(128)S(1)}, u32[]{:S(2)}) copy-start(s32[16]{0:T(128)S(1)} %compare_select_fusion.5) | copy-start | bytes 196
  104.4 419.1 %all-gather.7.cloned.1.call-start = ((), (), s32[]{:S(2)}) async-start(), calls=%async_computation.1 | async-start | bytes 4423680 | tf_op jit(solution)/shard_map/all_gather | solution.py:179
  124.9 302.5 %copy-start.20 = (bf16[16,32]{1,0:T(8,128)(2,1)}, bf16[16,32]{1,0:T(8,128)(2,1)S(1)}, u32[]{:S(2)}) copy-start(bf16[16,32]{1,0:T(8,128)(2,1)S(1)} %fusion.262) | copy-start | bytes 3076
  126.6 300.8 %copy-start.33 = (bf16[8,16,32]{2,1,0:T(8,128)(2,1)}, bf16[8,16,32]{2,1,0:T(8,128)(2,1)S(1)}, u32[]{:S(2)}) copy-start(bf16[8,16,32]{2,1,0:T(8,128)(2,1)S(1)} %get-tuple-element.129) | copy-start | bytes 24580
  126.6 300.8 %copy-start.31 = (bf16[8,16,32]{2,1,0:T(8,128)(2,1)}, bf16[8,16,32]{2,1,0:T(8,128)(2,1)S(1)}, u32[]{:S(2)}) copy-start(bf16[8,16,32]{2,1,0:T(8,128)(2,1)S(1)} %get-tuple-element.128) | copy-start | bytes 24580
  133.4 351.5 %copy-start = (bf16[32,192,192]{2,1,0:T(8,128)(2,1)}, bf16[32,192,192]{2,1,0:T(8,128)(2,1)S(1)}, u32[]{:S(2)}) copy-start(bf16[32,192,192]{2,1,0:T(8,128)(2,1)S(1)} %maximum_maximum_fusion) | copy-start | bytes 7077892
  487.8 783.1 %all-gather.9.cloned.1.call-start = ((), (), s32[]{:S(2)}) async-start(), calls=%async_computation.2 | async-start | bytes 66060288 | tf_op jit(solution)/shard_map/all_gather | solution.py:220
  488.6 55.1 %copy-start.35 = (bf16[1,48,48]{1,2,0:T(8,128)(2,1)}, bf16[1,48,48]{1,2,0:T(8,128)(2,1)S(1)}, u32[]{:S(2)}) copy-start(bf16[1,48,48]{1,2,0:T(8,128)(2,1)S(1)} %copy.364) | copy-start | bytes 13828
  488.6 55.0 %copy-start.38 = (bf16[1,48,48]{1,2,0:T(8,128)(2,1)}, bf16[1,48,48]{1,2,0:T(8,128)(2,1)S(1)}, u32[]{:S(2)}) copy-start(bf16[1,48,48]{1,2,0:T(8,128)(2,1)S(1)} %copy.363) | copy-start | bytes 13828
  490.1 83.1 %copy-start.25 = (bf16[256,16]{0,1:T(8,128)(2,1)}, bf16[256,16]{0,1:T(8,128)(2,1)S(1)}, u32[]{:S(2)}) copy-start(bf16[256,16]{0,1:T(8,128)(2,1)S(1)} %fusion.246) | copy-start | bytes 24580
  490.2 53.4 %copy-start.43 = (bf16[256,16]{0,1:T(8,128)(2,1)}, bf16[256,16]{0,1:T(8,128)(2,1)S(1)}, u32[]{:S(2)}) copy-start(bf16[256,16]{0,1:T(8,128)(2,1)S(1)} %get-tuple-element.134) | copy-start | bytes 24580
  490.2 82.9 %copy-start.41 = (bf16[256,16]{0,1:T(8,128)(2,1)}, bf16[256,16]{0,1:T(8,128)(2,1)S(1)}, u32[]{:S(2)}) copy-start(bf16[256,16]{0,1:T(8,128)(2,1)S(1)} %get-tuple-element.135) | copy-start | bytes 24580
  996.7 460.3 %all-reduce.3.cloned.1.call-start = ((), (), s32[]{:S(2)}) async-start(), calls=%async_computation.4 | async-start | bytes 3145728 | tf_op jit(solution)/shard_map/psum | solution.py:228
  1006.8 406.6 %copy-start.18 = (bf16[2,192,512]{2,1,0:T(8,128)(2,1)}, bf16[2,192,512]{2,1,0:T(8,128)(2,1)S(1)}, u32[]{:S(2)}) copy-start(bf16[2,192,512]{2,1,0:T(8,128)(2,1)S(1)} %get-tuple-element.94) | copy-start | bytes 1179652
  1009.1 261.7 %copy-start.34 = (bf16[8,16,32]{2,1,0:T(8,128)(2,1)S(1)}, bf16[8,16,32]{2,1,0:T(8,128)(2,1)}, u32[]{:S(2)}) copy-start(bf16[8,16,32]{2,1,0:T(8,128)(2,1)} %copy-done.33) | copy-start | bytes 24580
  1035.0 288.3 %copy-start.32 = (bf16[8,16,32]{2,1,0:T(8,128)(2,1)S(1)}, bf16[8,16,32]{2,1,0:T(8,128)(2,1)}, u32[]{:S(2)}) copy-start(bf16[8,16,32]{2,1,0:T(8,128)(2,1)} %copy-done.31) | copy-start | bytes 24580
  1384.0 107.4 %all-gather.11.cloned.1.call-start = ((), (), s32[]{:S(2)}) async-start(), calls=%async_computation.3 | async-start | bytes 4423680 | tf_op jit(solution)/shard_map/all_gather | solution.py:234
  1413.4 81.9 %copy-start.59 = (s32[16]{0:T(128)S(1)}, s32[16]{0:T(128)}, u32[]{:S(2)}) copy-start(s32[16]{0:T(128)} %copy-done.57) | copy-start | bytes 196
  1771.9 46.5 %copy-start.46 = (bf16[1,48,48]{1,2,0:T(8,128)(2,1)S(1)}, bf16[1,48,48]{1,2,0:T(8,128)(2,1)}, u32[]{:S(2)}) copy-start(bf16[1,48,48]{1,2,0:T(8,128)(2,1)} %copy.362) | copy-start | bytes 13828
  1771.9 46.5 %copy-start.48 = (bf16[1,48,48]{1,2,0:T(8,128)(2,1)S(1)}, bf16[1,48,48]{1,2,0:T(8,128)(2,1)}, u32[]{:S(2)}) copy-start(bf16[1,48,48]{1,2,0:T(8,128)(2,1)} %copy.361) | copy-start | bytes 13828
  1771.9 46.5 %copy-start.50 = (bf16[48,48]{0,1:T(8,128)(2,1)S(1)}, bf16[48,48]{0,1:T(8,128)(2,1)}, u32[]{:S(2)}) copy-start(bf16[48,48]{0,1:T(8,128)(2,1)} %get-tuple-element.138) | copy-start | bytes 13828
  1772.0 46.5 %copy-start.52 = (bf16[48,48]{0,1:T(8,128)(2,1)S(1)}, bf16[48,48]{0,1:T(8,128)(2,1)}, u32[]{:S(2)}) copy-start(bf16[48,48]{0,1:T(8,128)(2,1)} %get-tuple-element.139) | copy-start | bytes 13828
  1772.0 46.5 %copy-start.62 = (bf16[2,4,48,512]{3,2,1,0:T(8,128)(2,1)S(1)}, bf16[2,4,48,512]{3,2,1,0:T(8,128)(2,1)}, u32[]{:S(2)}) copy-start(bf16[2,4,48,512]{3,2,1,0:T(8,128)(2,1)} %param.13) | copy-start | bytes 1179652
  (44 other events, 766.8 us)
Sparse Core Ops, SparseCore 0:
  104.5 270.0 all-gather.4
  487.9 35.6 all-gather.6
  996.8 273.9 all-gather.8
  1384.1 70.1 all-reduce.2
  1456.7 34.6 all-gather.10
where the time goes:
time: 1880 us; the launch traced here: 1870 us
  matrix products  570 us (30%)
  waiting for transfers between devices  541 us (29%)
  local copies, waits for them, and re-layouts  436 us (23%)
  other arithmetic  223 us (12%)
  blocking collectives  84.1 us (4%)
    all_gather x1, waiting for transfers between devices, on_device(): lax.all_gather(columns[0][None], 'rows', axis=0, tiled=True)  241 us
    all_gather x1, waiting for transfers between devices, on_device(): lax.all_gather(row_grads[0][None], 'rows', axis=0, tiled=True)  236 us
    dot_general x16, matrix products, dual_einsum(): jnp.einsum(pattern, operand, tables[1], preferred_element_type=jnp.float32)  219 us
    dot_general x16, matrix products, dual_einsum(): jnp.einsum(pattern, operand, tables[0], preferred_element_type=jnp.float32)  217 us
    add x8, other arithmetic, combine(): left_parts[0] + sign_flip * right_parts[3]  93.1 us
    mul x4, local copies, waits for them, and re-layouts, on_device(): spec_back.reshape(samples, comp_width, cell_count) * (1.0 / bundle['side'])  91 us
    dot_general x2, matrix products, on_device(): jnp.einsum('sin,io->son', bundle['field'], lin_kernel, preferred_element_...  69.1 us
    slice x4, local copies, waits for them, and re-layouts, combine(): lax.index_in_dim(second, blade_id, axis_at, keepdims=False)  60.2 us
  transfers between devices with their start and end apart: 5, of which 4 were waited for; matrix products, arithmetic and copies ran while one was open for 3% of the time, Pallas kernels for 0%

commit v1 on v0

v1 whole, which is shorter than its diff:
```python
import math

import jax
import jax.numpy as jnp
import ml_dtypes
import numpy as np
from jax import lax
from jax.experimental import pallas as pl
from jax.experimental.pallas import tpu as pltpu
from jax.sharding import PartitionSpec as P

C = 48
MX = 16
N1 = 128
N2 = 64
W = 4 * C
MODES = MX * MX
BF = jnp.bfloat16
F32 = jnp.float32


def trig(side):
    a = np.arange(MX)
    freq = np.where(a < MX // 2, a, side - MX + a)
    phase = (np.arange(side)[:, None] * freq[None, :]) % side
    angle = phase.astype(np.float32) * np.float32(2.0 * math.pi / side)
    cos = np.cos(angle).astype(ml_dtypes.bfloat16).astype(np.float32)
    sin = np.sin(angle).astype(ml_dtypes.bfloat16).astype(np.float32)
    return cos, sin


def low(table):
    return table.astype(ml_dtypes.bfloat16)


class Geometry:
    def __init__(self, side, n):
        self.side = side
        self.rows = side // n
        self.cells = self.rows * side
        self.group = min(8, self.rows)
        self.ngroups = self.rows // self.group
        self.npairs = self.rows // 2
        self.qlanes = max(128, self.npairs * 64)
        self.hk = self.ngroups * 128
        cos, sin = trig(side)
        eye = np.eye(MX, dtype=np.float32)

        first = np.zeros((self.group, side, 256), np.float32)
        for h in range(self.group):
            first[h, :, h * MX : (h + 1) * MX] = cos
            first[h, :, 128 + h * MX : 128 + (h + 1) * MX] = sin
        self.first = low(first.reshape(self.group * side, 256))

        second = np.zeros((n, MX, MX, 2, self.ngroups, 128), np.float32)
        inverse = np.zeros((n, MX, MX, 2, self.qlanes), np.float32)
        for r in range(n):
            for h in range(self.rows):
                c, s = cos[r * self.rows + h], sin[r * self.rows + h]
                ce, se = c[:, None, None] * eye, s[:, None, None] * eye
                g, lane = h // self.group, (h % self.group) * MX
                second[r, :, :, 0, g, lane : lane + MX] = ce
                second[r, :, :, 1, g, lane : lane + MX] = se
                lane = h * 2 * MX
                inverse[r, :, :, 0, lane : lane + MX] = ce
                inverse[r, :, :, 0, lane + MX : lane + 2 * MX] = -se
                inverse[r, :, :, 1, lane : lane + MX] = -se
                inverse[r, :, :, 1, lane + MX : lane + 2 * MX] = -ce
        self.second = low(second.reshape(n, MODES, 2 * self.hk))
        self.inverse = low(inverse.reshape(n, MODES, 2 * self.qlanes))

        spread = np.zeros((4, 2, MX, 4, side), np.float32)
        for h in range(4):
            spread[h, 0, :, h] = cos.T
            spread[h, 1, :, h] = sin.T
        self.spread = low(spread.reshape(128, 4 * side))
        if self.npairs == 1:
            self.spread = self.spread[:, : 2 * side]
        self.pair_spread = low(spread.reshape(128, 4 * side))[:64, : 2 * side]


def turn(v):
    return jnp.concatenate([v[3 * C :], v[2 * C : 3 * C], -v[C : 2 * C], -v[:C]], axis=0)


def dot(a, b, dims=((1,), (0,))):
    return lax.dot_general(a, b, (dims, ((), ())), preferred_element_type=F32)


def forward_pair(geo, get, first, second, scale, keep=None):
    width = geo.group * geo.side
    parts = []
    for g in range(geo.ngroups):
        y = dot(get(g * width, width), first)
        if keep is not None:
            keep(y[:W] + y[W:])
        parts.append(y)
    stacked = []
    for s in range(2):
        cols = []
        for y in parts:
            col = y[W * s : W * s + W, :128] + turn(y[W * s : W * s + W, 128:])
            cols.append((col * scale).astype(BF))
        col = jnp.concatenate(cols, axis=1) if len(cols) > 1 else cols[0]
        stacked.append(jnp.concatenate([col, turn(col)], axis=1))
    a, b = stacked
    both = jnp.concatenate([a[:128], b[:128], a[128:], b[128:]], axis=0)
    return dot(second, both, ((1,), (1,)))


def inverse_pair(geo, modes, inverse, scale):
    uv = dot(modes, inverse, ((0,), (0,)))
    result = []
    for s in range(2):
        part = jnp.concatenate(
            [uv[128 * s : 128 * s + 128], uv[256 + 64 * s : 320 + 64 * s]], axis=0
        )
        q = part[:, : geo.qlanes] + turn(part[:, geo.qlanes :])
        result.append((q * scale).astype(BF))
    return result


def build_kernel(weights):
    rows_list = []
    for source in range(4):
        blocks = []
        for target in range(4):
            blade_id = source ^ target
            block_part = weights[..., blade_id, :, :]
            if blade_id >> 1 & source & 1:
                block_part = -block_part
            blocks.append(block_part)
        rows_list.append(jnp.concatenate(blocks, axis=-1))
    return jnp.concatenate(rows_list, axis=-2)


def fold_kernel(kernel_grad):
    blades = []
    for blade_id in range(4):
        summed = None
        for source in range(4):
            target = source ^ blade_id
            block_part = kernel_grad[
                ..., source * C : (source + 1) * C, target * C : (target + 1) * C
            ]
            if blade_id >> 1 & source & 1:
                block_part = -block_part
            summed = block_part if summed is None else summed + block_part
        blades.append(summed)
    return jnp.stack(blades, axis=-3)


def expand_tables():
    dup = np.concatenate([np.arange(192), np.arange(128, 192)])
    place = np.zeros((4, C, 4, 256), np.float32)
    for p in range(4):
        for q in range(4):
            sign = -1.0 if (p >> 1) & q & 1 else 1.0
            full = np.zeros((C, 192), np.float32)
            o = p ^ q
            full[:, o * C : (o + 1) * C] = sign * np.eye(C)
            place[p, :, q] = full[:, dup]
    return low(place.reshape(4, C, 1024))


class Plan:
    def __init__(self, mesh, nbig, nsmall):
        self.n = mesh.shape["rows"]
        self.own = MODES // self.n
        self.per = max(1, 16 // self.own)
        self.big = Geometry(N1, self.n)
        self.small = Geometry(N2, self.n)
        self.nbig, self.nsmall = nbig, nsmall
        assert nbig % (2 * self.per) == 0 and nsmall % 2 == 0 and nsmall // 2 <= self.per
        self.steps = nbig // (2 * self.per)
        self.block = self.per * self.own
        self.total = (self.steps + 1) * self.block
        self.slots = -(-(self.total // self.own) // 8) * 8


def wide(i, last):
    return jnp.minimum(i, last)


def params(**kw):
    return pltpu.CompilerParams(vmem_limit_bytes=56 * 1024 * 1024, **kw)


def const_spec(shape):
    return pl.BlockSpec(shape, lambda i, r: (0,) * len(shape))


def device_spec(shape):
    return pl.BlockSpec((None,) + shape, lambda i, r: (r[0],) + (0,) * len(shape))


def field_specs(plan):
    big, small = plan.big, plan.small
    last = plan.steps - 1
    return (
        pl.BlockSpec((2 * plan.per, 4, C, big.cells), lambda i, r: (wide(i, last), 0, 0, 0)),
        pl.BlockSpec((plan.nsmall, 4, C, small.cells), lambda i, r: (0, 0, 0, 0)),
    )


def mode_spec(plan):
    return pl.BlockSpec((plan.n, plan.block, 2 * W), lambda i, r: (0, i, 0))


def store_modes(plan, ref, pair, z):
    z = z.reshape(plan.n, plan.own, 2 * W).astype(BF)
    ref[:, pair * plan.own : (pair + 1) * plan.own, :] = z


def load_modes(plan, ref, pair):
    return ref[:, pair * plan.own : (pair + 1) * plan.own, :].reshape(MODES, 2 * W)


def cost(flops, moved):
    return pl.CostEstimate(flops=flops, bytes_accessed=moved, transcendentals=0)


def spectra(plan, rank, x_big, x_small):
    def body(r, xb, xs, fb, sb, fs, ss, z):
        i = pl.program_id(0)

        def run(x, geo, first, second, count):
            for pair in range(count):
                def get(start, width):
                    part = x[2 * pair : 2 * pair + 2, :, :, start : start + width]
                    return part.reshape(2 * W, width)

                out = forward_pair(geo, get, first[...], second[...], 1.0 / geo.side)
                store_modes(plan, z, pair, out)

        @pl.when(i < plan.steps)
        def _():
            run(xb, plan.big, fb, sb, plan.per)

        @pl.when(i == plan.steps)
        def _():
            if plan.nsmall // 2 < plan.per:
                z[...] = jnp.zeros_like(z)
            run(xs, plan.small, fs, ss, plan.nsmall // 2)

    big, small = plan.big, plan.small
    return pl.pallas_call(
        body,
        grid_spec=pltpu.PrefetchScalarGridSpec(
            num_scalar_prefetch=1,
            grid=(plan.steps + 1,),
            in_specs=[
                *field_specs(plan),
                const_spec(big.first.shape),
                device_spec(big.second.shape[1:]),
                const_spec(small.first.shape),
                device_spec(small.second.shape[1:]),
            ],
            out_specs=mode_spec(plan),
        ),
        out_shape=jax.ShapeDtypeStruct((plan.n, plan.total, 2 * W), BF),
        compiler_params=params(),
        name="spectra",
    )(rank, x_big, x_small, big.first, big.second, small.first, small.second)


def cells_pass(plan, rank, x_big, x_small, g_big, g_small, modes, lin, lin_t, bias):
    k0 = math.sqrt(2.0 / math.pi)
    k1 = k0 * 0.044715

    def body(r, xb, xs, gb, gs, m, fb, sb, vb, eb, fs, ss, vs, es, kk, kt, bias_ref,
             ob, os_, pb, ps, z, lin_acc, y_acc, grad_b, grad_s):
        i = pl.program_id(0)

        @pl.when(i == 0)
        def _():
            lin_acc[...] = jnp.zeros_like(lin_acc)
            y_acc[...] = jnp.zeros_like(y_acc)

        def run(x, g, o, d, geo, first, second, inverse, spread, scratch, count):
            wide_cells = 2 * geo.side
            lane = lax.broadcasted_iota(jnp.int32, (W, 128), 1)
            for pair in range(count):
                qs = inverse_pair(geo, load_modes(plan, m, pair), inverse[...], 1.0 / MX)
                for s in range(2):
                    at = 2 * pair + s
                    for p in range(geo.npairs):
                        lo = p * wide_cells
                        q = qs[s][:, 128 * (p // 2) : 128 * (p // 2) + 128]
                        xv = x[at, :, :, lo : lo + wide_cells].reshape(W, wide_cells)
                        if p % 2 == 0:
                            tail = jnp.where(lane < 64, q, kt[:, 128:256])
                            rhs = [xv[:128], spread[...], xv[128:]]
                        else:
                            tail = jnp.where(lane >= 64, q, kt[:, 256:384])
                            rhs = [xv[:128], xv[128:], spread[...]]
                        lhs = jnp.concatenate([kt[:, :128], tail], axis=1)
                        a = dot(lhs, jnp.concatenate(rhs, axis=0)) + bias_ref[...]
                        a2 = a * a
                        t = jnp.tanh(a * (k0 + k1 * a2))
                        h = 0.5 + 0.5 * t
                        o[at, :, :, lo : lo + wide_cells] = (
                            (xv.astype(F32) + a * h).astype(BF).reshape(4, C, wide_cells)
                        )
                        slope = h + (a * (2.0 * k0 + 6.0 * k1 * a2)) * (h - h * h)
                        gv = g[at, :, :, lo : lo + wide_cells].reshape(W, wide_cells).astype(F32)
                        pre = (gv * slope).astype(BF)
                        scratch[s * W : s * W + W, lo : lo + wide_cells] = pre
                        d[at, :, :, lo : lo + wide_cells] = (
                            (gv + dot(kk[...], pre)).astype(BF).reshape(4, C, wide_cells)
                        )
                    xa = x[at, :, :, :].reshape(W, geo.cells)
                    lin_acc[...] += dot(xa, scratch[s * W : s * W + W, :], ((1,), (1,)))

                def keep(y):
                    y_acc[...] += y

                out = forward_pair(
                    geo, lambda start, width: scratch[:, start : start + width],
                    first[...], second[...], 1.0, keep,
                )
                store_modes(plan, z, pair, out)

        @pl.when(i < plan.steps)
        def _():
            run(xb, gb, ob, pb, plan.big, fb, sb, vb, eb, grad_b, plan.per)

        @pl.when(i == plan.steps)
        def _():
            if plan.nsmall // 2 < plan.per:
                z[...] = jnp.zeros_like(z)
            run(xs, gs, os_, ps, plan.small, fs, ss, vs, es, grad_s, plan.nsmall // 2)

    big, small = plan.big, plan.small
    tables = []
    specs = []
    for geo in (big, small):
        tables += [geo.first, geo.second, geo.inverse, geo.pair_spread]
        specs += [
            const_spec(geo.first.shape),
            device_spec(geo.second.shape[1:]),
            device_spec(geo.inverse.shape[1:]),
            const_spec(geo.pair_spread.shape),
        ]
    return pl.pallas_call(
        body,
        grid_spec=pltpu.PrefetchScalarGridSpec(
            num_scalar_prefetch=1,
            grid=(plan.steps + 1,),
            in_specs=[
                *field_specs(plan),
                *field_specs(plan),
                mode_spec(plan),
                *specs,
                const_spec(lin.shape),
                const_spec(lin_t.shape),
                const_spec(bias.shape),
            ],
            out_specs=[
                *field_specs(plan),
                *field_specs(plan),
                mode_spec(plan),
                const_spec((W, W)),
                const_spec((W, 256)),
            ],
            scratch_shapes=[
                pltpu.VMEM((2 * W, big.cells), BF),
                pltpu.VMEM((2 * W, small.cells), BF),
            ],
        ),
        out_shape=[
            jax.ShapeDtypeStruct(x_big.shape, BF),
            jax.ShapeDtypeStruct(x_small.shape, BF),
            jax.ShapeDtypeStruct(x_big.shape, BF),
            jax.ShapeDtypeStruct(x_small.shape, BF),
            jax.ShapeDtypeStruct((plan.n, plan.total, 2 * W), BF),
            jax.ShapeDtypeStruct((W, W), F32),
            jax.ShapeDtypeStruct((W, 256), F32),
        ],
        compiler_params=params(),
        name="cells",
    )(rank, x_big, x_small, g_big, g_small, modes, *tables, lin, lin_t, bias)


def input_grads(plan, rank, part_big, part_small, modes):
    def body(r, pb, ps, m, vb, eb, vs, es, db, ds):
        i = pl.program_id(0)

        def run(part, d, geo, inverse, spread, count):
            span = spread.shape[1]
            for pair in range(count):
                qs = inverse_pair(geo, load_modes(plan, m, pair), inverse[...], 1.0)
                q = jnp.concatenate(qs, axis=0) * jnp.asarray(1.0 / geo.side, BF)
                for j in range(geo.cells // span):
                    v = dot(q[:, 128 * j : 128 * j + 128], spread[...])
                    at = (slice(2 * pair, 2 * pair + 2), slice(None), slice(None),
                          slice(j * span, (j + 1) * span))
                    d[at] = part[at].astype(F32) + v.reshape(2, 4, C, span)

        @pl.when(i < plan.steps)
        def _():
            run(pb, db, plan.big, vb, eb, plan.per)

        @pl.when(i == plan.steps)
        def _():
            run(ps, ds, plan.small, vs, es, plan.nsmall // 2)

    tables = []
    specs = []
    for geo in (plan.big, plan.small):
        tables += [geo.inverse, geo.spread]
        specs += [device_spec(geo.inverse.shape[1:]), const_spec(geo.spread.shape)]
    return pl.pallas_call(
        body,
        grid_spec=pltpu.PrefetchScalarGridSpec(
            num_scalar_prefetch=1,
            grid=(plan.steps + 1,),
            in_specs=[*field_specs(plan), mode_spec(plan), *specs],
            out_specs=[*field_specs(plan)],
        ),
        out_shape=[
            jax.ShapeDtypeStruct(part_big.shape, F32),
            jax.ShapeDtypeStruct(part_small.shape, F32),
        ],
        compiler_params=params(),
        name="input_grads",
    )(rank, part_big, part_small, modes, *tables)


def lanes(acc, count):
    return jnp.concatenate([acc[t, :count, :] for t in range(3)], axis=1)


def mix_rows(plan, acc, kernel, scale, dims):
    lane = lax.broadcasted_iota(jnp.int32, (plan.slots, 128), 1)
    low_half = lane < 64

    def one(m):
        rows = pl.ds(m, plan.slots, stride=plan.own)
        first, second, third = (acc[t, rows, :] * scale for t in range(3))
        a = jnp.concatenate([first, jnp.where(low_half, third, 0.0)], axis=1)
        b = jnp.concatenate([second, jnp.where(low_half, 0.0, third)], axis=1)
        lhs = jnp.concatenate([a, b], axis=0).astype(BF)
        res = dot(lhs, kernel[m], dims)
        ra, rb = res[: plan.slots], res[plan.slots :]
        acc[0, rows, :] = ra[:, :128]
        acc[1, rows, :] = rb[:, :128]
        acc[2, rows, :] = jnp.where(low_half, ra[:, 128:], rb[:, 128:])

    unroll = 4

    @pl.loop(0, plan.own // unroll)
    def _(j):
        for u in range(unroll):
            one(j * unroll + u)


def exchange(plan, body, collective_id, name, operands, extra_out):
    n, own, total = plan.n, plan.own, plan.total
    half = n // 2
    block = (total, 2 * W)
    nin = len(operands)
    nout = 1 + len(extra_out)

    def kernel(*refs):
        part = refs[0]
        result = refs[nin]
        (acc, sib_in, sib_sum, peer_in, s_sib, r_sib, s_peer, r_peer,
         s_out, r_out, s_fwd, r_fwd) = refs[nin + nout :]
        me = lax.axis_index("rows")
        chip, core = me // 2, me % 2
        other = chip * 2 + (1 - core)

        def peer(d):
            return lax.rem(chip + d, half)

        def source(d):
            return lax.rem(chip + half - d, half)

        barrier = pltpu.get_barrier_semaphore()
        pl.semaphore_signal(barrier, inc=1, device_id={"rows": other})
        for d in range(1, half):
            pl.semaphore_signal(barrier, inc=1, device_id={"rows": peer(d) * 2 + core})
        pl.semaphore_wait(barrier, half)

        def to_sibling(d):
            return pltpu.make_async_remote_copy(
                src_ref=part.at[peer(d) * 2 + (1 - core)],
                dst_ref=sib_in.at[d],
                send_sem=s_sib.at[d],
                recv_sem=r_sib.at[d],
                device_id={"rows": other},
            )

        def to_peer(d):
            return pltpu.make_async_remote_copy(
                src_ref=sib_sum.at[d],
                dst_ref=peer_in.at[d],
                send_sem=s_peer.at[d],
                recv_sem=r_peer.at[d],
                device_id={"rows": peer(d) * 2 + core},
            )

        order = list(range(1, half)) + [0]
        for d in order:
            to_sibling(d).start()
        for d in range(1, half):
            to_sibling(d).wait_recv()
            mine = part[peer(d) * 2 + core].astype(F32)
            sib_sum[d] = (mine + sib_in[d].astype(F32)).astype(BF)
            to_peer(d).start()
        finish = body(plan, refs[1:nin], refs[nin + 1 : nin + nout], acc)
        to_sibling(0).wait_recv()
        summed = part[me].astype(F32) + sib_in[0].astype(F32)
        for d in range(1, half):
            to_peer(d).wait_recv()
            summed = summed + peer_in[d].astype(F32)
        for t in range(3):
            acc[t, :total, :] = summed[:, 128 * t : 128 * t + 128]
        if plan.slots * own > total:
            acc[:, total:, :] = jnp.zeros((3, plan.slots * own - total, 128), F32)
        finish()
        result[me] = lanes(acc, total).astype(BF)

        def out_to(d):
            return pltpu.make_async_remote_copy(
                src_ref=result.at[me],
                dst_ref=result.at[me],
                send_sem=s_out.at[d],
                recv_sem=r_out.at[d],
                device_id={"rows": other if d == 0 else peer(d) * 2 + core},
            )

        def forward(d):
            at = source(d) * 2 + core
            return pltpu.make_async_remote_copy(
                src_ref=result.at[at],
                dst_ref=result.at[at],
                send_sem=s_fwd.at[d],
                recv_sem=r_fwd.at[d],
                device_id={"rows": other},
            )

        for d in order:
            out_to(d).start()
        for d in range(1, half):
            out_to(d).wait_recv()
            forward(d).start()
        out_to(0).wait_recv()
        for d in range(1, half):
            forward(d).wait_recv()
            forward(d).wait_send()
            out_to(d).wait_send()
            to_peer(d).wait_send()
        out_to(0).wait_send()
        for d in range(half):
            to_sibling(d).wait_send()

    vmem = pl.BlockSpec(memory_space=pltpu.VMEM)
    dma = pltpu.SemaphoreType.DMA((half,))
    return pl.pallas_call(
        kernel,
        in_specs=[vmem] * nin,
        out_specs=[vmem] * nout,
        out_shape=[jax.ShapeDtypeStruct((n,) + block, BF), *extra_out],
        scratch_shapes=[
            pltpu.VMEM((3, plan.slots * own, 128), F32),
            pltpu.VMEM((half,) + block, BF),
            pltpu.VMEM((half,) + block, BF),
            pltpu.VMEM((half,) + block, BF),
            *[dma] * 8,
        ],
        compiler_params=params(collective_id=collective_id, has_side_effects=True),
        name=name,
    )(*operands)


def forward_modes(plan, operands, outs, acc):
    place, weights = operands
    kernel, spectrum = outs
    flat = [weights[:, p].reshape(plan.own * C, C) for p in range(4)]
    for q in range(4):
        rows = None
        for p in range(4):
            term = dot(flat[p], place[p, :, 256 * q : 256 * q + 256])
            rows = term if rows is None else rows + term
        kernel[:, C * q : C * q + C, :] = rows.astype(BF).reshape(plan.own, C, 256)
    kernel[:, W:, :] = kernel[:, 128:W, :]

    def finish():
        spectrum[...] = lanes(acc, plan.total).astype(BF)
        mix_rows(plan, acc, kernel, 1.0, ((1,), (0,)))

    return finish


def backward_modes(plan, operands, outs, acc):
    (kernel,) = operands
    (grad,) = outs

    def finish():
        grad[...] = (lanes(acc, plan.total) * (1.0 / MX)).astype(BF)
        mix_rows(plan, acc, kernel, 1.0 / MX, ((1,), (1,)))

    return finish


def on_device(plan, x_big, x_small, spec_weight, lin_weight, lin_bias, grad_big, grad_small):
    rank = lax.axis_index("rows").reshape(1)
    lin = build_kernel(lin_weight)
    lin_t = lin.T
    zero = jnp.zeros((W, 64), BF)
    lin_t = jnp.concatenate([lin_t[:, :128], zero, lin_t[:, 128:], lin_t[:, 128:], zero], axis=1)
    bias = lin_bias.astype(F32).reshape(W, 1)

    block = (plan.total, 2 * W)
    part = spectra(plan, rank, x_big, x_small)
    modes, kernel, spectrum = exchange(
        plan, forward_modes, 1, "mix_modes",
        (part, jnp.asarray(expand_tables()), spec_weight),
        (
            jax.ShapeDtypeStruct((plan.own, 256, 256), BF),
            jax.ShapeDtypeStruct(block, BF),
        ),
    )
    out_big, out_small, part_big, part_small, part, lin_grad, columns = cells_pass(
        plan, rank, x_big, x_small, grad_big, grad_small, modes, lin, lin_t, bias
    )
    bias_grad = columns[:, :128:MX].sum(axis=1)
    lin_grads = lax.psum((fold_kernel(lin_grad), bias_grad.reshape(4, C)), ("samples", "rows"))
    modes, mode_grad = exchange(
        plan, backward_modes, 2, "mix_grads", (part, kernel),
        (jax.ShapeDtypeStruct(block, BF),),
    )

    def samples(v):
        v = v.reshape(plan.total // plan.own, plan.own, 2 * W)
        a = jnp.concatenate([v[..., :128], v[..., 256:320]], axis=-1)
        b = jnp.concatenate([v[..., 128:256], v[..., 320:]], axis=-1)
        return jnp.concatenate([a, b], axis=0)

    kernel_grad = jnp.einsum(
        "smi,smo->mio", samples(spectrum), samples(mode_grad), preferred_element_type=F32
    )
    spec_grad = lax.psum(fold_kernel(kernel_grad).astype(BF), "samples").astype(F32)
    dx_big, dx_small = input_grads(plan, rank, part_big, part_small, modes)
    return out_big, out_small, dx_big, dx_small, spec_grad, lin_grads[0], lin_grads[1]


def solution(mesh):
    fields = P("samples", None, None, "rows")
    spec = P("rows", None, None, None)

    def run(x_big, x_small, *rest):
        count = mesh.shape["samples"]
        plan = Plan(mesh, x_big.shape[0] // count, x_small.shape[0] // count)

        def local(*args):
            return on_device(plan, *args)

        return jax.shard_map(
            local,
            mesh=mesh,
            in_specs=(fields, fields, spec, P(), P(), fields, fields),
            out_specs=(fields, fields, fields, fields, spec, P(), P()),
            check_vma=False,
        )(x_big, x_small, *rest)

    return run
```

time: 1880 us -> 296 us (0.16)
  matrix products: 570 us -> 1.07 us
  waiting for transfers between devices: 541 us -> 0.02 us
  local copies, waits for them, and re-layouts: 436 us -> 11.9 us
  Pallas kernels: 0 us -> 220 us
  other arithmetic: 223 us -> 4.6 us
  blocking collectives: 84.1 us -> 43.1 us
    dot_general x41 -> x1, matrix products: 570 us -> 1.07 us  [on_device(): jnp.einsum('smi,smo->mio', samples(spectrum), samples(mode_grad), preferr...]
    all_gather x4 -> x0, waiting for transfers between devices: 541 us -> none  [the longest x1 241 us: on_device(): lax.all_gather(columns[0][None], 'rows', axis=0, tiled=True)]
    pallas_call x0 -> x5, Pallas kernels: none -> 220 us  [the longest x2 99.4 us: exchange(): pl.pallas_call(kernel, in_specs=[vmem] * nin, out_specs=[vmem] * nout, ou...]
    slice x8 -> x7, local copies, waits for them, and re-layouts: 120 us -> 4.49 us  [the longest x4 4.22 us: samples(): a = jnp.concatenate([v[..., :128], v[..., 256:320]], axis=-1)]
    reshape x11 -> x2, local copies, waits for them, and re-layouts: 104 us -> 0.84 us  [the longest x1 0.76 us: on_device(): bias = lin_bias.astype(F32).reshape(W, 1)]
    add x15 -> x0, other arithmetic: 93.9 us -> none  [the longest x8 93.1 us: combine(): left_parts[0] + sign_flip * right_parts[3]]
    mul x4 -> x0, local copies, waits for them, and re-layouts: 91 us -> none  [on_device(): spec_back.reshape(samples, comp_width, cell_count) * (1.0 / bundle['side'])]
    another operation x22 -> x0, other arithmetic: 67.7 us -> none  [the longest x12 57.9 us: combine(): jnp.stack([left_parts[0] + sign_flip * right_parts[3], left_parts[1] + si...]
  transfers between devices with their start and end apart: 5 -> 1, of which waited for: 4 -> 0; matrix products, arithmetic and copies ran while one was open for 3% -> 0% of each run, Pallas kernels for 0% -> 10%
where the time goes in v1:
time: 296 us; the launch traced here: 295 us
  Pallas kernels  220 us (74%)
  blocking collectives  43.1 us (15%)
  between operations  14.2 us (5%)
  local copies, waits for them, and re-layouts  11.9 us (4%)
  other arithmetic  4.6 us (2%)
    pallas_call x2, Pallas kernels, exchange(): pl.pallas_call(kernel, in_specs=[vmem] * nin, out_specs=[vmem] * nout, ou...  99.4 us
    pallas_call x1, Pallas kernels, cells_pass(): pl.pallas_call(body, grid_spec=pltpu.PrefetchScalarGridSpec(num_scalar_pr...  71.2 us
    psum x1, blocking collectives, on_device(): lax.psum((fold_kernel(lin_grad), bias_grad.reshape(4, C)), ('samples', 'r...  43.1 us
    pallas_call x1, Pallas kernels, input_grads(): pl.pallas_call(body, grid_spec=pltpu.PrefetchScalarGridSpec(num_scalar_pr...  29.8 us
    pallas_call x1, Pallas kernels, spectra(): pl.pallas_call(body, grid_spec=pltpu.PrefetchScalarGridSpec(num_scalar_pr...  19.7 us
  transfers between devices with their start and end apart: 1, of which 0 were waited for; matrix products, arithmetic and copies ran while one was open for 0% of the time, Pallas kernels for 10%

profile of v1, /device:TPU:0, one launch (start us, length us, event | category | flops | bytes accessed | tf_op | source)
XLA Modules:
  0.0 295.0 jit_solution(5648382810281909888)
XLA Ops:
  7.2 0.8 fusion.32
  8.2 0.1 copy.56
  8.4 0.1 maximum_maximum_fusion
  8.5 0.1 fusion.33
  8.7 19.7 %spectra.1.refs_0_ = bf16[8,480,384]{2,1,0:T(8,128)(2,1)} custom-call(s32[1]{0:T(128)} %bitcast.r, bf16[28,4,48,2048]{3,2,1,0:T(8,128)(2,1)} %xb.3, bf16[2,4,48,512]{3,2,1,0:T(8,128)(2,1)} %xs.3, bf16[1024,256]{1,0:T(8,128)(2,1)} %constant.30.clone.fb, bf16[8,256,512]{2,1,0:T(8,128)(2,1)} %constant.31.clone.sb, bf16[512,256]{1,0:T(8,128)(2,1)} %constant.32.clone.fs, ...), custom_call_target="tpu_custom_call" | custom-call | tf_op jit(solution)/shard_map/spectra/pallas_call | solution.py:247
  28.4 50.6 %mix_modes.1 = (bf16[8,480,384]{2,1,0:T(8,128)(2,1)}, bf16[32,256,256]{2,1,0:T(8,128)(2,1)}, bf16[480,384]{1,0:T(8,128)(2,1)}) custom-call(bf16[8,480,384]{2,1,0:T(8,128)(2,1)} %spectra.1.refs_0_, bf16[4,48,1024]{2,1,0:T(8,128)(2,1)} %constant.34.clone.refs_1_, bf16[32,4,48,48]{3,2,1,0:T(8,128)(2,1)} %refs_2_.1), custom_call_target="tpu_custom_call" | custom-call | tf_op jit(solution)/shard_map/mix_modes/pallas_call | solution.py:561
  79.1 1.2 fusion.31
  80.2 1.0 fusion.30
  81.2 0.7 copy.43.kk
  82.0 0.8 reshape.39.bias_ref
  82.7 0.8 concatenate.41.kt
  83.5 71.2 %cells.1 = (bf16[28,4,48,2048]{3,2,1,0:T(8,128)(2,1)}, bf16[2,4,48,512]{3,2,1,0:T(8,128)(2,1)}, bf16[28,4,48,2048]{3,2,1,0:T(8,128)(2,1)}, bf16[2,4,48,512]{3,2,...) custom-call(s32[1]{0:T(128)} %bitcast.r, bf16[28,4,48,2048]{3,2,1,0:T(8,128)(2,1)} %xb.3, ...), custom_call_target="tpu_custom_call" | custom-call | tf_op jit(solution)/shard_map/cells/pallas_call | solution.py:345
  154.7 48.7 %mix_grads.1 = (bf16[8,480,384]{2,1,0:T(8,128)(2,1)}, bf16[480,384]{1,0:T(8,128)(2,1)}) custom-call(bf16[8,480,384]{2,1,0:T(8,128)(2,1)} %get-tuple-element.26.refs_0_, bf16[32,256,256]{2,1,0:T(8,128)(2,1)} %get-tuple-element.27.refs_1_), custom_call_target="tpu_custom_call" | custom-call | tf_op jit(solution)/shard_map/mix_grads/pallas_call | solution.py:561
  203.5 1.1 fusion.29
  204.6 1.0 fusion.28
  206.0 1.1 fusion.8
  207.1 2.5 fusion.23
  209.6 1.6 pad_maximum_fusion
  211.2 0.3 slice.200
  211.5 0.1 reduce_sum.9
  211.7 29.8 %input_grads.1 = (f32[28,4,48,2048]{3,2,1,0:T(8,128)}, f32[2,4,48,512]{3,2,1,0:T(8,128)}) custom-call(s32[1]{0:T(128)} %bitcast.r, bf16[28,4,48,2048]{3,2,1,0:T(8,128)(2,1)} %get-tuple-element.24.pb, bf16[2,4,48,512]{3,2,1,0:T(8,128)(2,1)} %get-tuple-element.25.ps, bf16[8,480,384]{2,1,0:T(8,128)(2,1)} %get-tuple-element.28.m, ...), custom_call_target="tpu_custom_call" | custom-call | tf_op jit(solution)/shard_map/input_grads/pallas_call | solution.py:413
  241.4 0.1 add_bitcast_fusion.3
  241.6 43.1 %all-reduce = (f32[4,48,48]{2,1,0:T(8,128)}, f32[4,48]{1,0:T(4,128)}) all-reduce(f32[4,48,48]{2,1,0:T(8,128)S(1)} %pad_maximum_fusion.1, f32[4,48]{1,0:T(4,128)S(1)} %reshape.36), channel_id=1, replica_groups=mesh['samples'=4,'rows'=8] {'samples','rows'}, use_global_device_ids=true, to_apply=%region_1.0 | all-reduce | flops 9408 | bytes 75264 | tf_op jit(solution)/shard_map/psum | solution.py:630
  284.7 3.5 %copy.53 = f32[32,4,48,48]{3,2,1,0:T(8,128)} copy(bf16[32,4,48,48]{3,2,0,1:T(8,128)(2,1)} %all-reduce.3.cloned.1.call-done) | data formatting | bytes 1769472
  (26 shorter events, 0.9 us)
Async XLA Ops:
  7.2 277.5 %all-reduce.3.cloned.1.call-start = ((), (), s32[]{:S(2)}) async-start(), calls=%async_computation | async-start | bytes 3145728 | tf_op jit(solution)/shard_map/psum | solution.py:645
  28.4 53.6 %copy-start.2 = (bf16[4,48]{1,0:T(4,128)(2,1)S(1)}, bf16[4,48]{1,0:T(4,128)(2,1)}, u32[]{:S(2)}) copy-start(bf16[4,48]{1,0:T(4,128)(2,1)} %param.22) | copy-start | bytes 1156
  209.6 1.6 copy-start.1
  211.7 29.8 %copy-start = (f32[192,192]{1,0:T(8,128)S(1)}, f32[192,192]{1,0:T(8,128)}, u32[]{:S(2)}) copy-start(f32[192,192]{1,0:T(8,128)} %get-tuple-element.33) | copy-start | bytes 442372
Sparse Core Ops, SparseCore 0:
  211.3 70.5 all-reduce.2

commit v2 on v1

v2 whole, which is shorter than its diff:
```python
import math

import jax
import jax.numpy as jnp
import ml_dtypes
import numpy as np
from jax import lax
from jax.experimental import pallas as pl
from jax.experimental.pallas import tpu as pltpu
from jax.sharding import PartitionSpec as P

C = 48
MX = 16
N1 = 128
N2 = 64
W = 4 * C
MODES = MX * MX
BF = jnp.bfloat16
F32 = jnp.float32


def trig(side):
    a = np.arange(MX)
    freq = np.where(a < MX // 2, a, side - MX + a)
    phase = (np.arange(side)[:, None] * freq[None, :]) % side
    angle = phase.astype(np.float32) * np.float32(2.0 * math.pi / side)
    cos = np.cos(angle).astype(ml_dtypes.bfloat16).astype(np.float32)
    sin = np.sin(angle).astype(ml_dtypes.bfloat16).astype(np.float32)
    return cos, sin


def low(table):
    return table.astype(ml_dtypes.bfloat16)


class Geometry:
    def __init__(self, side, n):
        self.side = side
        self.rows = side // n
        self.cells = self.rows * side
        self.group = min(8, self.rows)
        self.ngroups = self.rows // self.group
        self.npairs = self.rows // 2
        self.qlanes = max(128, self.npairs * 64)
        self.hk = self.ngroups * 128
        cos, sin = trig(side)
        eye = np.eye(MX, dtype=np.float32)

        first = np.zeros((self.group, side, 256), np.float32)
        for h in range(self.group):
            first[h, :, h * MX : (h + 1) * MX] = cos
            first[h, :, 128 + h * MX : 128 + (h + 1) * MX] = sin
        self.first = low(first.reshape(self.group * side, 256))

        second = np.zeros((n, MX, MX, 2, self.ngroups, 128), np.float32)
        inverse = np.zeros((n, MX, MX, 2, self.qlanes), np.float32)
        for r in range(n):
            for h in range(self.rows):
                c, s = cos[r * self.rows + h], sin[r * self.rows + h]
                ce, se = c[:, None, None] * eye, s[:, None, None] * eye
                g, lane = h // self.group, (h % self.group) * MX
                second[r, :, :, 0, g, lane : lane + MX] = ce
                second[r, :, :, 1, g, lane : lane + MX] = se
                lane = h * 2 * MX
                inverse[r, :, :, 0, lane : lane + MX] = ce
                inverse[r, :, :, 0, lane + MX : lane + 2 * MX] = -se
                inverse[r, :, :, 1, lane : lane + MX] = -se
                inverse[r, :, :, 1, lane + MX : lane + 2 * MX] = -ce
        self.second = low(second.reshape(n, MODES, 2 * self.hk))
        inverse[..., MX : self.rows * 2 * MX : 2 * MX] = 0.0
        self.inverse = low(inverse.reshape(n, MODES, 2 * self.qlanes))

        spread = np.zeros((4, 2, MX, 4, side), np.float32)
        for h in range(4):
            spread[h, 0, :, h] = cos.T
            spread[h, 1, :, h] = sin.T
        self.spread = low(spread.reshape(128, 4 * side))
        if self.npairs == 1:
            self.spread = self.spread[:, : 2 * side]
        for h in range(4):
            spread[h, 1, 0, h] = 1.0
        self.pair_spread = low(spread.reshape(128, 4 * side))[:64, : 2 * side]


def turn(v):
    return jnp.concatenate([v[3 * C :], v[2 * C : 3 * C], -v[C : 2 * C], -v[:C]], axis=0)


def dot(a, b, dims=((1,), (0,))):
    return lax.dot_general(a, b, (dims, ((), ())), preferred_element_type=F32)


def forward_pair(geo, get, first, second, scale, keep=None):
    width = geo.group * geo.side
    parts = []
    for g in range(geo.ngroups):
        y = dot(get(g * width, width), first)
        if keep is not None:
            keep(y[:W] + y[W:])
        parts.append(y)
    stacked = []
    for s in range(2):
        cols = []
        for y in parts:
            col = y[W * s : W * s + W, :128] + turn(y[W * s : W * s + W, 128:])
            cols.append((col * scale).astype(BF))
        col = jnp.concatenate(cols, axis=1) if len(cols) > 1 else cols[0]
        stacked.append(jnp.concatenate([col, turn(col)], axis=1))
    a, b = stacked
    both = jnp.concatenate([a[:128], b[:128], a[128:], b[128:]], axis=0)
    return dot(second, both, ((1,), (1,)))


def inverse_pair(geo, modes, inverse, scale):
    uv = dot(modes, inverse, ((0,), (0,)))
    result = []
    for s in range(2):
        part = jnp.concatenate(
            [uv[128 * s : 128 * s + 128], uv[256 + 64 * s : 320 + 64 * s]], axis=0
        )
        q = part[:, : geo.qlanes] + turn(part[:, geo.qlanes :])
        result.append((q * scale).astype(BF))
    return result


def build_kernel(weights):
    rows_list = []
    for source in range(4):
        blocks = []
        for target in range(4):
            blade_id = source ^ target
            block_part = weights[..., blade_id, :, :]
            if blade_id >> 1 & source & 1:
                block_part = -block_part
            blocks.append(block_part)
        rows_list.append(jnp.concatenate(blocks, axis=-1))
    return jnp.concatenate(rows_list, axis=-2)


def fold_kernel(kernel_grad):
    blades = []
    for blade_id in range(4):
        summed = None
        for source in range(4):
            target = source ^ blade_id
            block_part = kernel_grad[
                ..., source * C : (source + 1) * C, target * C : (target + 1) * C
            ]
            if blade_id >> 1 & source & 1:
                block_part = -block_part
            summed = block_part if summed is None else summed + block_part
        blades.append(summed)
    return jnp.stack(blades, axis=-3)


def fold_tables():
    dup = np.concatenate([np.arange(192), np.arange(128, 192)])
    pick = np.zeros((192, 4, 128), np.float32)
    move = np.zeros((192, 4, 192), np.float32)
    for q in range(4):
        pick[q * C : q * C + C, q, :C] = np.eye(C)
        for p in range(4):
            sign = -1.0 if (p >> 1) & q & 1 else 1.0
            o = p ^ q
            move[o * C : o * C + C, q, p * C : p * C + C] = sign * np.eye(C)
    return (
        low(pick[dup].reshape(256, 512)),
        low(move[dup][:, :, dup].reshape(256, 1024)),
        move.transpose(1, 0, 2).copy(),
    )


def expand_tables():
    dup = np.concatenate([np.arange(192), np.arange(128, 192)])
    place = np.zeros((4, C, 4, 256), np.float32)
    for p in range(4):
        for q in range(4):
            sign = -1.0 if (p >> 1) & q & 1 else 1.0
            full = np.zeros((C, 192), np.float32)
            o = p ^ q
            full[:, o * C : (o + 1) * C] = sign * np.eye(C)
            place[p, :, q] = full[:, dup]
    return low(place.reshape(4, C, 1024))


class Plan:
    def __init__(self, mesh, nbig, nsmall):
        self.n = mesh.shape["rows"]
        self.nz = mesh.shape["samples"]
        self.own = MODES // self.n
        self.per = max(1, 16 // self.own)
        self.big = Geometry(N1, self.n)
        self.small = Geometry(N2, self.n)
        self.nbig, self.nsmall = nbig, nsmall
        assert nbig % (2 * self.per) == 0 and nsmall % 2 == 0 and nsmall // 2 <= self.per
        self.steps = nbig // (2 * self.per)
        self.count = self.steps + 1
        self.block = self.per * self.own
        self.total = self.count * self.block
        self.chunks = next(c for c in (3, 2, 1) if self.count % c == 0)
        self.span = self.count // self.chunks
        self.crow = self.span * self.block
        self.half = self.crow // 2
        self.slots = -(-(self.span * self.per) // 8) * 8
        self.acc_rows = self.slots * self.own
        self.chips = self.n // 2
        bits = list(range(1, self.n.bit_length() - 1))
        self.orders = (bits, bits[::-1])
        self.levels = len(bits)
        self.wrows = self.own // 2 * C
        self.zrows = -(-self.wrows // (16 * self.nz)) * 16

    def mask(self, h, idx):
        m = 0
        for t, b in enumerate(self.orders[h]):
            if idx >> (self.levels - 1 - t) & 1:
                m |= 1 << b
        return m


def wide(i, last):
    return jnp.minimum(i, last)


def params(**kw):
    return pltpu.CompilerParams(vmem_limit_bytes=56 * 1024 * 1024, **kw)


def const_spec(shape):
    return pl.BlockSpec(shape, lambda i, r: (0,) * len(shape))


def device_spec(shape):
    return pl.BlockSpec((None,) + shape, lambda i, r: (r[0],) + (0,) * len(shape))


def field_specs(plan):
    big, small = plan.big, plan.small
    last = plan.steps - 1
    return (
        pl.BlockSpec((2 * plan.per, 4, C, big.cells), lambda i, r: (wide(i, last), 0, 0, 0)),
        pl.BlockSpec((plan.nsmall, 4, C, small.cells), lambda i, r: (0, 0, 0, 0)),
    )


def mode_spec(plan):
    return pl.BlockSpec((plan.n, plan.block, 2 * W), lambda i, r: (0, i, 0))


def store_modes(plan, ref, pair, z):
    z = z.reshape(plan.n, plan.own, 2 * W).astype(BF)
    ref[:, pair * plan.own : (pair + 1) * plan.own, :] = z


def load_modes(plan, ref, pair):
    return ref[:, pair * plan.own : (pair + 1) * plan.own, :].reshape(MODES, 2 * W)


def cost(flops, moved):
    return pl.CostEstimate(flops=flops, bytes_accessed=moved, transcendentals=0)


def flip(index, mask):
    result = index
    for b in range(mask.bit_length()):
        if mask >> b & 1:
            bit = lax.rem(lax.div(index, 1 << b), 2)
            result = result + (1 - 2 * bit) * (1 << b)
    return result


def tiles(v):
    return [v[:, 128 * t : 128 * t + 128] for t in range(v.shape[1] // 128)]


def sample_rows(first, second, third):
    lane = lax.broadcasted_iota(jnp.int32, third.shape, 1)
    a = jnp.concatenate([first, jnp.where(lane < 64, third, 0.0)], axis=1)
    b = jnp.concatenate([second, jnp.where(lane < 64, 0.0, third)], axis=1)
    return jnp.concatenate([a, b], axis=0)


def pair_tiles(a, b):
    lane = lax.broadcasted_iota(jnp.int32, (a.shape[0], 128), 1)
    return a[:, :128], b[:, :128], jnp.where(lane < 64, a[:, 128:], b[:, 128:])


def remote(src, dst, send, recv, device):
    return pltpu.make_async_remote_copy(
        src_ref=src, dst_ref=dst, send_sem=send, recv_sem=recv, device_id=device
    )


class Exchange:
    SCRATCH = 16

    @staticmethod
    def scratch(plan):
        n, chips, width = plan.n, plan.chips, 2 * W
        dma = pltpu.SemaphoreType.DMA
        part = (plan.chunks, 2)
        return [
            pltpu.VMEM((chips, plan.total, width), BF),
            pltpu.VMEM((2, chips, plan.chunks * plan.half, width), BF),
            pltpu.VMEM((2, chips, plan.chunks * plan.half, width), BF),
            pltpu.VMEM((chips, 2, plan.total, width), BF),
            pltpu.VMEM((3, plan.acc_rows, 128), F32),
            pltpu.VMEM((3, plan.acc_rows, 128), F32),
            dma((plan.chunks,)),
            dma((plan.chunks,)),
            dma(part + (plan.levels,)),
            dma(part + (plan.levels,)),
            dma(part + (chips,)),
            dma(part + (chips,)),
            dma(part + (chips,)),
            dma(part + (chips,)),
            dma((plan.chunks,)),
            pltpu.VMEM((plan.own, 256, 256), BF),
        ]

    def __init__(self, plan, part, out, refs):
        self.plan, self.part, self.out = plan, part, out
        (self.sib, self.sums, self.lev, self.res, self.acc, self.mixed,
         self.sib_s, self.sib_r, self.lev_s, self.lev_r, self.ag_s, self.ag_r,
         self.fw_s, self.fw_r, self.out_s, self.kernel) = refs
        self.me = lax.axis_index("rows")
        self.core = lax.rem(self.me, 2)

    def partners(self):
        return [flip(self.me, 1 << b) for b in range(self.plan.n.bit_length() - 1)]

    def to_sibling(self, c):
        rows = pl.ds(c * self.plan.crow, self.plan.crow)
        return remote(
            self.part.at[:, 1 - self.core, rows, :], self.sib.at[:, rows, :],
            self.sib_s.at[c], self.sib_r.at[c], {"rows": flip(self.me, 1)},
        )

    def level(self, c, h, t):
        plan = self.plan
        count = plan.chips >> (t + 1)
        rows = pl.ds(c * plan.half, plan.half)
        at = plan.chips - 2 * count
        return remote(
            self.sums.at[h, pl.ds(count, count), rows, :],
            self.lev.at[h, pl.ds(at, count), rows, :],
            self.lev_s.at[c, h, t], self.lev_r.at[c, h, t],
            {"rows": flip(self.me, 1 << plan.orders[h][t])},
        )

    def rows(self, c, h):
        return pl.ds(c * self.plan.crow + h * self.plan.half, self.plan.half)

    def block(self, c, h, owner):
        return self.res.at[lax.div(owner, 2), lax.rem(owner, 2), self.rows(c, h), :]

    def gather(self, c, h, u, idx):
        plan = self.plan
        sem = (1 << u) - 1 + idx
        ref = self.block(c, h, flip(self.me, plan.mask(h, idx)))
        return remote(
            ref, ref, self.ag_s.at[c, h, sem], self.ag_r.at[c, h, sem],
            {"rows": flip(self.me, 1 << plan.orders[h][plan.levels - 1 - u])},
        )

    def forward(self, c, h, idx):
        ref = self.block(c, h, flip(self.me, self.plan.mask(h, idx)))
        return remote(
            ref, ref, self.fw_s.at[c, h, idx], self.fw_r.at[c, h, idx],
            {"rows": flip(self.me, 1)},
        )

    def store(self, c):
        rows = pl.ds(c * self.plan.crow, self.plan.crow)
        return pltpu.make_async_copy(
            self.res.at[:, :, rows, :], self.out.at[:, :, rows, :], self.out_s.at[c]
        )

    def begin(self, c):
        self.to_sibling(c).start()

    def add_sibling(self, c):
        plan = self.plan
        self.to_sibling(c).wait_recv()
        for far in (1, 0):
            for h in range(2):
                span = plan.chips // 2
                for idx in range(far * span, far * span + span):
                    owner = flip(self.me, plan.mask(h, idx))
                    chip = lax.div(owner, 2)
                    rows = self.rows(c, h)
                    v = self.part[chip, self.core, rows, :].astype(F32)
                    v = v + self.sib[chip, rows, :].astype(F32)
                    self.sums[h, idx, pl.ds(c * plan.half, plan.half), :] = v.astype(BF)
                if far:
                    self.level(c, h, 0).start()

    def next_level(self, c, t):
        plan = self.plan
        rows = pl.ds(c * plan.half, plan.half)
        count = plan.chips >> t
        at = plan.chips - 2 * count
        for h in range(2):
            self.level(c, h, t - 1).wait_recv()
            for idx in reversed(range(count)):
                v = self.sums[h, idx, rows, :].astype(F32)
                v = v + self.lev[h, at + idx, rows, :].astype(F32)
                self.sums[h, idx, rows, :] = v.astype(BF)
                if idx == count // 2:
                    self.level(c, h, t).start()

    def finish_sum(self, c, scale):
        plan = self.plan
        rows = pl.ds(c * plan.half, plan.half)
        for h in range(2):
            self.level(c, h, plan.levels - 1).wait_recv()
            v = self.sums[h, 0, rows, :].astype(F32)
            v = (v + self.lev[h, plan.chips - 2, rows, :].astype(F32)) * scale
            for t, tile in enumerate(tiles(v)):
                self.acc[t, h * plan.half : (h + 1) * plan.half, :] = tile

    def mix(self, c, dims):
        plan = self.plan

        def one(m):
            rows = pl.ds(m, plan.slots, stride=plan.own)
            lhs = sample_rows(*(self.acc[t, rows, :] for t in range(3))).astype(BF)
            res = dot(lhs, self.kernel[m], dims)
            for t, tile in enumerate(pair_tiles(res[: plan.slots], res[plan.slots :])):
                self.mixed[t, rows, :] = tile

        unroll = 8

        @pl.loop(0, plan.own // unroll)
        def _(j):
            for u in range(unroll):
                one(j * unroll + u)

        result = jnp.concatenate([self.mixed[t, : plan.crow, :] for t in range(3)], axis=1)
        self.res[lax.div(self.me, 2), self.core, pl.ds(c * plan.crow, plan.crow), :] = (
            result.astype(BF)
        )
        for h in range(2):
            self.gather(c, h, 0, 0).start()
            self.forward(c, h, 0).start()

    def spread(self, c, u):
        for h in range(2):
            got = 1 << (u - 1)
            for idx in range(got):
                self.gather(c, h, u - 1, idx).wait_recv()
            if u < self.plan.levels:
                for idx in reversed(range(2 * got)):
                    self.gather(c, h, u, idx).start()
            for idx in range(got, 2 * got):
                self.forward(c, h, idx).start()

    def close(self, c):
        for h in range(2):
            for idx in range(self.plan.chips):
                self.forward(c, h, idx).wait_recv()
        self.store(c).start()

    def drain(self):
        plan = self.plan
        for c in range(plan.chunks):
            self.to_sibling(c).wait_send()
            for h in range(2):
                for t in range(plan.levels):
                    self.level(c, h, t).wait_send()
                for u in range(plan.levels):
                    for idx in range(1 << u):
                        self.gather(c, h, u, idx).wait_send()
                for idx in range(plan.chips):
                    self.forward(c, h, idx).wait_send()
            self.store(c).wait()

    def clear(self):
        plan = self.plan
        if plan.acc_rows > plan.crow:
            rest = plan.acc_rows - plan.crow
            self.acc[:, plan.crow :, :] = jnp.zeros((3, rest, 128), F32)

    def tasks(self, c, total):
        plan = self.plan
        todo = [lambda: self.begin(c), lambda: self.add_sibling(c)]
        todo += [lambda t=t: self.next_level(c, t) for t in range(1, plan.levels)]
        todo += [lambda: total(c)]
        todo += [lambda u=u: self.spread(c, u) for u in range(1, plan.levels + 1)]
        todo += [lambda: self.close(c)]
        return todo


def greet(devices):
    barrier = pltpu.get_barrier_semaphore()
    for device in devices:
        pl.semaphore_signal(barrier, inc=1, device_id=device)
    pl.semaphore_wait(barrier, len(devices))


def build_modes(plan, place, weights, kernel):
    flat = [weights[:, p].reshape(plan.own * C, C) for p in range(4)]
    for q in range(4):
        rows = None
        for p in range(4):
            term = dot(flat[p], place[p, :, 256 * q : 256 * q + 256])
            rows = term if rows is None else rows + term
        kernel[:, C * q : C * q + C, :] = rows.astype(BF).reshape(plan.own, C, 256)
    kernel[:, W:, :] = kernel[:, 128:W, :]


def plain_fields(plan):
    big, small = plan.big, plan.small
    last = plan.steps - 1
    return [
        pl.BlockSpec((2 * plan.per, 4, C, big.cells), lambda i: (wide(i, last), 0, 0, 0)),
        pl.BlockSpec((plan.nsmall, 4, C, small.cells), lambda i: (0, 0, 0, 0)),
    ]


def fixed(shape):
    return pl.BlockSpec(shape, lambda i: (0,) * len(shape))


ANYWHERE = pl.BlockSpec(memory_space=pl.ANY)


def forward_kernel(plan, x_big, x_small, spec_weight):
    big, small = plan.big, plan.small

    def kernel(xb, xs, fb, fs, place, weights, sb_all, ss_all, out, kernel_out, spectrum,
               part, sb, ss, table_sem, *refs):
        i = pl.program_id(0)
        ex = Exchange(plan, part, out, refs)
        loads = [
            pltpu.make_async_copy(sb_all.at[ex.me], sb, table_sem.at[0]),
            pltpu.make_async_copy(ss_all.at[ex.me], ss, table_sem.at[1]),
        ]
        keep = pltpu.make_async_copy(ex.kernel, kernel_out, table_sem.at[2])

        @pl.when(i == 0)
        def _():
            for load in loads:
                load.start()
            greet([{"rows": d} for d in ex.partners()])
            ex.clear()
            for load in loads:
                load.wait()

        def run(x, geo, first, second, count):
            parts = []
            for pair in range(count):
                def get(start, width):
                    v = x[2 * pair : 2 * pair + 2, :, :, start : start + width]
                    return v.reshape(2 * W, width)

                z = forward_pair(geo, get, first[...], second[...], 1.0 / geo.side)
                parts.append(z.reshape(plan.chips, 2, plan.own, 2 * W))
            parts += [jnp.zeros_like(parts[0])] * (plan.per - count)
            z = jnp.concatenate(parts, axis=2) if plan.per > 1 else parts[0]
            rows = pl.ds(pl.multiple_of(i * plan.block, 16), plan.block)
            part[:, :, rows, :] = z.astype(BF)

        @pl.when(i < plan.steps)
        def _():
            run(xb, big, fb, sb, plan.per)

        @pl.when(i == plan.steps)
        def _():
            run(xs, small, fs, ss, plan.nsmall // 2)

        def total(c):
            ex.finish_sum(c, 1.0)
            spectrum[pl.ds(c * plan.crow, plan.crow), :] = jnp.concatenate(
                [ex.acc[t, : plan.crow, :] for t in range(3)], axis=1
            ).astype(BF)
            ex.mix(c, ((1,), (0,)))

        def prepare():
            build_modes(plan, place, weights, ex.kernel)
            keep.start()

        starts = [(c + 1) * plan.span - 1 for c in range(plan.chunks)]
        schedule(plan, ex, i, total, starts, 2, [(starts[0], prepare)])

        @pl.when(i == plan.steps)
        def _():
            ex.drain()
            keep.wait()

    return pl.pallas_call(
        kernel,
        grid=(plan.count,),
        in_specs=[
            *plain_fields(plan),
            fixed(big.first.shape),
            fixed(small.first.shape),
            fixed((4, C, 1024)),
            fixed(spec_weight.shape),
            ANYWHERE,
            ANYWHERE,
        ],
        out_specs=[ANYWHERE, ANYWHERE, fixed((plan.total, 2 * W))],
        out_shape=[
            jax.ShapeDtypeStruct((plan.chips, 2, plan.total, 2 * W), BF),
            jax.ShapeDtypeStruct((plan.own, 256, 256), BF),
            jax.ShapeDtypeStruct((plan.total, 2 * W), BF),
        ],
        scratch_shapes=[
            pltpu.VMEM((plan.chips, 2, plan.total, 2 * W), BF),
            pltpu.VMEM(big.second.shape[1:], BF),
            pltpu.VMEM(small.second.shape[1:], BF),
            pltpu.SemaphoreType.DMA((3,)),
            *Exchange.scratch(plan),
        ],
        compiler_params=params(collective_id=1, has_side_effects=True),
        name="mode_forward",
    )(x_big, x_small, big.first, small.first, expand_tables(), spec_weight,
      big.second, small.second)


def schedule(plan, ex, i, total, starts, gap, hooks):
    last = plan.count - 1
    at = {}
    for c in range(plan.chunks):
        for k, task in enumerate(ex.tasks(c, total)):
            when = starts[c] + gap * k
            at.setdefault(min(when, last), []).append((when, c, task))
    for when, task in hooks:
        at.setdefault(min(when, last), []).append((when, -1, task))
    for step in sorted(at):
        @pl.when(i == step)
        def _(step=step):
            for _, _, task in sorted(at[step], key=lambda v: v[:2]):
                task()


def cells_pass(plan, rank, x_big, x_small, g_big, g_small, modes, lin_t, bias):
    k0 = math.sqrt(2.0 / math.pi)
    k1 = k0 * 0.044715

    def body(r, xb, xs, gb, gs, m, fb, sb, vb, eb, fs, ss, vs, es, kt, bias_ref,
             ob, os_, pb, ps, z, lin_acc, y_acc):
        i = pl.program_id(0)

        @pl.when(i == 0)
        def _():
            lin_acc[...] = jnp.zeros_like(lin_acc)
            y_acc[...] = jnp.zeros_like(y_acc)

        def run(x, g, o, d, geo, first, second, inverse, spread, count):
            wide_cells = 2 * geo.side
            lane = lax.broadcasted_iota(jnp.int32, (W, 128), 1)

            def main(at, q_all, p):
                lo = p * wide_cells
                cells = slice(lo, lo + wide_cells)
                q = q_all[:, 128 * (p // 2) : 128 * (p // 2) + 128]
                xv = x[at, :, :, cells].reshape(W, wide_cells)
                if p % 2 == 0:
                    tail = jnp.where(lane < 64, q, kt[:, 128:256])
                    rhs = [xv[:128], spread[...], xv[128:]]
                else:
                    tail = jnp.where(lane >= 64, q, kt[:, 256:384])
                    rhs = [xv[:128], xv[128:], spread[...]]
                lhs = jnp.concatenate([kt[:, :128], tail], axis=1)
                b = dot(lhs, jnp.concatenate(rhs, axis=0))
                s = b * b
                t = jnp.tanh(b * (2.0 * k0 + 8.0 * k1 * s))
                e = 1.0 + t
                o[at, :, :, cells] = (xv + (b * e).astype(BF)).reshape(4, C, wide_cells)
                slope = e * (0.5 + b * (k0 + 12.0 * k1 * s) * (1.0 - t))
                gv = g[at, :, :, cells].reshape(W, wide_cells)
                d[at, :, :, cells] = (gv * slope.astype(BF)).reshape(4, C, wide_cells)

            def weight_grad(at):
                xa = x[at, :, :, :].reshape(W, geo.cells)
                pa = d[at, :, :, :].reshape(W, geo.cells)
                lin_acc[...] += dot(xa, pa, ((1,), (1,)))

            def keep(y):
                y_acc[...] += y

            for pair in range(count):
                qs = inverse_pair(geo, load_modes(plan, m, pair), inverse[...], 0.5 / MX)
                for s in range(2):
                    q_all = qs[s] + jnp.concatenate([bias_ref[...]] * (geo.qlanes // 128), axis=1)
                    for p in range(geo.npairs):
                        main(2 * pair + s, q_all, p)
                    weight_grad(2 * pair + s)

                def get(start, width):
                    v = d[2 * pair : 2 * pair + 2, :, :, start : start + width]
                    return v.reshape(2 * W, width)

                out = forward_pair(geo, get, first[...], second[...], 1.0, keep)
                store_modes(plan, z, pair, out)

        @pl.when(i < plan.steps)
        def _():
            run(xb, gb, ob, pb, plan.big, fb, sb, vb, eb, plan.per)

        @pl.when(i == plan.steps)
        def _():
            if plan.nsmall // 2 < plan.per:
                z[...] = jnp.zeros_like(z)
            run(xs, gs, os_, ps, plan.small, fs, ss, vs, es, plan.nsmall // 2)

    big, small = plan.big, plan.small
    tables = []
    specs = []
    for geo in (big, small):
        tables += [geo.first, geo.second, geo.inverse, geo.pair_spread]
        specs += [
            const_spec(geo.first.shape),
            device_spec(geo.second.shape[1:]),
            device_spec(geo.inverse.shape[1:]),
            const_spec(geo.pair_spread.shape),
        ]
    return pl.pallas_call(
        body,
        grid_spec=pltpu.PrefetchScalarGridSpec(
            num_scalar_prefetch=1,
            grid=(plan.count,),
            in_specs=[
                *field_specs(plan),
                *field_specs(plan),
                mode_spec(plan),
                *specs,
                const_spec(lin_t.shape),
                const_spec(bias.shape),
            ],
            out_specs=[
                *field_specs(plan),
                *field_specs(plan),
                mode_spec(plan),
                const_spec((W, W)),
                const_spec((W, 256)),
            ],
        ),
        out_shape=[
            jax.ShapeDtypeStruct(x_big.shape, BF),
            jax.ShapeDtypeStruct(x_small.shape, BF),
            jax.ShapeDtypeStruct(x_big.shape, BF),
            jax.ShapeDtypeStruct(x_small.shape, BF),
            jax.ShapeDtypeStruct((plan.n, plan.total, 2 * W), BF),
            jax.ShapeDtypeStruct((W, W), F32),
            jax.ShapeDtypeStruct((W, 256), F32),
        ],
        compiler_params=params(),
        name="cells",
    )(rank, x_big, x_small, g_big, g_small, modes, *tables, lin_t, bias)


def backward_kernel(plan, part, p_big, p_small, g_big, g_small, kernel_all, spectrum, lin,
                    lin_grad, columns):
    big, small = plan.big, plan.small
    stages = plan.n.bit_length() - 1 + plan.nz.bit_length() - 1
    rows_bits = plan.n.bit_length() - 1
    pick_all, move_all, move_lin = fold_tables()
    zero_lanes = np.zeros((8, 256), np.float32)
    zero_lanes[0, : 128 : MX] = 1.0

    def kernel(pb, ps, gb, gs, kk, spec, lin_in, col_in, pick, move, shift, line, part_in, kernel_in,
               db, ds, out, weight_out, lin_out,
               part, sa, mb, dacc, send_z, recv_z, lin_buf, lin_recv,
               in_sem, zs, zr, ls, lr, *refs):
        i = pl.program_id(0)
        ex = Exchange(plan, part, out, refs)
        here = lax.axis_index("samples")
        loads = [
            pltpu.make_async_copy(part_in, part, in_sem.at[0]),
            pltpu.make_async_copy(kernel_in, ex.kernel, in_sem.at[1]),
        ]

        def z_peer(d):
            return lax.rem(here + d, plan.nz)

        def to_z(d):
            return remote(
                send_z.at[z_peer(d)], recv_z.at[d], zs.at[d], zr.at[d], {"samples": z_peer(d)}
            )

        def lin_partner(k):
            if k < rows_bits:
                return {"rows": flip(ex.me, 1 << k)}
            return {"samples": flip(here, 1 << (k - rows_bits))}

        def lin_step(k):
            return remote(lin_buf.at[k], lin_recv.at[k], ls.at[k], lr.at[k], lin_partner(k))

        @pl.when(i == 0)
        def _():
            for load in loads:
                load.start()
            greet([{"rows": d} for d in ex.partners()]
                  + [{"samples": z_peer(d)} for d in range(1, plan.nz)])
            ex.clear()
            folded = None
            for q in range(4):
                term = lax.dot_general(
                    lin_in[C * q : C * q + C, :], shift[q], (((1,), (0,)), ((), ())),
                    precision=lax.Precision.HIGHEST, preferred_element_type=F32,
                )
                folded = term if folded is None else folded + term
            lin_buf[0, :C, :] = folded
            lin_buf[0, C:, :] = lax.dot_general(
                line[...], col_in[...], (((1,), (1,)), ((), ())),
                precision=lax.Precision.HIGHEST, preferred_element_type=F32,
            )
            lin_step(0).start()
            sa[...] = jnp.zeros_like(sa)
            mb[...] = jnp.zeros_like(mb)
            dacc[...] = jnp.zeros_like(dacc)
            send_z[...] = jnp.zeros_like(send_z)
            for load in loads:
                load.wait()

        def run(p, g, d, geo, count):
            for at in range(2 * count):
                v = dot(kk[...], p[at, :, :, :].reshape(W, geo.cells))
                v = g[at, :, :, :].reshape(W, geo.cells) + v.astype(BF)
                d[at, :, :, :] = v.reshape(4, C, geo.cells)

        @pl.when(i < plan.steps)
        def _():
            run(pb, gb, db, big, plan.per)

        @pl.when(i == plan.steps)
        def _():
            run(ps, gs, ds, small, plan.nsmall // 2)

        def total(c):
            ex.finish_sum(c, 1.0 / MX)
            ex.mix(c, ((1,), (1,)))

        def weight_grad(c):
            crow = plan.crow
            grads = sample_rows(*(ex.acc[t, :crow, :] for t in range(3))).astype(BF)
            held = spec[pl.ds(c * crow, crow), :].astype(F32)
            spectra = sample_rows(*tiles(held)).astype(BF)
            for t, tile in enumerate(tiles(dot(spectra, pick[...]))):
                sa[t, 0, :crow, :] = tile[:crow]
                sa[t, 1, :crow, :] = tile[crow:]
            for t, tile in enumerate(tiles(dot(grads, move[...]))):
                mb[t, 0, :crow, :] = tile[:crow]
                mb[t, 1, :crow, :] = tile[crow:]

            def one(m):
                rows = pl.ds(m, plan.slots, stride=plan.own)
                left = [sa[q, s, rows, :] for q in range(4) for s in range(2)]
                right = [
                    jnp.concatenate([mb[2 * q, s, rows, :], mb[2 * q + 1, s, rows, :]], axis=1)
                    for q in range(4) for s in range(2)
                ]
                v = dot(
                    jnp.concatenate(left, axis=0).astype(BF),
                    jnp.concatenate(right, axis=0).astype(BF),
                    ((0,), (0,)),
                )
                dacc[m] += v[:C]

            unroll = 4

            @pl.loop(0, plan.own // unroll)
            def _(j):
                for u in range(unroll):
                    one(j * unroll + u)

        def send_weights():
            pairs = []
            for j in range(plan.own // 2):
                pairs.append(jnp.concatenate(pair_tiles(dacc[2 * j], dacc[2 * j + 1]), axis=1))
            rows = jnp.concatenate(pairs, axis=0).astype(BF)
            for z in range(plan.nz):
                lo = z * plan.zrows
                hi = min(lo + plan.zrows, plan.wrows)
                if hi > lo:
                    send_z[z, : hi - lo, :] = rows[lo:hi]
            for d in range(1, plan.nz):
                to_z(d).start()

        def sum_weights():
            v = send_z[here].astype(F32)
            for d in range(1, plan.nz):
                to_z(d).wait_recv()
                v = v + recv_z[d].astype(F32)
            weight_out[...] = v.astype(BF)

        def lin_next(k):
            lin_step(k).wait_recv()
            v = lin_buf[k] + lin_recv[k]
            if k + 1 < stages:
                lin_buf[k + 1] = v
                lin_step(k + 1).start()
            else:
                lin_out[...] = v

        def chunk_total(c):
            ex.finish_sum(c, 1.0 / MX)
            weight_grad(c)
            ex.mix(c, ((1,), (1,)))
            if c == plan.chunks - 1:
                send_weights()

        last = plan.count - 1
        hooks = [(2 * k + 1, lambda k=k: lin_next(k)) for k in range(stages)]
        hooks.append((4 * plan.count, sum_weights))
        starts = [c for c in range(plan.chunks)]
        schedule(plan, ex, i, chunk_total, starts, 2, hooks)

        @pl.when(i == last)
        def _():
            ex.drain()
            for d in range(1, plan.nz):
                to_z(d).wait_send()
            for k in range(stages):
                lin_step(k).wait_send()

    acc = plan.acc_rows
    dma = pltpu.SemaphoreType.DMA
    return pl.pallas_call(
        kernel,
        grid=(plan.count,),
        in_specs=[
            *plain_fields(plan),
            *plain_fields(plan),
            fixed((W, W)),
            fixed((plan.total, 2 * W)),
            fixed((W, W)),
            fixed((W, 256)),
            fixed(pick_all.shape),
            fixed(move_all.shape),
            fixed(move_lin.shape),
            fixed(zero_lanes.shape),
            ANYWHERE,
            ANYWHERE,
        ],
        out_specs=[
            *plain_fields(plan),
            ANYWHERE,
            fixed((plan.zrows, 2 * W)),
            fixed((C + 8, W)),
        ],
        out_shape=[
            jax.ShapeDtypeStruct(p_big.shape, BF),
            jax.ShapeDtypeStruct(p_small.shape, BF),
            jax.ShapeDtypeStruct((plan.chips, 2, plan.total, 2 * W), BF),
            jax.ShapeDtypeStruct((plan.zrows, 2 * W), BF),
            jax.ShapeDtypeStruct((C + 8, W), F32),
        ],
        scratch_shapes=[
            pltpu.VMEM((plan.chips, 2, plan.total, 2 * W), BF),
            pltpu.VMEM((4, 2, acc, 128), F32),
            pltpu.VMEM((8, 2, acc, 128), F32),
            pltpu.VMEM((plan.own, C, 256), F32),
            pltpu.VMEM((plan.nz, plan.zrows, 2 * W), BF),
            pltpu.VMEM((plan.nz, plan.zrows, 2 * W), BF),
            pltpu.VMEM((stages, C + 8, W), F32),
            pltpu.VMEM((stages, C + 8, W), F32),
            dma((2,)),
            dma((plan.nz,)),
            dma((plan.nz,)),
            dma((stages,)),
            dma((stages,)),
            *Exchange.scratch(plan),
        ],
        compiler_params=params(collective_id=2, has_side_effects=True),
        name="mode_backward",
    )(p_big, p_small, g_big, g_small, lin, spectrum, lin_grad, columns,
      pick_all, move_all, move_lin, zero_lanes, part, kernel_all)


def input_grads(plan, rank, part_big, part_small, modes):
    def body(r, pb, ps, m, vb, eb, vs, es, db, ds):
        i = pl.program_id(0)

        def run(part, d, geo, inverse, spread, count):
            span = spread.shape[1]
            for pair in range(count):
                qs = inverse_pair(geo, load_modes(plan, m, pair), inverse[...], 1.0)
                q = jnp.concatenate(qs, axis=0) * jnp.asarray(1.0 / geo.side, BF)
                for j in range(geo.cells // span):
                    v = dot(q[:, 128 * j : 128 * j + 128], spread[...])
                    at = (slice(2 * pair, 2 * pair + 2), slice(None), slice(None),
                          slice(j * span, (j + 1) * span))
                    d[at] = part[at].astype(F32) + v.reshape(2, 4, C, span)

        @pl.when(i < plan.steps)
        def _():
            run(pb, db, plan.big, vb, eb, plan.per)

        @pl.when(i == plan.steps)
        def _():
            run(ps, ds, plan.small, vs, es, plan.nsmall // 2)

    tables = []
    specs = []
    for geo in (plan.big, plan.small):
        tables += [geo.inverse, geo.spread]
        specs += [device_spec(geo.inverse.shape[1:]), const_spec(geo.spread.shape)]
    return pl.pallas_call(
        body,
        grid_spec=pltpu.PrefetchScalarGridSpec(
            num_scalar_prefetch=1,
            grid=(plan.steps + 1,),
            in_specs=[*field_specs(plan), mode_spec(plan), *specs],
            out_specs=[*field_specs(plan)],
        ),
        out_shape=[
            jax.ShapeDtypeStruct(part_big.shape, F32),
            jax.ShapeDtypeStruct(part_small.shape, F32),
        ],
        compiler_params=params(),
        name="input_grads",
    )(rank, part_big, part_small, modes, *tables)


def on_device(plan, x_big, x_small, spec_weight, lin_weight, lin_bias, grad_big, grad_small):
    rank = lax.axis_index("rows").reshape(1)
    lin = build_kernel(lin_weight)
    half = lin.T * jnp.asarray(0.5, BF)
    zero = jnp.zeros((W, 64), BF)
    half = jnp.concatenate([half[:, :128], zero, half[:, 128:], half[:, 128:], zero], axis=1)
    bias_lane = np.arange(128) % (2 * MX) == MX
    bias = lin_bias.reshape(W, 1) * jnp.asarray(0.5 * bias_lane, BF)

    whole = (plan.n, plan.total, 2 * W)
    modes, kernel, spectrum = forward_kernel(plan, x_big, x_small, spec_weight)
    out_big, out_small, pre_big, pre_small, part, lin_grad, columns = cells_pass(
        plan, rank, x_big, x_small, grad_big, grad_small, modes.reshape(whole), half, bias
    )
    part_big, part_small, modes, weight_part, lin_sum = backward_kernel(
        plan, part.reshape(plan.chips, 2, plan.total, 2 * W), pre_big, pre_small,
        grad_big, grad_small, kernel, spectrum, lin, lin_grad, columns,
    )
    here = lax.axis_index("samples")
    pieces = [weight_part]
    for d in range(1, plan.nz):
        pairs = [(z, (z + d) % plan.nz) for z in range(plan.nz)]
        pieces.append(lax.ppermute(weight_part, "samples", pairs))
    dx_big, dx_small = input_grads(plan, rank, part_big, part_small, modes.reshape(whole))
    order = lax.rem(here - jnp.arange(plan.nz) + plan.nz, plan.nz)
    rows = jnp.stack(pieces)[order].reshape(plan.nz * plan.zrows, 2 * W)
    rows = rows[: plan.wrows].reshape(plan.own // 2, C, 2 * W)
    even = jnp.concatenate([rows[..., :128], rows[..., 256:320]], axis=-1)
    odd = jnp.concatenate([rows[..., 128:256], rows[..., 320:]], axis=-1)
    spec_grad = jnp.stack([even, odd], axis=1).reshape(plan.own, C, 4, C)
    spec_grad = spec_grad.transpose(0, 2, 1, 3).astype(F32)
    lin_weight_grad = lin_sum[:C].reshape(C, 4, C).transpose(1, 0, 2)
    lin_bias_grad = lin_sum[C].reshape(4, C)
    return out_big, out_small, dx_big, dx_small, spec_grad, lin_weight_grad, lin_bias_grad


def solution(mesh):
    fields = P("samples", None, None, "rows")
    spec = P("rows", None, None, None)

    def run(x_big, x_small, *rest):
        count = mesh.shape["samples"]
        plan = Plan(mesh, x_big.shape[0] // count, x_small.shape[0] // count)

        def local(*args):
            return on_device(plan, *args)

        return jax.shard_map(
            local,
            mesh=mesh,
            in_specs=(fields, fields, spec, P(), P(), fields, fields),
            out_specs=(fields, fields, fields, fields, spec, P(), P()),
            check_vma=False,
        )(x_big, x_small, *rest)

    return run
```

time: 296 us -> 222 us (0.75)
  blocking collectives: 43.1 us -> 0 us
  Pallas kernels: 220 us -> 198 us
  between operations: 14.2 us -> 0.77 us
  starting transfers between devices: 0.04 us -> 6.41 us
    psum x1 -> x0, blocking collectives: 43.1 us -> none  [on_device(): lax.psum((fold_kernel(lin_grad), bias_grad.reshape(4, C)), ('samples', 'r...]
    pallas_call x1, Pallas kernels: 71.2 us -> 55.2 us  [cells_pass(): pl.pallas_call(body, grid_spec=pltpu.PrefetchScalarGridSpec(num_scalar_pr...]
    ppermute x0 -> x3, starting transfers between devices: none -> 6.41 us  [on_device(): pieces.append(lax.ppermute(weight_part, 'samples', pairs))]
    pallas_call x3 -> x2, Pallas kernels: 119 us -> 113 us  [the longest x1 59.2 us: forward_kernel(): pl.pallas_call(kernel, grid=(plan.count,), in_specs=[*plain_fields(plan),...]
    another operation x4 -> x2, other arithmetic: 4.2 us -> 0.27 us  [the longest x1 0.18 us: on_device(): spec_grad = jnp.stack([even, odd], axis=1).reshape(plan.own, C, 4, C)]
    slice x8 -> x4, local copies, waits for them, and re-layouts: 5.25 us -> 1.71 us  [the longest x1 0.8 us: on_device(): lin_weight_grad = lin_sum[:C].reshape(C, 4, C).transpose(1, 0, 2)]
    convert_element_type x0 -> x1, local copies, waits for them, and re-layouts: none -> 3.04 us  [on_device(): spec_grad = spec_grad.transpose(0, 2, 1, 3).astype(F32)]
  transfers between devices with their start and end apart: 1 -> 3, of which waited for: 0 -> 0; matrix products, arithmetic and copies ran while one was open for 0% -> 1% of each run, Pallas kernels for 10% -> 13%
where the time goes in v2:
time: 222 us; the launch traced here: 221 us
  Pallas kernels  198 us (89%)
  local copies, waits for them, and re-layouts  11.1 us (5%)
  starting transfers between devices  6.41 us (3%)
  other arithmetic  4.48 us (2%)
    pallas_call x1, Pallas kernels, forward_kernel(): pl.pallas_call(kernel, grid=(plan.count,), in_specs=[*plain_fields(plan),...  59.2 us
    pallas_call x1, Pallas kernels, cells_pass(): pl.pallas_call(body, grid_spec=pltpu.PrefetchScalarGridSpec(num_scalar_pr...  55.2 us
    pallas_call x1, Pallas kernels, backward_kernel(): pl.pallas_call(kernel, grid=(plan.count,), in_specs=[*plain_fields(plan),...  53.8 us
    pallas_call x1, Pallas kernels, input_grads(): pl.pallas_call(body, grid_spec=pltpu.PrefetchScalarGridSpec(num_scalar_pr...  29.7 us
    ppermute x3, starting transfers between devices, on_device(): pieces.append(lax.ppermute(weight_part, 'samples', pairs))  6.41 us
  transfers between devices with their start and end apart: 3, of which 0 were waited for; matrix products, arithmetic and copies ran while one was open for 1% of the time, Pallas kernels for 13%

profile of v2, /device:TPU:0, one launch (start us, length us, event | category | flops | bytes accessed | tf_op | source)
XLA Modules:
  0.0 220.7 jit_solution(13979567959791265593)
XLA Ops:
  0.6 0.8 slice_bitcast_fusion.1
  1.4 0.7 fusion.3
  2.1 0.8 multiply_bitcast_fusion
  3.0 0.8 copy.32.kt
  3.7 0.8 mul.27
  4.5 1.4 broadcast_multiply_fusion.bias_ref
  5.9 59.2 %mode_forward.1 = (bf16[4,2,480,384]{3,2,1,0:T(8,128)(2,1)}, bf16[32,256,256]{2,1,0:T(8,128)(2,1)}, bf16[480,384]{1,0:T(8,128)(2,1)}) custom-call(bf16[28,4,48,2048]{3,2,1,0:T(8,128)(2,1)} %xb.3, bf16[2,4,48,512]{3,2,1,0:T(8,128)(2,1)} %xs.3, bf16[1024,256]{1,0:T(8,128)(2,1)} %constant.52.clone.fb, bf16[512,256]{1,0:T(8,128)(2,1)} %constant.53.clone.fs, ...), custom_call_target="tpu_custom_call" | custom-call | tf_op jit(solution)/shard_map/mode_forward/pallas_call | solution.py:591
  65.1 55.2 %cells.1 = (bf16[28,4,48,2048]{3,2,1,0:T(8,128)(2,1)}, bf16[2,4,48,512]{3,2,1,0:T(8,128)(2,1)}, bf16[28,4,48,2048]{3,2,1,0:T(8,128)(2,1)}, bf16[2,4,48,512]{3,2,...) custom-call(s32[1]{0:T(128)} %bitcast.r, bf16[28,4,48,2048]{3,2,1,0:T(8,128)(2,1)} %xb.3, ...), custom_call_target="tpu_custom_call" | custom-call | tf_op jit(solution)/shard_map/cells/pallas_call | solution.py:720
  120.3 53.8 %mode_backward.1 = (bf16[28,4,48,2048]{3,2,1,0:T(8,128)(2,1)}, bf16[2,4,48,512]{3,2,1,0:T(8,128)(2,1)}, bf16[4,2,480,384]{3,2,1,0:T(8,128)(2,1)}, bf16[192,384]{1,0:T(8,128)(2,1)}, f32[56,192]{1,0:T(8,128)}) custom-call(bf16[28,4,48,2048]{3,2,1,0:T(8,128)(2,1)} %get-tuple-element.27.pb, bf16[2,4,48,512]{3,2,1,0:T(8,128)(2,1)} %get-tuple-element.28.ps, ...), custom_call_target="tpu_custom_call" | custom-call | tf_op jit(solution)/shard_map/mode_backward/pallas_call | solution.py:922
  174.1 5.8 %collective-permute-start.2 = (bf16[192,384]{1,0:T(8,128)(2,1)}, bf16[192,384]{1,0:T(8,128)(2,1)S(1)}, u32[]{:S(2)}, u32[]{:S(2)}) collective-permute-start(bf16[192,384]{1,0:T(8,128)(2,1)} %get-tuple-element.39), channel_id=1, source_target_pairs={{0,24},{8,0},{16,8},{24,16},{1,25},{9,1},{17,9},{25,17},{2,26},{10... | collective-permute-start | bytes 442376 | tf_op jit(solution)/shard_map/ppermute | solution.py:1041
  179.8 0.6 collective-permute-start
  180.5 0.7 slice_reduce_fusion
  181.2 0.8 slice.59
  182.0 0.1 reshape.76
  182.1 0.6 copy.37
  182.8 0.7 reshape_squeeze.3
  183.4 29.7 %input_grads.1 = (f32[28,4,48,2048]{3,2,1,0:T(8,128)}, f32[2,4,48,512]{3,2,1,0:T(8,128)}) custom-call(s32[1]{0:T(128)} %bitcast.r, bf16[28,4,48,2048]{3,2,1,0:T(8,128)(2,1)} %get-tuple-element.34.pb, bf16[2,4,48,512]{3,2,1,0:T(8,128)(2,1)} %get-tuple-element.35.ps, bf16[8,480,384]{2,1,0:T(8,128)(2,1)} %bitcast.40, bf16[8,256,1024]{2,1,0:T(8,128)(2,1)} %constant.57.clone.vb, ...), custom_call_target="tpu_custom_call" | custom-call | tf_op jit(solution)/shard_map/input_grads/pallas_call | solution.py:1002
  213.2 0.1 pad_maximum_fusion
  213.3 0.7 gather_fusion
  214.0 0.1 fusion.5
  214.2 0.2 maximum_bitcast_fusion
  214.3 1.3 maximum_convert_fusion
  215.7 3.0 %reshape.77 = f32[32,48,4,48]{3,2,1,0:T(4,128)S(1)} reshape(f32[16,2,48,192]{3,2,1,0:T(8,128)} %maximum_convert_fusion) | data formatting | bytes 2359296 | tf_op jit(solution)/shard_map/convert_element_type | solution.py:1049
  218.7 2.0 copy.35
  (14 shorter events, 0.1 us)
Async XLA Ops:
  174.1 39.1 %collective-permute-start.2 = (bf16[192,384]{1,0:T(8,128)(2,1)}, bf16[192,384]{1,0:T(8,128)(2,1)S(1)}, u32[]{:S(2)}, u32[]{:S(2)}) collective-permute-start(bf16[192,384]{1,0:T(8,128)(2,1)} %get-tuple-element.39), channel_id=1, source_target_pairs={{0,24},{8,0},{16,8},{24,16},{1,25},{9,1},{17,9},{25,17},{2,26},{10... | collective-permute-start | bytes 442376 | tf_op jit(solution)/shard_map/ppermute | solution.py:1041
  179.8 33.3 %collective-permute-start.1 = (bf16[192,384]{1,0:T(8,128)(2,1)}, bf16[192,384]{1,0:T(8,128)(2,1)S(1)}, u32[]{:S(2)}, u32[]{:S(2)}) collective-permute-start(bf16[192,384]{1,0:T(8,128)(2,1)} %get-tuple-element.39), channel_id=1, source_target_pairs={{0,16},{8,24},{16,0},{24,8},{1,17},{9,25},{17,1},{25,9},{2,18},{10... | collective-permute-start | bytes 442376 | tf_op jit(solution)/shard_map/ppermute | solution.py:1041
  179.8 33.3 %collective-permute-start = (bf16[192,384]{1,0:T(8,128)(2,1)}, bf16[192,384]{1,0:T(8,128)(2,1)S(1)}, u32[]{:S(2)}, u32[]{:S(2)}) collective-permute-start(bf16[192,384]{1,0:T(8,128)(2,1)} %get-tuple-element.39), channel_id=1, source_target_pairs={{0,8},{8,16},{16,24},{24,0},{1,9},{9,17},{17,25},{25,1},{2,10},{10... | collective-permute-start | bytes 442376 | tf_op jit(solution)/shard_map/ppermute | solution.py:1041
  183.4 29.7 %copy-start = (bf16[192,384]{1,0:T(8,128)(2,1)S(1)}, bf16[192,384]{1,0:T(8,128)(2,1)}, u32[]{:S(2)}) copy-start(bf16[192,384]{1,0:T(8,128)(2,1)} %get-tuple-element.39) | copy-start | bytes 442372

commit v3 on v2

--- a/solution.py
+++ b/solution.py
@@ -90,25 +90,35 @@
     return lax.dot_general(a, b, (dims, ((), ())), preferred_element_type=F32)
 
 
-def forward_pair(geo, get, first, second, scale, keep=None):
-    width = geo.group * geo.side
-    parts = []
-    for g in range(geo.ngroups):
-        y = dot(get(g * width, width), first)
-        if keep is not None:
-            keep(y[:W] + y[W:])
-        parts.append(y)
+def forward_group(field, first, scale, keep=None):
+    y = dot(field, first)
+    grids = range(y.shape[0] // W)
+    if keep is not None:
+        keep(sum(y[W * s : W * s + W, :128] for s in grids))
+    cols = []
+    for s in grids:
+        col = y[W * s : W * s + W, :128] + turn(y[W * s : W * s + W, 128:])
+        cols.append((col * scale).astype(BF))
+    return cols
+
+
+def forward_rows(groups, second):
     stacked = []
     for s in range(2):
-        cols = []
-        for y in parts:
-            col = y[W * s : W * s + W, :128] + turn(y[W * s : W * s + W, 128:])
-            cols.append((col * scale).astype(BF))
-        col = jnp.concatenate(cols, axis=1) if len(cols) > 1 else cols[0]
-        stacked.append(jnp.concatenate([col, turn(col)], axis=1))
+        cols = [cols[s] for cols in groups]
+        stacked.append(jnp.concatenate(cols + [turn(col) for col in cols], axis=1))
     a, b = stacked
     both = jnp.concatenate([a[:128], b[:128], a[128:], b[128:]], axis=0)
     return dot(second, both, ((1,), (1,)))
+
+
+def forward_grids(geo, get, first, second, scale):
+    width = geo.group * geo.side
+    groups = [forward_group(get(g * width, width), first, scale) for g in range(geo.ngroups)]
+    return [
+        forward_rows([cols[2 * k : 2 * k + 2] for cols in groups], second)
+        for k in range(len(groups[0]) // 2)
+    ]
 
 
 def inverse_pair(geo, modes, inverse, scale):
@@ -121,36 +131,6 @@
         q = part[:, : geo.qlanes] + turn(part[:, geo.qlanes :])
         result.append((q * scale).astype(BF))
     return result
-
-
-def build_kernel(weights):
-    rows_list = []
-    for source in range(4):
-        blocks = []
-        for target in range(4):
-            blade_id = source ^ target
-            block_part = weights[..., blade_id, :, :]
-            if blade_id >> 1 & source & 1:
-                block_part = -block_part
-            blocks.append(block_part)
-        rows_list.append(jnp.concatenate(blocks, axis=-1))
-    return jnp.concatenate(rows_list, axis=-2)
-
-
-def fold_kernel(kernel_grad):
-    blades = []
-    for blade_id in range(4):
-        summed = None
-        for source in range(4):
-            target = source ^ blade_id
-            block_part = kernel_grad[
-                ..., source * C : (source + 1) * C, target * C : (target + 1) * C
-            ]
-            if blade_id >> 1 & source & 1:
-                block_part = -block_part
-            summed = block_part if summed is None else summed + block_part
-        blades.append(summed)
-    return jnp.stack(blades, axis=-3)
 
 
 def fold_tables():
@@ -180,7 +160,7 @@
             o = p ^ q
             full[:, o * C : (o + 1) * C] = sign * np.eye(C)
             place[p, :, q] = full[:, dup]
-    return low(place.reshape(4, C, 1024))
+    return low(place.reshape(W, 1024))
 
 
 class Plan:
@@ -195,6 +175,8 @@
         assert nbig % (2 * self.per) == 0 and nsmall % 2 == 0 and nsmall // 2 <= self.per
         self.steps = nbig // (2 * self.per)
         self.count = self.steps + 1
+        self.wide_per = 2 * self.per if self.steps % 2 == 0 else self.per
+        self.wide_steps = nbig // (2 * self.wide_per)
         self.block = self.per * self.own
         self.total = self.count * self.block
         self.chunks = next(c for c in (3, 2, 1) if self.count % c == 0)
@@ -289,6 +271,51 @@
     return pltpu.make_async_remote_copy(
         src_ref=src, dst_ref=dst, send_sem=send, recv_sem=recv, device_id=device
     )
+
+
+class Stream:
+    def __init__(self, field, ring, sems, grids):
+        self.field, self.ring, self.sems, self.grids = field, ring, sems, grids
+        self.depth = ring.shape[0]
+
+    @staticmethod
+    def scratch(depth, grids, cells):
+        return [pltpu.VMEM((depth, grids, 4, C, cells), BF), pltpu.SemaphoreType.DMA((depth,))]
+
+    def slot(self, i):
+        return self.ring.at[lax.rem(i, self.depth)]
+
+    def copy(self, i, out=False):
+        block = self.field.at[pl.ds(i * self.grids, self.grids)]
+        sem = self.sems.at[lax.rem(i, self.depth)]
+        if out:
+            return pltpu.make_async_copy(self.slot(i), block, sem)
+        return pltpu.make_async_copy(block, self.slot(i), sem)
+
+    def read(self, i, count):
+        @pl.when(i == 0)
+        def _():
+            for k in range(min(self.depth, count)):
+                self.copy(jnp.int32(k)).start()
+
+        self.copy(i).wait()
+        return self.slot(i)
+
+    def ahead(self, i, count):
+        @pl.when(i + self.depth < count)
+        def _():
+            self.copy(i + self.depth).start()
+
+    def reserve(self, i):
+        @pl.when(i >= self.depth)
+        def _():
+            self.copy(i - self.depth, True).wait()
+
+        return self.slot(i)
+
+    def flush(self, count):
+        for k in range(max(0, count - self.depth), count):
+            self.copy(jnp.int32(k), True).wait()
 
 
 class Exchange:
@@ -318,8 +345,9 @@
             pltpu.VMEM((plan.own, 256, 256), BF),
         ]
 
-    def __init__(self, plan, part, out, refs):
+    def __init__(self, plan, part, out, refs, origin=None):
         self.plan, self.part, self.out = plan, part, out
+        self.origin = part if origin is None else origin
         (self.sib, self.sums, self.lev, self.res, self.acc, self.mixed,
          self.sib_s, self.sib_r, self.lev_s, self.lev_r, self.ag_s, self.ag_r,
          self.fw_s, self.fw_r, self.out_s, self.kernel) = refs
@@ -332,7 +360,7 @@
     def to_sibling(self, c):
         rows = pl.ds(c * self.plan.crow, self.plan.crow)
         return remote(
-            self.part.at[:, 1 - self.core, rows, :], self.sib.at[:, rows, :],
+            self.origin.at[:, 1 - self.core, rows, :], self.sib.at[:, rows, :],
             self.sib_s.at[c], self.sib_r.at[c], {"rows": flip(self.me, 1)},
         )
 
@@ -481,14 +509,20 @@
             rest = plan.acc_rows - plan.crow
             self.acc[:, plan.crow :, :] = jnp.zeros((3, rest, 128), F32)
 
-    def tasks(self, c, total):
+    def waves(self, total):
         plan = self.plan
-        todo = [lambda: self.begin(c), lambda: self.add_sibling(c)]
-        todo += [lambda t=t: self.next_level(c, t) for t in range(1, plan.levels)]
-        todo += [lambda: total(c)]
-        todo += [lambda u=u: self.spread(c, u) for u in range(1, plan.levels + 1)]
-        todo += [lambda: self.close(c)]
-        return todo
+        todo = []
+        for c in range(plan.chunks):
+            chain = [lambda c=c, t=t: self.next_level(c, t) for t in range(1, plan.levels)]
+            chain += [lambda c=c: total(c)]
+            chain += [lambda c=c, u=u: self.spread(c, u) for u in range(1, plan.levels + 1)]
+            chain += [lambda c=c: self.close(c)]
+            todo.append(chain)
+        waves = []
+        for w in range(len(todo[0]) + plan.chunks - 1):
+            at = [(c, w - c) for c in reversed(range(plan.chunks))]
+            waves.append([todo[c][k] for c, k in at if 0 <= k < len(todo[c])])
+        return waves
 
 
 def greet(devices):
@@ -499,14 +533,27 @@
 
 
 def build_modes(plan, place, weights, kernel):
-    flat = [weights[:, p].reshape(plan.own * C, C) for p in range(4)]
+    flat = jnp.concatenate([weights[:, p].reshape(-1, C) for p in range(4)], axis=1)
     for q in range(4):
-        rows = None
-        for p in range(4):
-            term = dot(flat[p], place[p, :, 256 * q : 256 * q + 256])
-            rows = term if rows is None else rows + term
+        rows = dot(flat, place[:, 256 * q : 256 * q + 256])
         kernel[:, C * q : C * q + C, :] = rows.astype(BF).reshape(plan.own, C, 256)
     kernel[:, W:, :] = kernel[:, 128:W, :]
+
+
+def build_lin(place, weight):
+    flat = jnp.concatenate([weight[p] for p in range(4)], axis=1)
+    rows = [dot(flat, place[:, 256 * q : 256 * q + 256]) for q in range(4)]
+    return jnp.concatenate(rows, axis=0).astype(BF)
+
+
+def half_tables():
+    rows = np.zeros((192, 384), np.float32)
+    rows[:128, :128] = 0.5 * np.eye(128)
+    rows[128:, 192:256] = 0.5 * np.eye(64)
+    rows[128:, 256:320] = 0.5 * np.eye(64)
+    line = np.zeros((128, C), np.float32)
+    line[MX :: 2 * MX] = 0.5
+    return low(rows), low(line), low(np.eye(C, dtype=np.float32))
 
 
 def plain_fields(plan):
@@ -527,10 +574,12 @@
 
 def forward_kernel(plan, x_big, x_small, spec_weight):
     big, small = plan.big, plan.small
-
-    def kernel(xb, xs, fb, fs, place, weights, sb_all, ss_all, out, kernel_out, spectrum,
-               part, sb, ss, table_sem, *refs):
+    last = plan.wide_steps
+
+    def kernel(x_hbm, xs, fb, fs, place, weights, sb_all, ss_all, out, kernel_out, spectrum,
+               part, sb, ss, table_sem, ring, ring_sem, *refs):
         i = pl.program_id(0)
+        stream = Stream(x_hbm, ring, ring_sem, 2 * plan.wide_per)
         ex = Exchange(plan, part, out, refs)
         loads = [
             pltpu.make_async_copy(sb_all.at[ex.me], sb, table_sem.at[0]),
@@ -547,27 +596,26 @@
             for load in loads:
                 load.wait()
 
-        def run(x, geo, first, second, count):
-            parts = []
-            for pair in range(count):
-                def get(start, width):
-                    v = x[2 * pair : 2 * pair + 2, :, :, start : start + width]
-                    return v.reshape(2 * W, width)
-
-                z = forward_pair(geo, get, first[...], second[...], 1.0 / geo.side)
-                parts.append(z.reshape(plan.chips, 2, plan.own, 2 * W))
-            parts += [jnp.zeros_like(parts[0])] * (plan.per - count)
-            z = jnp.concatenate(parts, axis=2) if plan.per > 1 else parts[0]
-            rows = pl.ds(pl.multiple_of(i * plan.block, 16), plan.block)
+        def run(x, geo, first, second, count, per):
+            def get(start, width):
+                v = x[: 2 * count, :, :, start : start + width]
+                return v.reshape(2 * count * W, width)
+
+            zs = forward_grids(geo, get, first[...], second[...], 1.0 / geo.side)
+            parts = [z.reshape(plan.chips, 2, plan.own, 2 * W) for z in zs]
+            parts += [jnp.zeros_like(parts[0])] * (per - count)
+            z = jnp.concatenate(parts, axis=2) if per > 1 else parts[0]
+            rows = pl.ds(pl.multiple_of(i * plan.wide_per * plan.own, 16), per * plan.own)
             part[:, :, rows, :] = z.astype(BF)
 
-        @pl.when(i < plan.steps)
-        def _():
-            run(xb, big, fb, sb, plan.per)
-
-        @pl.when(i == plan.steps)
-        def _():
-            run(xs, small, fs, ss, plan.nsmall // 2)
+        @pl.when(i < last)
+        def _():
+            run(stream.read(i, last), big, fb, sb, plan.wide_per, plan.wide_per)
+            stream.ahead(i, last)
+
+        @pl.when(i == last)
+        def _():
+            run(xs, small, fs, ss, plan.nsmall // 2, plan.per)
 
         def total(c):
             ex.finish_sum(c, 1.0)
@@ -580,22 +628,33 @@
             build_modes(plan, place, weights, ex.kernel)
             keep.start()
 
-        starts = [(c + 1) * plan.span - 1 for c in range(plan.chunks)]
-        schedule(plan, ex, i, total, starts, 2, [(starts[0], prepare)])
-
-        @pl.when(i == plan.steps)
+        waves = ex.waves(total)
+        items = []
+        for c in range(plan.chunks):
+            pairs = (c + 1) * plan.span * plan.per
+            end = min(-(-pairs // plan.wide_per) - 1, last)
+            items.append((end, lambda c=c: ex.begin(c)))
+            if c == plan.chunks - 1:
+                items.append((last, prepare))
+                items += [(last, task) for task in waves.pop(0)]
+            items.append((min(end + 1, last), lambda c=c: ex.add_sibling(c)))
+        items += [(last, task) for wave in waves for task in wave]
+        schedule(last, i, items)
+
+        @pl.when(i == last)
         def _():
             ex.drain()
             keep.wait()
 
     return pl.pallas_call(
         kernel,
-        grid=(plan.count,),
+        grid=(last + 1,),
         in_specs=[
-            *plain_fields(plan),
+            ANYWHERE,
+            plain_fields(plan)[1],
             fixed(big.first.shape),
             fixed(small.first.shape),
-            fixed((4, C, 1024)),
+            fixed((W, 1024)),
             fixed(spec_weight.shape),
             ANYWHERE,
             ANYWHERE,
@@ -611,6 +670,7 @@
             pltpu.VMEM(big.second.shape[1:], BF),
             pltpu.VMEM(small.second.shape[1:], BF),
             pltpu.SemaphoreType.DMA((3,)),
+            *Stream.scratch(min(4, last), 2 * plan.wide_per, big.cells),
             *Exchange.scratch(plan),
         ],
         compiler_params=params(collective_id=1, has_side_effects=True),
@@ -619,43 +679,58 @@
       big.second, small.second)
 
 
-def schedule(plan, ex, i, total, starts, gap, hooks):
-    last = plan.count - 1
-    at = {}
-    for c in range(plan.chunks):
-        for k, task in enumerate(ex.tasks(c, total)):
-            when = starts[c] + gap * k
-            at.setdefault(min(when, last), []).append((when, c, task))
-    for when, task in hooks:
-        at.setdefault(min(when, last), []).append((when, -1, task))
-    for step in sorted(at):
-        @pl.when(i == step)
-        def _(step=step):
-            for _, _, task in sorted(at[step], key=lambda v: v[:2]):
-                task()
-
-
-def cells_pass(plan, rank, x_big, x_small, g_big, g_small, modes, lin_t, bias):
+def schedule(last, i, items):
+    for step in range(last + 1):
+        now = [task for when, task in items if min(when, last) == step]
+        if now:
+            @pl.when(i == step)
+            def _(now=now):
+                for task in now:
+                    task()
+
+
+def cells_pass(plan, rank, x_big, x_small, g_big, g_small, modes, lin_weight,
+               lin_bias):
     k0 = math.sqrt(2.0 / math.pi)
     k1 = k0 * 0.044715
 
-    def body(r, xb, xs, gb, gs, m, fb, sb, vb, eb, fs, ss, vs, es, kt, bias_ref,
-             ob, os_, pb, ps, z, lin_acc, y_acc):
+    def low_of(value):
+        return jnp.asarray(value, BF)
+
+    per, steps = plan.wide_per, plan.wide_steps
+    last = steps - 1
+
+    def body(r, xb, xs, gb, gs, m, ms, fb, sb, vb, eb, fs, ss, vs, es,
+             place, rows_table, line, eye, lw, lb, ob, os_, pb, ps, z, lin_acc, y_acc,
+             kt, bias_ref):
         i = pl.program_id(0)
 
         @pl.when(i == 0)
         def _():
+            full = build_lin(place[...], lw)[:, :W]
+            kt[...] = dot(full, rows_table[...], ((0,), (0,))).astype(BF)
+            for q in range(4):
+                bias_ref[C * q : C * q + C, :] = dot(
+                    eye[...], line[...] * lb[q : q + 1, :], ((1,), (1,))
+                ).astype(BF)
             lin_acc[...] = jnp.zeros_like(lin_acc)
             y_acc[...] = jnp.zeros_like(y_acc)
 
-        def run(x, g, o, d, geo, first, second, inverse, spread, count):
+        def run(x, g, o, d, m, z, geo, first, second, inverse, spread, count):
             wide_cells = 2 * geo.side
             lane = lax.broadcasted_iota(jnp.int32, (W, 128), 1)
-
-            def main(at, q_all, p):
+            held, groups = {}, {}
+
+            def rows_back(pair):
+                qs = inverse_pair(geo, load_modes(plan, m, pair), inverse[...], 0.5 / MX)
+                line = jnp.concatenate([bias_ref[...]] * (geo.qlanes // 128), axis=1)
+                for s in range(2):
+                    held[2 * pair + s] = qs[s] + line
+
+            def main(at, p):
                 lo = p * wide_cells
                 cells = slice(lo, lo + wide_cells)
-                q = q_all[:, 128 * (p // 2) : 128 * (p // 2) + 128]
+                q = held[at][:, 128 * (p // 2) : 128 * (p // 2) + 128]
                 xv = x[at, :, :, cells].reshape(W, wide_cells)
                 if p % 2 == 0:
                     tail = jnp.where(lane < 64, q, kt[:, 128:256])
@@ -665,46 +740,59 @@
                     rhs = [xv[:128], xv[128:], spread[...]]
                 lhs = jnp.concatenate([kt[:, :128], tail], axis=1)
                 b = dot(lhs, jnp.concatenate(rhs, axis=0))
-                s = b * b
-                t = jnp.tanh(b * (2.0 * k0 + 8.0 * k1 * s))
-                e = 1.0 + t
-                o[at, :, :, cells] = (xv + (b * e).astype(BF)).reshape(4, C, wide_cells)
-                slope = e * (0.5 + b * (k0 + 12.0 * k1 * s) * (1.0 - t))
+                b = b.astype(BF)
+                b2 = b * b
+                e = low_of(1.0) + jnp.tanh(b * (low_of(2.0 * k0) + low_of(8.0 * k1) * b2))
+                o[at, :, :, cells] = (xv + b * e).reshape(4, C, wide_cells)
+                rise = b * (low_of(k0) + low_of(12.0 * k1) * b2)
+                slope = e * (low_of(0.5) + rise * (low_of(2.0) - e))
                 gv = g[at, :, :, cells].reshape(W, wide_cells)
-                d[at, :, :, cells] = (gv * slope.astype(BF)).reshape(4, C, wide_cells)
-
-            def weight_grad(at):
-                xa = x[at, :, :, :].reshape(W, geo.cells)
-                pa = d[at, :, :, :].reshape(W, geo.cells)
+                d[at, :, :, cells] = (gv * slope).reshape(4, C, wide_cells)
+
+            def weight_grad(at, part):
+                span = geo.cells // 2
+                xa = x[at, :, :, part * span : part * span + span].reshape(W, span)
+                pa = d[at, :, :, part * span : part * span + span].reshape(W, span)
                 lin_acc[...] += dot(xa, pa, ((1,), (1,)))
 
             def keep(y):
                 y_acc[...] += y
 
-            for pair in range(count):
-                qs = inverse_pair(geo, load_modes(plan, m, pair), inverse[...], 0.5 / MX)
-                for s in range(2):
-                    q_all = qs[s] + jnp.concatenate([bias_ref[...]] * (geo.qlanes // 128), axis=1)
-                    for p in range(geo.npairs):
-                        main(2 * pair + s, q_all, p)
-                    weight_grad(2 * pair + s)
-
-                def get(start, width):
-                    v = d[2 * pair : 2 * pair + 2, :, :, start : start + width]
-                    return v.reshape(2 * W, width)
-
-                out = forward_pair(geo, get, first[...], second[...], 1.0, keep)
-                store_modes(plan, z, pair, out)
-
-        @pl.when(i < plan.steps)
-        def _():
-            run(xb, gb, ob, pb, plan.big, fb, sb, vb, eb, plan.per)
-
-        @pl.when(i == plan.steps)
-        def _():
-            if plan.nsmall // 2 < plan.per:
+            def columns(pair, k):
+                width = geo.group * geo.side
+                v = d[2 * pair : 2 * pair + 2, :, :, k * width : k * width + width]
+                cols = forward_group(v.reshape(2 * W, width), first[...], 1.0, keep)
+                groups.setdefault(pair, []).append(cols)
+
+            def rows_out(pair):
+                store_modes(plan, z, pair, forward_rows(groups[pair], second[...]))
+
+            side = []
+            rows_back(0)
+            for at in range(2 * count):
+                pair = at // 2
+                if at % 2 == 0 and pair + 1 < count:
+                    side.append(lambda pair=pair: rows_back(pair + 1))
+                for p in range(geo.npairs):
+                    main(at, p)
+                    if side:
+                        side.pop(0)()
+                side += [lambda at=at, k=k: weight_grad(at, k) for k in range(2)]
+                if at % 2 == 1:
+                    side += [lambda pair=pair, k=k: columns(pair, k) for k in range(geo.ngroups)]
+                    side.append(lambda pair=pair: rows_out(pair))
+            for task in side:
+                task()
+
+        @pl.when(i < steps)
+        def _():
+            run(xb, gb, ob, pb, m, z, plan.big, fb, sb, vb, eb, per)
+
+        @pl.when(i == steps)
+        def _():
+            if plan.nsmall // 2 < per:
                 z[...] = jnp.zeros_like(z)
-            run(xs, gs, os_, ps, plan.small, fs, ss, vs, es, plan.nsmall // 2)
+            run(xs, gs, os_, ps, ms, z, plan.small, fs, ss, vs, es, plan.nsmall // 2)
 
     big, small = plan.big, plan.small
     tables = []
@@ -717,59 +805,73 @@
             device_spec(geo.inverse.shape[1:]),
             const_spec(geo.pair_spread.shape),
         ]
+    extra = [expand_tables(), *half_tables(), lin_weight, lin_bias]
+    small_field = field_specs(plan)[1]
+    big_field = pl.BlockSpec((2 * per, 4, C, big.cells), lambda i, r: (wide(i, last), 0, 0, 0))
+    rows = per * plan.own
     return pl.pallas_call(
         body,
         grid_spec=pltpu.PrefetchScalarGridSpec(
             num_scalar_prefetch=1,
-            grid=(plan.count,),
+            grid=(steps + 1,),
             in_specs=[
-                *field_specs(plan),
-                *field_specs(plan),
-                mode_spec(plan),
+                big_field,
+                small_field,
+                big_field,
+                small_field,
+                pl.BlockSpec((plan.n, rows, 2 * W), lambda i, r: (0, wide(i, last), 0)),
+                pl.BlockSpec((plan.n, plan.block, 2 * W), lambda i, r: (0, plan.steps, 0)),
                 *specs,
-                const_spec(lin_t.shape),
-                const_spec(bias.shape),
+                *[const_spec(v.shape) for v in extra],
             ],
             out_specs=[
-                *field_specs(plan),
-                *field_specs(plan),
-                mode_spec(plan),
+                big_field,
+                small_field,
+                big_field,
+                small_field,
+                pl.BlockSpec((plan.n, rows, 2 * W), lambda i, r: (0, i, 0)),
                 const_spec((W, W)),
-                const_spec((W, 256)),
+                const_spec((W, 128)),
             ],
+            scratch_shapes=[pltpu.VMEM((W, 2 * W), BF), pltpu.VMEM((W, 128), BF)],
         ),
         out_shape=[
             jax.ShapeDtypeStruct(x_big.shape, BF),
             jax.ShapeDtypeStruct(x_small.shape, BF),
             jax.ShapeDtypeStruct(x_big.shape, BF),
             jax.ShapeDtypeStruct(x_small.shape, BF),
-            jax.ShapeDtypeStruct((plan.n, plan.total, 2 * W), BF),
+            jax.ShapeDtypeStruct((plan.n, (steps + 1) * rows, 2 * W), BF),
             jax.ShapeDtypeStruct((W, W), F32),
-            jax.ShapeDtypeStruct((W, 256), F32),
+            jax.ShapeDtypeStruct((W, 128), F32),
         ],
         compiler_params=params(),
         name="cells",
-    )(rank, x_big, x_small, g_big, g_small, modes, *tables, lin_t, bias)
-
-
-def backward_kernel(plan, part, p_big, p_small, g_big, g_small, kernel_all, spectrum, lin,
-                    lin_grad, columns):
+    )(rank, x_big, x_small, g_big, g_small, modes, modes, *tables, *extra)
+
+
+def backward_kernel(plan, part, p_big, p_small, g_big, g_small, kernel_all, spectrum,
+                    lin_weight, lin_grad, columns):
     big, small = plan.big, plan.small
     stages = plan.n.bit_length() - 1 + plan.nz.bit_length() - 1
     rows_bits = plan.n.bit_length() - 1
     pick_all, move_all, move_lin = fold_tables()
-    zero_lanes = np.zeros((8, 256), np.float32)
-    zero_lanes[0, : 128 : MX] = 1.0
-
-    def kernel(pb, ps, gb, gs, kk, spec, lin_in, col_in, pick, move, shift, line, part_in, kernel_in,
+    zero_lanes = np.zeros((8, 128), np.float32)
+    zero_lanes[0, ::MX] = 1.0
+
+    def kernel(pb, ps, gb, gs, place, lw, spec, lin_in, col_in, pick, move, shift, line, part_in, kernel_in,
                db, ds, out, weight_out, lin_out,
-               part, sa, mb, dacc, send_z, recv_z, lin_buf, lin_recv,
-               in_sem, zs, zr, ls, lr, *refs):
+               part, kk, sa, mb, dacc, send_z, recv_z, lin_buf, lin_recv,
+               in_sem, zs, zr, ls, lr, p_ring, p_sem, g_ring, g_sem, d_ring, d_sem, *refs):
         i = pl.program_id(0)
-        ex = Exchange(plan, part, out, refs)
+        p_stream = Stream(pb, p_ring, p_sem, 2 * plan.per)
+        g_stream = Stream(gb, g_ring, g_sem, 2 * plan.per)
+        d_stream = Stream(db, d_ring, d_sem, 2 * plan.per)
+        ex = Exchange(plan, part, out, refs, part_in)
         here = lax.axis_index("samples")
         loads = [
-            pltpu.make_async_copy(part_in, part, in_sem.at[0]),
+            pltpu.make_async_copy(
+                part_in.at[:, :, pl.ds(0, plan.total), :], part, in_sem.at[0]
+            ),
             pltpu.make_async_copy(kernel_in, ex.kernel, in_sem.at[1]),
         ]
 
@@ -795,7 +897,8 @@
                 load.start()
             greet([{"rows": d} for d in ex.partners()]
                   + [{"samples": z_peer(d)} for d in range(1, plan.nz)])
-            ex.clear()
+            for c in range(plan.chunks):
+                ex.begin(c)
             folded = None
             for q in range(4):
                 term = lax.dot_general(
@@ -809,12 +912,16 @@
                 precision=lax.Precision.HIGHEST, preferred_element_type=F32,
             )
             lin_step(0).start()
+            kk[...] = build_lin(place[...], lw)[:, :W]
+            loads[0].wait()
+            for c in range(plan.chunks):
+                ex.add_sibling(c)
+            ex.clear()
             sa[...] = jnp.zeros_like(sa)
             mb[...] = jnp.zeros_like(mb)
             dacc[...] = jnp.zeros_like(dacc)
             send_z[...] = jnp.zeros_like(send_z)
-            for load in loads:
-                load.wait()
+            loads[1].wait()
 
         def run(p, g, d, geo, count):
             for at in range(2 * count):
@@ -824,15 +931,16 @@
 
         @pl.when(i < plan.steps)
         def _():
-            run(pb, gb, db, big, plan.per)
+            p = p_stream.read(i, plan.steps)
+            g = g_stream.read(i, plan.steps)
+            run(p, g, d_stream.reserve(i), big, plan.per)
+            d_stream.copy(i, True).start()
+            p_stream.ahead(i, plan.steps)
+            g_stream.ahead(i, plan.steps)
 
         @pl.when(i == plan.steps)
         def _():
             run(ps, gs, ds, small, plan.nsmall // 2)
-
-        def total(c):
-            ex.finish_sum(c, 1.0 / MX)
-            ex.mix(c, ((1,), (1,)))
 
         def weight_grad(c):
             crow = plan.crow
@@ -898,20 +1006,22 @@
 
         def chunk_total(c):
             ex.finish_sum(c, 1.0 / MX)
+            ex.mix(c, ((1,), (1,)))
             weight_grad(c)
-            ex.mix(c, ((1,), (1,)))
             if c == plan.chunks - 1:
                 send_weights()
 
         last = plan.count - 1
-        hooks = [(2 * k + 1, lambda k=k: lin_next(k)) for k in range(stages)]
-        hooks.append((4 * plan.count, sum_weights))
-        starts = [c for c in range(plan.chunks)]
-        schedule(plan, ex, i, chunk_total, starts, 2, hooks)
+        items = [(2 * k + 1, lambda k=k: lin_next(k)) for k in range(stages)]
+        for w, wave in enumerate(ex.waves(chunk_total)):
+            items += [(2 + 2 * w, task) for task in wave]
+        items.append((last, sum_weights))
+        schedule(last, i, items)
 
         @pl.when(i == last)
         def _():
             ex.drain()
+            d_stream.flush(plan.steps)
             for d in range(1, plan.nz):
                 to_z(d).wait_send()
             for k in range(stages):
@@ -923,12 +1033,15 @@
         kernel,
         grid=(plan.count,),
         in_specs=[
-            *plain_fields(plan),
-            *plain_fields(plan),
-            fixed((W, W)),
+            ANYWHERE,
+            plain_fields(plan)[1],
+            ANYWHERE,
+            plain_fields(plan)[1],
+            fixed((W, 1024)),
+            fixed((4, C, C)),
             fixed((plan.total, 2 * W)),
             fixed((W, W)),
-            fixed((W, 256)),
+            fixed((W, 128)),
             fixed(pick_all.shape),
             fixed(move_all.shape),
             fixed(move_lin.shape),
@@ -937,7 +1050,8 @@
             ANYWHERE,
         ],
         out_specs=[
-            *plain_fields(plan),
+            ANYWHERE,
+            plain_fields(plan)[1],
             ANYWHERE,
             fixed((plan.zrows, 2 * W)),
             fixed((C + 8, W)),
@@ -951,6 +1065,7 @@
         ],
         scratch_shapes=[
             pltpu.VMEM((plan.chips, 2, plan.total, 2 * W), BF),
+            pltpu.VMEM((W, W), BF),
             pltpu.VMEM((4, 2, acc, 128), F32),
             pltpu.VMEM((8, 2, acc, 128), F32),
             pltpu.VMEM((plan.own, C, 256), F32),
@@ -963,92 +1078,146 @@
             dma((plan.nz,)),
             dma((stages,)),
             dma((stages,)),
+            *Stream.scratch(min(4, plan.steps), 2 * plan.per, big.cells),
+            *Stream.scratch(min(4, plan.steps), 2 * plan.per, big.cells),
+            *Stream.scratch(min(3, plan.steps), 2 * plan.per, big.cells),
             *Exchange.scratch(plan),
         ],
         compiler_params=params(collective_id=2, has_side_effects=True),
         name="mode_backward",
-    )(p_big, p_small, g_big, g_small, lin, spectrum, lin_grad, columns,
+    )(p_big, p_small, g_big, g_small, expand_tables(), lin_weight, spectrum, lin_grad, columns,
       pick_all, move_all, move_lin, zero_lanes, part, kernel_all)
 
 
-def input_grads(plan, rank, part_big, part_small, modes):
-    def body(r, pb, ps, m, vb, eb, vs, es, db, ds):
+def input_grads(plan, rank, part_big, part_small, modes, lin_sum):
+    big, small = plan.big, plan.small
+    per, steps = plan.wide_per, plan.wide_steps
+    last = steps - 1
+
+    split = np.zeros((W, 4, 128), np.float32)
+    for p in range(4):
+        split[p * C : p * C + C, p, :C] = np.eye(C)
+    split = split.reshape(W, 512)
+
+    def body(r, pb, ps, mb, ms, vb, eb, vs, es, lin, cut, db, ds, lin_out, bias_out):
         i = pl.program_id(0)
 
-        def run(part, d, geo, inverse, spread, count):
+        @pl.when(i == 0)
+        def _():
+            v = lax.dot_general(
+                lin[...], cut[...], (((1,), (0,)), ((), ())),
+                precision=lax.Precision.HIGHEST, preferred_element_type=F32,
+            )
+            for p in range(4):
+                lin_out[p] = v[:C, 128 * p : 128 * p + C]
+                bias_out[p : p + 1, :] = v[C : C + 1, 128 * p : 128 * p + C]
+
+        def run(part, m, d, geo, inverse, spread, count):
             span = spread.shape[1]
+            qs = []
             for pair in range(count):
-                qs = inverse_pair(geo, load_modes(plan, m, pair), inverse[...], 1.0)
-                q = jnp.concatenate(qs, axis=0) * jnp.asarray(1.0 / geo.side, BF)
-                for j in range(geo.cells // span):
-                    v = dot(q[:, 128 * j : 128 * j + 128], spread[...])
-                    at = (slice(2 * pair, 2 * pair + 2), slice(None), slice(None),
-                          slice(j * span, (j + 1) * span))
-                    d[at] = part[at].astype(F32) + v.reshape(2, 4, C, span)
-
-        @pl.when(i < plan.steps)
-        def _():
-            run(pb, db, plan.big, vb, eb, plan.per)
-
-        @pl.when(i == plan.steps)
-        def _():
-            run(ps, ds, plan.small, vs, es, plan.nsmall // 2)
+                qs += inverse_pair(geo, load_modes(plan, m, pair), inverse[...], 1.0)
+            q = jnp.concatenate(qs, axis=0) * jnp.asarray(1.0 / geo.side, BF)
+            for j in range(geo.cells // span):
+                v = dot(q[:, 128 * j : 128 * j + 128], spread[...])
+                at = (slice(0, 2 * count), slice(None), slice(None),
+                      slice(j * span, (j + 1) * span))
+                d[at] = part[at].astype(F32) + v.reshape(2 * count, 4, C, span)
+
+        @pl.when(i < steps)
+        def _():
+            run(pb, mb, db, big, vb, eb, per)
+
+        @pl.when(i == steps)
+        def _():
+            run(ps, ms, ds, small, vs, es, plan.nsmall // 2)
 
     tables = []
     specs = []
-    for geo in (plan.big, plan.small):
+    for geo in (big, small):
         tables += [geo.inverse, geo.spread]
         specs += [device_spec(geo.inverse.shape[1:]), const_spec(geo.spread.shape)]
+    small_field = field_specs(plan)[1]
+    big_field = pl.BlockSpec((2 * per, 4, C, big.cells), lambda i, r: (wide(i, last), 0, 0, 0))
     return pl.pallas_call(
         body,
         grid_spec=pltpu.PrefetchScalarGridSpec(
             num_scalar_prefetch=1,
-            grid=(plan.steps + 1,),
-            in_specs=[*field_specs(plan), mode_spec(plan), *specs],
-            out_specs=[*field_specs(plan)],
+            grid=(steps + 1,),
+            in_specs=[
+                big_field,
+                small_field,
+                pl.BlockSpec((plan.n, per * plan.own, 2 * W), lambda i, r: (0, wide(i, last), 0)),
+                pl.BlockSpec((plan.n, plan.block, 2 * W), lambda i, r: (0, plan.steps, 0)),
+                *specs,
+                const_spec(lin_sum.shape),
+                const_spec(split.shape),
+            ],
+            out_specs=[big_field, small_field, const_spec((4, C, C)), const_spec((4, C))],
         ),
         out_shape=[
             jax.ShapeDtypeStruct(part_big.shape, F32),
             jax.ShapeDtypeStruct(part_small.shape, F32),
+            jax.ShapeDtypeStruct((4, C, C), F32),
+            jax.ShapeDtypeStruct((4, C), F32),
         ],
         compiler_params=params(),
         name="input_grads",
-    )(rank, part_big, part_small, modes, *tables)
+    )(rank, part_big, part_small, modes, modes, *tables, lin_sum, split)
+
+
+def collect(plan, here, pieces):
+    pick = np.zeros((2, 2 * W, 4, 128), np.float32)
+    for odd in range(2):
+        for lane in range(W):
+            at = lane + 128 * odd if lane < 128 else 128 + 64 * odd + lane
+            pick[odd, at, lane // C, lane % C] = 1.0
+    pick = low(pick.reshape(2, 2 * W, 512))
+
+    def body(z, pick_ref, *refs):
+        pieces, out, rows = refs[: plan.nz], refs[plan.nz], refs[plan.nz + 1]
+        for d, piece in enumerate(pieces):
+            at = lax.rem(z[0] + plan.nz - d, plan.nz) * plan.zrows
+            rows[pl.ds(pl.multiple_of(at, 16), plan.zrows), :] = piece[...]
+        for odd in range(2):
+            v = dot(rows[: plan.wrows, :], pick_ref[odd])
+            for j in range(plan.own // 2):
+                for p in range(4):
+                    out[2 * j + odd, p] = v[j * C : j * C + C, 128 * p : 128 * p + C]
+
+    vmem = pl.BlockSpec(memory_space=pltpu.VMEM)
+    return pl.pallas_call(
+        body,
+        in_specs=[pl.BlockSpec(memory_space=pltpu.SMEM)] + [vmem] * (1 + plan.nz),
+        out_specs=vmem,
+        out_shape=jax.ShapeDtypeStruct((plan.own, 4, C, C), F32),
+        scratch_shapes=[pltpu.VMEM((plan.nz * plan.zrows, 2 * W), BF)],
+        compiler_params=params(),
+        name="collect",
+    )(here, pick, *pieces)
 
 
 def on_device(plan, x_big, x_small, spec_weight, lin_weight, lin_bias, grad_big, grad_small):
     rank = lax.axis_index("rows").reshape(1)
-    lin = build_kernel(lin_weight)
-    half = lin.T * jnp.asarray(0.5, BF)
-    zero = jnp.zeros((W, 64), BF)
-    half = jnp.concatenate([half[:, :128], zero, half[:, 128:], half[:, 128:], zero], axis=1)
-    bias_lane = np.arange(128) % (2 * MX) == MX
-    bias = lin_bias.reshape(W, 1) * jnp.asarray(0.5 * bias_lane, BF)
-
+    here = lax.axis_index("samples").reshape(1)
     whole = (plan.n, plan.total, 2 * W)
     modes, kernel, spectrum = forward_kernel(plan, x_big, x_small, spec_weight)
     out_big, out_small, pre_big, pre_small, part, lin_grad, columns = cells_pass(
-        plan, rank, x_big, x_small, grad_big, grad_small, modes.reshape(whole), half, bias
+        plan, rank, x_big, x_small, grad_big, grad_small, modes.reshape(whole), lin_weight,
+        lin_bias,
     )
     part_big, part_small, modes, weight_part, lin_sum = backward_kernel(
-        plan, part.reshape(plan.chips, 2, plan.total, 2 * W), pre_big, pre_small,
-        grad_big, grad_small, kernel, spectrum, lin, lin_grad, columns,
+        plan, part.reshape(plan.chips, 2, -1, 2 * W), pre_big, pre_small,
+        grad_big, grad_small, kernel, spectrum, lin_weight, lin_grad, columns,
     )
-    here = lax.axis_index("samples")
     pieces = [weight_part]
     for d in range(1, plan.nz):
         pairs = [(z, (z + d) % plan.nz) for z in range(plan.nz)]
         pieces.append(lax.ppermute(weight_part, "samples", pairs))
-    dx_big, dx_small = input_grads(plan, rank, part_big, part_small, modes.reshape(whole))
-    order = lax.rem(here - jnp.arange(plan.nz) + plan.nz, plan.nz)
-    rows = jnp.stack(pieces)[order].reshape(plan.nz * plan.zrows, 2 * W)
-    rows = rows[: plan.wrows].reshape(plan.own // 2, C, 2 * W)
-    even = jnp.concatenate([rows[..., :128], rows[..., 256:320]], axis=-1)
-    odd = jnp.concatenate([rows[..., 128:256], rows[..., 320:]], axis=-1)
-    spec_grad = jnp.stack([even, odd], axis=1).reshape(plan.own, C, 4, C)
-    spec_grad = spec_grad.transpose(0, 2, 1, 3).astype(F32)
-    lin_weight_grad = lin_sum[:C].reshape(C, 4, C).transpose(1, 0, 2)
-    lin_bias_grad = lin_sum[C].reshape(4, C)
+    dx_big, dx_small, lin_weight_grad, lin_bias_grad = input_grads(
+        plan, rank, part_big, part_small, modes.reshape(whole), lin_sum
+    )
+    spec_grad = collect(plan, here, pieces)
     return out_big, out_small, dx_big, dx_small, spec_grad, lin_weight_grad, lin_bias_grad
 
 

time: 222 us -> 178 us (0.80)
  Pallas kernels: 198 us -> 171 us
  local copies, waits for them, and re-layouts: 11.1 us -> 0.71 us
  other arithmetic: 4.48 us -> 0 us
    pallas_call x2 -> x3, Pallas kernels: 113 us -> 99.6 us  [the longest x1 52.7 us: backward_kernel(): pl.pallas_call(kernel, grid=(plan.count,), in_specs=[ANYWHERE, plain_fiel...]
    pallas_call x1, Pallas kernels: 55.2 us -> 44.6 us  [cells_pass(): pl.pallas_call(body, grid_spec=pltpu.PrefetchScalarGridSpec(num_scalar_pr...]
    convert_element_type x1 -> x0, local copies, waits for them, and re-layouts: 3.04 us -> none  [on_device(): spec_grad = spec_grad.transpose(0, 2, 1, 3).astype(F32)]
    pallas_call x1, Pallas kernels: 29.7 us -> 26.9 us  [input_grads(): pl.pallas_call(body, grid_spec=pltpu.PrefetchScalarGridSpec(num_scalar_pr...]
  transfers between devices with their start and end apart: 3 -> 3, of which waited for: 0 -> 0; matrix products, arithmetic and copies ran while one was open for 1% -> 0% of each run, Pallas kernels for 13% -> 15%
where the time goes in v3:
time: 178 us
  Pallas kernels  171 us (96%)
  starting transfers between devices  5.32 us (3%)
    pallas_call x1, Pallas kernels, backward_kernel(): pl.pallas_call(kernel, grid=(plan.count,), in_specs=[ANYWHERE, plain_fiel...  52.7 us
    pallas_call x1, Pallas kernels, cells_pass(): pl.pallas_call(body, grid_spec=pltpu.PrefetchScalarGridSpec(num_scalar_pr...  44.6 us
    pallas_call x1, Pallas kernels, forward_kernel(): pl.pallas_call(kernel, grid=(last + 1,), in_specs=[ANYWHERE, plain_fields...  42.9 us
    pallas_call x1, Pallas kernels, input_grads(): pl.pallas_call(body, grid_spec=pltpu.PrefetchScalarGridSpec(num_scalar_pr...  26.9 us
    ppermute x3, starting transfers between devices, on_device(): pieces.append(lax.ppermute(weight_part, 'samples', pairs))  5.32 us
    pallas_call x1, Pallas kernels, collect(): pl.pallas_call(body, in_specs=[pl.BlockSpec(memory_space=pltpu.SMEM)] + [...  3.98 us
  transfers between devices with their start and end apart: 3, of which 0 were waited for; matrix products, arithmetic and copies ran while one was open for 0% of the time, Pallas kernels for 15%

profile of v3, /device:TPU:0, one launch (start us, length us, event | category | flops | bytes accessed | tf_op | source)
XLA Modules:
  0.0 178.0 jit_solution(15265996677692171224)
XLA Ops:
  0.6 42.9 %mode_forward.1 = (bf16[4,2,480,384]{3,2,1,0:T(8,128)(2,1)}, bf16[32,256,256]{2,1,0:T(8,128)(2,1)}, bf16[480,384]{1,0:T(8,128)(2,1)}) custom-call(bf16[28,4,48,2048]{3,2,1,0:T(8,128)(2,1)} %xb.1, bf16[2,4,48,512]{3,2,1,0:T(8,128)(2,1)} %xs.3, bf16[1024,256]{1,0:T(8,128)(2,1)} %constant.48.clone.fb, bf16[512,256]{1,0:T(8,128)(2,1)} %constant.49.clone.fs, ...), custom_call_target="tpu_custom_call" | custom-call | tf_op jit(solution)/shard_map/mode_forward/pallas_call | solution.py:649
  43.6 44.6 %cells.1 = (bf16[28,4,48,2048]{3,2,1,0:T(8,128)(2,1)}, bf16[2,4,48,512]{3,2,1,0:T(8,128)(2,1)}, bf16[28,4,48,2048]{3,2,1,0:T(8,128)(2,1)}, bf16[2,4,48,512]{3,2,...) custom-call(s32[1]{0:T(128)} %bitcast.r, bf16[28,4,48,2048]{3,2,1,0:T(8,128)(2,1)} %xb.1, ...), custom_call_target="tpu_custom_call" | custom-call | tf_op jit(solution)/shard_map/cells/pallas_call | solution.py:812
  88.2 52.7 %mode_backward.1 = (bf16[28,4,48,2048]{3,2,1,0:T(8,128)(2,1)}, bf16[2,4,48,512]{3,2,1,0:T(8,128)(2,1)}, bf16[4,2,480,384]{3,2,1,0:T(8,128)(2,1)}, bf16[192,384]{1,0:T(8,128)(2,1)}, f32[56,192]{1,0:T(8,128)}) custom-call(bf16[28,4,48,2048]{3,2,1,0:T(8,128)(2,1)} %get-tuple-element.29.pb, bf16[2,4,48,512]{3,2,1,0:T(8,128)(2,1)} %get-tuple-element.30.ps, ...), custom_call_target="tpu_custom_call" | custom-call | tf_op jit(solution)/shard_map/mode_backward/pallas_call | solution.py:1032
  140.9 2.9 %collective-permute-start = (bf16[192,384]{1,0:T(8,128)(2,1)}, bf16[192,384]{1,0:T(8,128)(2,1)S(1)}, u32[]{:S(2)}, u32[]{:S(2)}) collective-permute-start(bf16[192,384]{1,0:T(8,128)(2,1)} %get-tuple-element.42.refs_0_), channel_id=1, source_target_pairs={{0,8},{8,16},{16,24},{24,0},{1,9},{9,17},{17,25},{25,1},{2,10},{10... | collective-permute-start | bytes 442376 | tf_op jit(solution)/shard_map/ppermute | solution.py:1216
  143.8 2.4 %collective-permute-start.1 = (bf16[192,384]{1,0:T(8,128)(2,1)}, bf16[192,384]{1,0:T(8,128)(2,1)S(1)}, u32[]{:S(2)}, u32[]{:S(2)}) collective-permute-start(bf16[192,384]{1,0:T(8,128)(2,1)} %get-tuple-element.42.refs_0_), channel_id=1, source_target_pairs={{0,16},{8,24},{16,0},{24,8},{1,17},{9,25},{17,1},{25,9},{2,18},{10... | collective-permute-start | bytes 442376 | tf_op jit(solution)/shard_map/ppermute | solution.py:1216
  146.2 0.1 collective-permute-start.2
  146.3 26.9 %input_grads.1 = (f32[28,4,48,2048]{3,2,1,0:T(8,128)}, f32[2,4,48,512]{3,2,1,0:T(8,128)}, f32[4,48,48]{2,1,0:T(8,128)}, f32[4,48]{1,0:T(4,128)}) custom-call(s32[1]{0:T(128)} %bitcast.r, bf16[28,4,48,2048]{3,2,1,0:T(8,128)(2,1)} %get-tuple-element.36.pb, bf16[2,4,48,512]{3,2,1,0:T(8,128)(2,1)} %get-tuple-element.37.ps, bf16[8,480,384]{2,1,0:T(8,128)(2,1)} %bitcast.5, ...), custom_call_target="tpu_custom_call" | custom-call | tf_op jit(solution)/shard_map/input_grads/pallas_call | solution.py:1142
  173.2 0.0 collective-permute-done.refs_1_
  173.2 0.0 copy-start
  173.2 0.0 collective-permute-done.1.refs_2_
  173.2 0.0 copy-start.1
  173.2 0.0 collective-permute-done.2.refs_3_
  173.3 0.0 copy-start.2
  173.3 0.6 copy-done
  173.9 0.1 copy-done.1
  173.9 0.0 copy-done.2
  174.0 4.0 %collect.1 = f32[32,4,48,48]{3,2,1,0:T(8,128)} custom-call(s32[1]{0:T(128)} %bitcast.4.z, bf16[2,384,512]{2,1,0:T(8,128)(2,1)} %constant.67.clone.pick_ref, bf16[192,384]{1,0:T(8,128)(2,1)} %get-tuple-element.42.refs_0_, bf16[192,384]{1,0:T(8,128)(2,1)} %copy-done, bf16[192,384]{1,0:T(8,128)(2,1)} %copy-done.1, bf16[192,384]{1,0:T(8,128)(2,1)} %copy-done.2), custom_call_target="tpu_custom_call" | custom-call | tf_op jit(solution)/shard_map/collect/pallas_call | solution.py:1189
Async XLA Ops:
  140.9 32.3 %collective-permute-start = (bf16[192,384]{1,0:T(8,128)(2,1)}, bf16[192,384]{1,0:T(8,128)(2,1)S(1)}, u32[]{:S(2)}, u32[]{:S(2)}) collective-permute-start(bf16[192,384]{1,0:T(8,128)(2,1)} %get-tuple-element.42.refs_0_), channel_id=1, source_target_pairs={{0,8},{8,16},{16,24},{24,0},{1,9},{9,17},{17,25},{25,1},{2,10},{10... | collective-permute-start | bytes 442376 | tf_op jit(solution)/shard_map/ppermute | solution.py:1216
  143.8 29.4 %collective-permute-start.1 = (bf16[192,384]{1,0:T(8,128)(2,1)}, bf16[192,384]{1,0:T(8,128)(2,1)S(1)}, u32[]{:S(2)}, u32[]{:S(2)}) collective-permute-start(bf16[192,384]{1,0:T(8,128)(2,1)} %get-tuple-element.42.refs_0_), channel_id=1, source_target_pairs={{0,16},{8,24},{16,0},{24,8},{1,17},{9,25},{17,1},{25,9},{2,18},{10... | collective-permute-start | bytes 442376 | tf_op jit(solution)/shard_map/ppermute | solution.py:1216
  146.2 27.1 %collective-permute-start.2 = (bf16[192,384]{1,0:T(8,128)(2,1)}, bf16[192,384]{1,0:T(8,128)(2,1)S(1)}, u32[]{:S(2)}, u32[]{:S(2)}) collective-permute-start(bf16[192,384]{1,0:T(8,128)(2,1)} %get-tuple-element.42.refs_0_), channel_id=1, source_target_pairs={{0,24},{8,0},{16,8},{24,16},{1,25},{9,1},{17,9},{25,17},{2,26},{10... | collective-permute-start | bytes 442376 | tf_op jit(solution)/shard_map/ppermute | solution.py:1216
  173.2 0.6 copy-start
  173.2 0.7 copy-start.1
  173.3 0.7 copy-start.2

commit v4 on v3

--- a/solution.py
+++ b/solution.py
@@ -163,6 +163,20 @@
     return low(place.reshape(W, 1024))
 
 
+class Layout:
+    def __init__(self, chunks, pairs, modes, by_mode):
+        self.chunks, self.pairs, self.modes, self.by_mode = chunks, pairs, modes, by_mode
+        self.crow = pairs * modes
+        first = -(-self.crow // 32) * 16
+        self.halves = (first, self.crow - first)
+        self.slots = -(-pairs // 8) * 8
+        self.acc_rows = self.slots * modes
+        self.total = chunks * self.crow
+
+    def first_mode(self, c):
+        return c * self.modes if self.by_mode else 0
+
+
 class Plan:
     def __init__(self, mesh, nbig, nsmall):
         self.n = mesh.shape["rows"]
@@ -179,18 +193,19 @@
         self.wide_steps = nbig // (2 * self.wide_per)
         self.block = self.per * self.own
         self.total = self.count * self.block
-        self.chunks = next(c for c in (3, 2, 1) if self.count % c == 0)
-        self.span = self.count // self.chunks
-        self.crow = self.span * self.block
-        self.half = self.crow // 2
-        self.slots = -(-(self.span * self.per) // 8) * 8
-        self.acc_rows = self.slots * self.own
+        pairs = self.count * self.per
+        parts = next(c for c in (3, 2, 1) if self.count % c == 0)
+        self.by_pairs = Layout(parts, pairs // parts, self.own, False)
+        parts = max(1, self.own // 16)
+        self.by_modes = Layout(parts, pairs, self.own // parts, True)
         self.chips = self.n // 2
         bits = list(range(1, self.n.bit_length() - 1))
         self.orders = (bits, bits[::-1])
         self.levels = len(bits)
-        self.wrows = self.own // 2 * C
-        self.zrows = -(-self.wrows // (16 * self.nz)) * 16
+        self.wrows = self.by_modes.modes // 2 * C
+        self.pieces = 2
+        self.zrows = self.wrows // self.pieces
+        assert self.nz % 2 == 0 and self.zrows % 16 == 0
 
     def mask(self, h, idx):
         m = 0
@@ -229,17 +244,19 @@
     return pl.BlockSpec((plan.n, plan.block, 2 * W), lambda i, r: (0, i, 0))
 
 
-def store_modes(plan, ref, pair, z):
-    z = z.reshape(plan.n, plan.own, 2 * W).astype(BF)
-    ref[:, pair * plan.own : (pair + 1) * plan.own, :] = z
+def store_by_modes(plan, ref, pair, z):
+    lay = plan.by_modes
+    z = z.reshape(plan.n, lay.chunks, lay.modes, 2 * W).astype(BF)
+    ref[:, :, pair * lay.modes : (pair + 1) * lay.modes, :] = z
+
+
+def load_by_modes(plan, ref, pair):
+    lay = plan.by_modes
+    return ref[:, :, pair * lay.modes : (pair + 1) * lay.modes, :].reshape(MODES, 2 * W)
 
 
 def load_modes(plan, ref, pair):
     return ref[:, pair * plan.own : (pair + 1) * plan.own, :].reshape(MODES, 2 * W)
-
-
-def cost(flops, moved):
-    return pl.CostEstimate(flops=flops, bytes_accessed=moved, transcendentals=0)
 
 
 def flip(index, mask):
@@ -319,35 +336,33 @@
 
 
 class Exchange:
-    SCRATCH = 16
-
     @staticmethod
-    def scratch(plan):
-        n, chips, width = plan.n, plan.chips, 2 * W
+    def scratch(plan, lay):
+        chips, width = plan.chips, 2 * W
         dma = pltpu.SemaphoreType.DMA
-        part = (plan.chunks, 2)
+        part = (lay.chunks, 2)
+        moving = (2, chips, lay.chunks * lay.halves[0], width)
         return [
-            pltpu.VMEM((chips, plan.total, width), BF),
-            pltpu.VMEM((2, chips, plan.chunks * plan.half, width), BF),
-            pltpu.VMEM((2, chips, plan.chunks * plan.half, width), BF),
-            pltpu.VMEM((chips, 2, plan.total, width), BF),
-            pltpu.VMEM((3, plan.acc_rows, 128), F32),
-            pltpu.VMEM((3, plan.acc_rows, 128), F32),
-            dma((plan.chunks,)),
-            dma((plan.chunks,)),
+            pltpu.VMEM((chips, lay.total, width), BF),
+            pltpu.VMEM(moving, BF),
+            pltpu.VMEM(moving, BF),
+            pltpu.VMEM((chips, 2, lay.total, width), BF),
+            pltpu.VMEM((3, lay.acc_rows, 128), F32),
+            pltpu.VMEM((3, lay.acc_rows, 128), F32),
+            dma((lay.chunks,)),
+            dma((lay.chunks,)),
             dma(part + (plan.levels,)),
             dma(part + (plan.levels,)),
             dma(part + (chips,)),
             dma(part + (chips,)),
             dma(part + (chips,)),
             dma(part + (chips,)),
-            dma((plan.chunks,)),
+            dma((lay.chunks,)),
             pltpu.VMEM((plan.own, 256, 256), BF),
         ]
 
-    def __init__(self, plan, part, out, refs, origin=None):
-        self.plan, self.part, self.out = plan, part, out
-        self.origin = part if origin is None else origin
+    def __init__(self, plan, lay, part, out, refs, origin):
+        self.plan, self.lay, self.part, self.out, self.origin = plan, lay, part, out, origin
         (self.sib, self.sums, self.lev, self.res, self.acc, self.mixed,
          self.sib_s, self.sib_r, self.lev_s, self.lev_r, self.ag_s, self.ag_r,
          self.fw_s, self.fw_r, self.out_s, self.kernel) = refs
@@ -357,17 +372,25 @@
     def partners(self):
         return [flip(self.me, 1 << b) for b in range(self.plan.n.bit_length() - 1)]
 
+    def chunk(self, c):
+        return pl.ds(c * self.lay.crow, self.lay.crow)
+
+    def rows(self, c, h):
+        return pl.ds(c * self.lay.crow + h * self.lay.halves[0], self.lay.halves[h])
+
+    def moving(self, c, h):
+        return pl.ds(c * self.lay.halves[0], self.lay.halves[h])
+
     def to_sibling(self, c):
-        rows = pl.ds(c * self.plan.crow, self.plan.crow)
         return remote(
-            self.origin.at[:, 1 - self.core, rows, :], self.sib.at[:, rows, :],
+            self.origin(c, 1 - self.core), self.sib.at[:, self.chunk(c), :],
             self.sib_s.at[c], self.sib_r.at[c], {"rows": flip(self.me, 1)},
         )
 
     def level(self, c, h, t):
         plan = self.plan
         count = plan.chips >> (t + 1)
-        rows = pl.ds(c * plan.half, plan.half)
+        rows = self.moving(c, h)
         at = plan.chips - 2 * count
         return remote(
             self.sums.at[h, pl.ds(count, count), rows, :],
@@ -375,9 +398,6 @@
             self.lev_s.at[c, h, t], self.lev_r.at[c, h, t],
             {"rows": flip(self.me, 1 << plan.orders[h][t])},
         )
-
-    def rows(self, c, h):
-        return pl.ds(c * self.plan.crow + h * self.plan.half, self.plan.half)
 
     def block(self, c, h, owner):
         return self.res.at[lax.div(owner, 2), lax.rem(owner, 2), self.rows(c, h), :]
@@ -399,7 +419,7 @@
         )
 
     def store(self, c):
-        rows = pl.ds(c * self.plan.crow, self.plan.crow)
+        rows = self.chunk(c)
         return pltpu.make_async_copy(
             self.res.at[:, :, rows, :], self.out.at[:, :, rows, :], self.out_s.at[c]
         )
@@ -419,16 +439,16 @@
                     rows = self.rows(c, h)
                     v = self.part[chip, self.core, rows, :].astype(F32)
                     v = v + self.sib[chip, rows, :].astype(F32)
-                    self.sums[h, idx, pl.ds(c * plan.half, plan.half), :] = v.astype(BF)
+                    self.sums[h, idx, self.moving(c, h), :] = v.astype(BF)
                 if far:
                     self.level(c, h, 0).start()
 
     def next_level(self, c, t):
         plan = self.plan
-        rows = pl.ds(c * plan.half, plan.half)
         count = plan.chips >> t
         at = plan.chips - 2 * count
         for h in range(2):
+            rows = self.moving(c, h)
             self.level(c, h, t - 1).wait_recv()
             for idx in reversed(range(count)):
                 v = self.sums[h, idx, rows, :].astype(F32)
@@ -438,36 +458,35 @@
                     self.level(c, h, t).start()
 
     def finish_sum(self, c, scale):
-        plan = self.plan
-        rows = pl.ds(c * plan.half, plan.half)
+        plan, lay = self.plan, self.lay
         for h in range(2):
+            rows = self.moving(c, h)
             self.level(c, h, plan.levels - 1).wait_recv()
             v = self.sums[h, 0, rows, :].astype(F32)
             v = (v + self.lev[h, plan.chips - 2, rows, :].astype(F32)) * scale
+            at = h * lay.halves[0]
             for t, tile in enumerate(tiles(v)):
-                self.acc[t, h * plan.half : (h + 1) * plan.half, :] = tile
+                self.acc[t, at : at + lay.halves[h], :] = tile
 
     def mix(self, c, dims):
-        plan = self.plan
+        lay = self.lay
 
         def one(m):
-            rows = pl.ds(m, plan.slots, stride=plan.own)
+            rows = pl.ds(m, lay.slots, stride=lay.modes)
             lhs = sample_rows(*(self.acc[t, rows, :] for t in range(3))).astype(BF)
-            res = dot(lhs, self.kernel[m], dims)
-            for t, tile in enumerate(pair_tiles(res[: plan.slots], res[plan.slots :])):
+            res = dot(lhs, self.kernel[lay.first_mode(c) + m], dims)
+            for t, tile in enumerate(pair_tiles(res[: lay.slots], res[lay.slots :])):
                 self.mixed[t, rows, :] = tile
 
         unroll = 8
 
-        @pl.loop(0, plan.own // unroll)
+        @pl.loop(0, lay.modes // unroll)
         def _(j):
             for u in range(unroll):
                 one(j * unroll + u)
 
-        result = jnp.concatenate([self.mixed[t, : plan.crow, :] for t in range(3)], axis=1)
-        self.res[lax.div(self.me, 2), self.core, pl.ds(c * plan.crow, plan.crow), :] = (
-            result.astype(BF)
-        )
+        result = jnp.concatenate([self.mixed[t, : lay.crow, :] for t in range(3)], axis=1)
+        self.res[lax.div(self.me, 2), self.core, self.chunk(c), :] = result.astype(BF)
         for h in range(2):
             self.gather(c, h, 0, 0).start()
             self.forward(c, h, 0).start()
@@ -491,7 +510,7 @@
 
     def drain(self):
         plan = self.plan
-        for c in range(plan.chunks):
+        for c in range(self.lay.chunks):
             self.to_sibling(c).wait_send()
             for h in range(2):
                 for t in range(plan.levels):
@@ -504,23 +523,22 @@
             self.store(c).wait()
 
     def clear(self):
-        plan = self.plan
-        if plan.acc_rows > plan.crow:
-            rest = plan.acc_rows - plan.crow
-            self.acc[:, plan.crow :, :] = jnp.zeros((3, rest, 128), F32)
+        lay = self.lay
+        if lay.acc_rows > lay.crow:
+            self.acc[:, lay.crow :, :] = jnp.zeros((3, lay.acc_rows - lay.crow, 128), F32)
 
     def waves(self, total):
-        plan = self.plan
+        plan, chunks = self.plan, self.lay.chunks
         todo = []
-        for c in range(plan.chunks):
+        for c in range(chunks):
             chain = [lambda c=c, t=t: self.next_level(c, t) for t in range(1, plan.levels)]
             chain += [lambda c=c: total(c)]
             chain += [lambda c=c, u=u: self.spread(c, u) for u in range(1, plan.levels + 1)]
             chain += [lambda c=c: self.close(c)]
             todo.append(chain)
         waves = []
-        for w in range(len(todo[0]) + plan.chunks - 1):
-            at = [(c, w - c) for c in reversed(range(plan.chunks))]
+        for w in range(len(todo[0]) + chunks - 1):
+            at = [(c, w - c) for c in reversed(range(chunks))]
             waves.append([todo[c][k] for c, k in at if 0 <= k < len(todo[c])])
         return waves
 
@@ -574,13 +592,16 @@
 
 def forward_kernel(plan, x_big, x_small, spec_weight):
     big, small = plan.big, plan.small
+    lay = plan.by_pairs
     last = plan.wide_steps
 
     def kernel(x_hbm, xs, fb, fs, place, weights, sb_all, ss_all, out, kernel_out, spectrum,
                part, sb, ss, table_sem, ring, ring_sem, *refs):
         i = pl.program_id(0)
         stream = Stream(x_hbm, ring, ring_sem, 2 * plan.wide_per)
-        ex = Exchange(plan, part, out, refs)
+        ex = Exchange(plan, lay, part, out, refs, lambda c, core: part.at[
+            :, core, pl.ds(c * lay.crow, lay.crow), :
+        ])
         loads = [
             pltpu.make_async_copy(sb_all.at[ex.me], sb, table_sem.at[0]),
             pltpu.make_async_copy(ss_all.at[ex.me], ss, table_sem.at[1]),
@@ -619,8 +640,8 @@
 
         def total(c):
             ex.finish_sum(c, 1.0)
-            spectrum[pl.ds(c * plan.crow, plan.crow), :] = jnp.concatenate(
-                [ex.acc[t, : plan.crow, :] for t in range(3)], axis=1
+            spectrum[ex.chunk(c), :] = jnp.concatenate(
+                [ex.acc[t, : lay.crow, :] for t in range(3)], axis=1
             ).astype(BF)
             ex.mix(c, ((1,), (0,)))
 
@@ -630,11 +651,11 @@
 
         waves = ex.waves(total)
         items = []
-        for c in range(plan.chunks):
-            pairs = (c + 1) * plan.span * plan.per
+        for c in range(lay.chunks):
+            pairs = (c + 1) * lay.pairs
             end = min(-(-pairs // plan.wide_per) - 1, last)
             items.append((end, lambda c=c: ex.begin(c)))
-            if c == plan.chunks - 1:
+            if c == lay.chunks - 1:
                 items.append((last, prepare))
                 items += [(last, task) for task in waves.pop(0)]
             items.append((min(end + 1, last), lambda c=c: ex.add_sibling(c)))
@@ -659,19 +680,19 @@
             ANYWHERE,
             ANYWHERE,
         ],
-        out_specs=[ANYWHERE, ANYWHERE, fixed((plan.total, 2 * W))],
+        out_specs=[ANYWHERE, ANYWHERE, fixed((plan.by_pairs.total, 2 * W))],
         out_shape=[
-            jax.ShapeDtypeStruct((plan.chips, 2, plan.total, 2 * W), BF),
+            jax.ShapeDtypeStruct((plan.chips, 2, plan.by_pairs.total, 2 * W), BF),
             jax.ShapeDtypeStruct((plan.own, 256, 256), BF),
-            jax.ShapeDtypeStruct((plan.total, 2 * W), BF),
+            jax.ShapeDtypeStruct((plan.by_pairs.total, 2 * W), BF),
         ],
         scratch_shapes=[
-            pltpu.VMEM((plan.chips, 2, plan.total, 2 * W), BF),
+            pltpu.VMEM((plan.chips, 2, plan.by_pairs.total, 2 * W), BF),
             pltpu.VMEM(big.second.shape[1:], BF),
             pltpu.VMEM(small.second.shape[1:], BF),
             pltpu.SemaphoreType.DMA((3,)),
             *Stream.scratch(min(4, last), 2 * plan.wide_per, big.cells),
-            *Exchange.scratch(plan),
+            *Exchange.scratch(plan, plan.by_pairs),
         ],
         compiler_params=params(collective_id=1, has_side_effects=True),
         name="mode_forward",
@@ -765,7 +786,7 @@
                 groups.setdefault(pair, []).append(cols)
 
             def rows_out(pair):
-                store_modes(plan, z, pair, forward_rows(groups[pair], second[...]))
+                store_by_modes(plan, z, pair, forward_rows(groups[pair], second[...]))
 
             side = []
             rows_back(0)
@@ -809,6 +830,7 @@
     small_field = field_specs(plan)[1]
     big_field = pl.BlockSpec((2 * per, 4, C, big.cells), lambda i, r: (wide(i, last), 0, 0, 0))
     rows = per * plan.own
+    lay = plan.by_modes
     return pl.pallas_call(
         body,
         grid_spec=pltpu.PrefetchScalarGridSpec(
@@ -829,7 +851,9 @@
                 small_field,
                 big_field,
                 small_field,
-                pl.BlockSpec((plan.n, rows, 2 * W), lambda i, r: (0, i, 0)),
+                pl.BlockSpec(
+                    (plan.n, lay.chunks, per * lay.modes, 2 * W), lambda i, r: (0, 0, i, 0)
+                ),
                 const_spec((W, W)),
                 const_spec((W, 128)),
             ],
@@ -840,7 +864,9 @@
             jax.ShapeDtypeStruct(x_small.shape, BF),
             jax.ShapeDtypeStruct(x_big.shape, BF),
             jax.ShapeDtypeStruct(x_small.shape, BF),
-            jax.ShapeDtypeStruct((plan.n, (steps + 1) * rows, 2 * W), BF),
+            jax.ShapeDtypeStruct(
+                (plan.n, lay.chunks, (steps + 1) * per * lay.modes, 2 * W), BF
+            ),
             jax.ShapeDtypeStruct((W, W), F32),
             jax.ShapeDtypeStruct((W, 128), F32),
         ],
@@ -852,41 +878,63 @@
 def backward_kernel(plan, part, p_big, p_small, g_big, g_small, kernel_all, spectrum,
                     lin_weight, lin_grad, columns):
     big, small = plan.big, plan.small
+    lay = plan.by_modes
     stages = plan.n.bit_length() - 1 + plan.nz.bit_length() - 1
-    rows_bits = plan.n.bit_length() - 1
+    z_bits = plan.nz.bit_length() - 1
     pick_all, move_all, move_lin = fold_tables()
     zero_lanes = np.zeros((8, 128), np.float32)
     zero_lanes[0, ::MX] = 1.0
 
     def kernel(pb, ps, gb, gs, place, lw, spec, lin_in, col_in, pick, move, shift, line, part_in, kernel_in,
                db, ds, out, weight_out, lin_out,
-               part, kk, sa, mb, dacc, send_z, recv_z, lin_buf, lin_recv,
-               in_sem, zs, zr, ls, lr, p_ring, p_sem, g_ring, g_sem, d_ring, d_sem, *refs):
+               part, kk, sa, mb, w_rows, w_part, w_sum, w_recv, w_cross, w_full, lin_buf, lin_recv,
+               in_sem, zs, zr, zc, zos, zor, ls, lr, p_ring, p_sem, g_ring, g_sem, d_ring, d_sem, *refs):
         i = pl.program_id(0)
         p_stream = Stream(pb, p_ring, p_sem, 2 * plan.per)
         g_stream = Stream(gb, g_ring, g_sem, 2 * plan.per)
         d_stream = Stream(db, d_ring, d_sem, 2 * plan.per)
-        ex = Exchange(plan, part, out, refs, part_in)
+        ex = Exchange(plan, lay, part, out, refs, lambda c, core: part_in.at[
+            :, core, c, pl.ds(0, lay.crow), :
+        ])
         here = lax.axis_index("samples")
         loads = [
             pltpu.make_async_copy(
-                part_in.at[:, :, pl.ds(0, plan.total), :], part, in_sem.at[0]
-            ),
-            pltpu.make_async_copy(kernel_in, ex.kernel, in_sem.at[1]),
+                part_in.at[:, :, c, pl.ds(0, lay.crow), :], part.at[:, :, ex.chunk(c), :],
+                in_sem.at[1 + c],
+            )
+            for c in range(lay.chunks)
         ]
-
-        def z_peer(d):
-            return lax.rem(here + d, plan.nz)
-
-        def to_z(d):
-            return remote(
-                send_z.at[z_peer(d)], recv_z.at[d], zs.at[d], zr.at[d], {"samples": z_peer(d)}
-            )
+        load_kernel = pltpu.make_async_copy(kernel_in, ex.kernel, in_sem.at[0])
+
+        left = here < plan.nz // 2
+        place_z = jnp.where(left, here, plan.nz - 1 - here)
+        at_end = place_z == 0
+        at_middle = place_z == plan.nz // 2 - 1
+        inward = {"samples": jnp.where(left, here + 1, here - 1)}
+        outward = {"samples": jnp.where(left, here - 1, here + 1)}
+
+        def to_inner(p):
+            return remote(w_sum.at[p], w_recv.at[p], zs.at[p], zr.at[p], inward)
+
+        def across(p):
+            return remote(w_sum.at[p], w_cross.at[p], zs.at[p], zc.at[p], inward)
+
+        def to_outer(p):
+            return remote(w_full.at[p], w_full.at[p], zos.at[p], zor.at[p], outward)
+
+        def send_inward(p):
+            @pl.when(at_middle)
+            def _():
+                across(p).start()
+
+            @pl.when(jnp.logical_not(at_middle))
+            def _():
+                to_inner(p).start()
 
         def lin_partner(k):
-            if k < rows_bits:
-                return {"rows": flip(ex.me, 1 << k)}
-            return {"samples": flip(here, 1 << (k - rows_bits))}
+            if k < z_bits:
+                return {"samples": flip(here, 1 << k)}
+            return {"rows": flip(ex.me, 1 << (k - z_bits))}
 
         def lin_step(k):
             return remote(lin_buf.at[k], lin_recv.at[k], ls.at[k], lr.at[k], lin_partner(k))
@@ -895,9 +943,10 @@
         def _():
             for load in loads:
                 load.start()
+            load_kernel.start()
             greet([{"rows": d} for d in ex.partners()]
-                  + [{"samples": z_peer(d)} for d in range(1, plan.nz)])
-            for c in range(plan.chunks):
+                  + [{"samples": lax.rem(here + d, plan.nz)} for d in range(1, plan.nz)])
+            for c in range(lay.chunks):
                 ex.begin(c)
             folded = None
             for q in range(4):
@@ -913,15 +962,15 @@
             )
             lin_step(0).start()
             kk[...] = build_lin(place[...], lw)[:, :W]
-            loads[0].wait()
-            for c in range(plan.chunks):
+            for c, load in enumerate(loads):
+                load.wait()
                 ex.add_sibling(c)
             ex.clear()
-            sa[...] = jnp.zeros_like(sa)
-            mb[...] = jnp.zeros_like(mb)
-            dacc[...] = jnp.zeros_like(dacc)
-            send_z[...] = jnp.zeros_like(send_z)
-            loads[1].wait()
+            if lay.acc_rows > lay.crow:
+                rest = lay.acc_rows - lay.crow
+                sa[:, :, lay.crow :, :] = jnp.zeros((4, 2, rest, 128), F32)
+                mb[:, :, lay.crow :, :] = jnp.zeros((8, 2, rest, 128), F32)
+            load_kernel.wait()
 
         def run(p, g, d, geo, count):
             for at in range(2 * count):
@@ -943,10 +992,10 @@
             run(ps, gs, ds, small, plan.nsmall // 2)
 
         def weight_grad(c):
-            crow = plan.crow
+            crow, modes = lay.crow, lay.modes
             grads = sample_rows(*(ex.acc[t, :crow, :] for t in range(3))).astype(BF)
-            held = spec[pl.ds(c * crow, crow), :].astype(F32)
-            spectra = sample_rows(*tiles(held)).astype(BF)
+            held = spec[:, lay.first_mode(c) : lay.first_mode(c) + modes, :]
+            spectra = sample_rows(*tiles(held.reshape(crow, 2 * W).astype(F32))).astype(BF)
             for t, tile in enumerate(tiles(dot(spectra, pick[...]))):
                 sa[t, 0, :crow, :] = tile[:crow]
                 sa[t, 1, :crow, :] = tile[crow:]
@@ -955,7 +1004,7 @@
                 mb[t, 1, :crow, :] = tile[crow:]
 
             def one(m):
-                rows = pl.ds(m, plan.slots, stride=plan.own)
+                rows = pl.ds(m, lay.slots, stride=modes)
                 left = [sa[q, s, rows, :] for q in range(4) for s in range(2)]
                 right = [
                     jnp.concatenate([mb[2 * q, s, rows, :], mb[2 * q + 1, s, rows, :]], axis=1)
@@ -966,34 +1015,57 @@
                     jnp.concatenate(right, axis=0).astype(BF),
                     ((0,), (0,)),
                 )
-                dacc[m] += v[:C]
-
-            unroll = 4
-
-            @pl.loop(0, plan.own // unroll)
+                return v[:C]
+
+            unroll = 2
+
+            @pl.loop(0, modes // (2 * unroll))
             def _(j):
                 for u in range(unroll):
-                    one(j * unroll + u)
-
-        def send_weights():
-            pairs = []
-            for j in range(plan.own // 2):
-                pairs.append(jnp.concatenate(pair_tiles(dacc[2 * j], dacc[2 * j + 1]), axis=1))
-            rows = jnp.concatenate(pairs, axis=0).astype(BF)
-            for z in range(plan.nz):
-                lo = z * plan.zrows
-                hi = min(lo + plan.zrows, plan.wrows)
-                if hi > lo:
-                    send_z[z, : hi - lo, :] = rows[lo:hi]
-            for d in range(1, plan.nz):
-                to_z(d).start()
-
-        def sum_weights():
-            v = send_z[here].astype(F32)
-            for d in range(1, plan.nz):
-                to_z(d).wait_recv()
-                v = v + recv_z[d].astype(F32)
-            weight_out[...] = v.astype(BF)
+                    pair = j * unroll + u
+                    v = pair_tiles(one(2 * pair), one(2 * pair + 1))
+                    v = jnp.concatenate(v, axis=1).astype(BF)
+                    w_rows[pl.ds(pl.multiple_of(pair * C, 16), C), :] = v
+
+            for k in range(plan.pieces):
+                p = c * plan.pieces + k
+                w_part[p] = w_rows[k * plan.zrows : (k + 1) * plan.zrows, :]
+
+                @pl.when(at_end)
+                def _(p=p):
+                    w_sum[p] = w_part[p]
+                    send_inward(p)
+
+        def sum_weights(c):
+            for p in range(c * plan.pieces, (c + 1) * plan.pieces):
+                @pl.when(jnp.logical_not(at_end))
+                def _(p=p):
+                    to_inner(p).wait_recv()
+                    w_sum[p] = (w_part[p].astype(F32) + w_recv[p].astype(F32)).astype(BF)
+                    send_inward(p)
+
+        def cross_weights(c):
+            for p in range(c * plan.pieces, (c + 1) * plan.pieces):
+                @pl.when(at_middle)
+                def _(p=p):
+                    across(p).wait_recv()
+                    w_full[p] = (w_sum[p].astype(F32) + w_cross[p].astype(F32)).astype(BF)
+
+                    @pl.when(jnp.logical_not(at_end))
+                    def _():
+                        to_outer(p).start()
+
+        def finish_weights(c):
+            for p in range(c * plan.pieces, (c + 1) * plan.pieces):
+                @pl.when(jnp.logical_not(at_middle))
+                def _(p=p):
+                    to_outer(p).wait_recv()
+
+                    @pl.when(jnp.logical_not(at_end))
+                    def _():
+                        to_outer(p).start()
+
+                weight_out[p * plan.zrows : (p + 1) * plan.zrows, :] = w_full[p]
 
         def lin_next(k):
             lin_step(k).wait_recv()
@@ -1007,27 +1079,41 @@
         def chunk_total(c):
             ex.finish_sum(c, 1.0 / MX)
             ex.mix(c, ((1,), (1,)))
-            weight_grad(c)
-            if c == plan.chunks - 1:
-                send_weights()
 
         last = plan.count - 1
-        items = [(2 * k + 1, lambda k=k: lin_next(k)) for k in range(stages)]
-        for w, wave in enumerate(ex.waves(chunk_total)):
-            items += [(2 + 2 * w, task) for task in wave]
-        items.append((last, sum_weights))
+        items = [(1 + k, lambda k=k: lin_next(k)) for k in range(z_bits)]
+        waves = ex.waves(chunk_total)
+        first = plan.levels - 1
+        for w, wave in enumerate(waves):
+            step = 2 + 2 * w
+            items += [(step, task) for task in wave]
+            for lag, task in enumerate((weight_grad, sum_weights, cross_weights)):
+                if 0 <= w - first - lag < lay.chunks:
+                    at = len(items) if lag < 2 else len(items) - len(wave)
+                    items.insert(at, (step, lambda task=task, c=w - first - lag: task(c)))
+            if w >= 3 and z_bits + w -3 < stages:
+                items.append((step, lambda k=z_bits + w -3: lin_next(k)))
+        for lag, task in ((1, sum_weights), (2, cross_weights)):
+            items += [(last, lambda task=task, c=c: task(c))
+                      for c in range(max(0, len(waves) - first - lag), lay.chunks)]
+        items += [(last, lambda c=c: finish_weights(c)) for c in range(lay.chunks)]
         schedule(last, i, items)
 
         @pl.when(i == last)
         def _():
             ex.drain()
             d_stream.flush(plan.steps)
-            for d in range(1, plan.nz):
-                to_z(d).wait_send()
+            for p in range(lay.chunks * plan.pieces):
+                to_inner(p).wait_send()
+
+                @pl.when(jnp.logical_not(at_end))
+                def _(p=p):
+                    to_outer(p).wait_send()
+
             for k in range(stages):
                 lin_step(k).wait_send()
 
-    acc = plan.acc_rows
+    acc = lay.acc_rows
     dma = pltpu.SemaphoreType.DMA
     return pl.pallas_call(
         kernel,
@@ -1039,7 +1125,7 @@
             plain_fields(plan)[1],
             fixed((W, 1024)),
             fixed((4, C, C)),
-            fixed((plan.total, 2 * W)),
+            fixed(spectrum.shape),
             fixed((W, W)),
             fixed((W, 128)),
             fixed(pick_all.shape),
@@ -1053,35 +1139,33 @@
             ANYWHERE,
             plain_fields(plan)[1],
             ANYWHERE,
-            fixed((plan.zrows, 2 * W)),
+            fixed((lay.chunks * plan.wrows, 2 * W)),
             fixed((C + 8, W)),
         ],
         out_shape=[
             jax.ShapeDtypeStruct(p_big.shape, BF),
             jax.ShapeDtypeStruct(p_small.shape, BF),
-            jax.ShapeDtypeStruct((plan.chips, 2, plan.total, 2 * W), BF),
-            jax.ShapeDtypeStruct((plan.zrows, 2 * W), BF),
+            jax.ShapeDtypeStruct((plan.chips, 2, plan.by_pairs.total, 2 * W), BF),
+            jax.ShapeDtypeStruct((lay.chunks * plan.wrows, 2 * W), BF),
             jax.ShapeDtypeStruct((C + 8, W), F32),
         ],
         scratch_shapes=[
-            pltpu.VMEM((plan.chips, 2, plan.total, 2 * W), BF),
+            pltpu.VMEM((plan.chips, 2, plan.by_pairs.total, 2 * W), BF),
             pltpu.VMEM((W, W), BF),
             pltpu.VMEM((4, 2, acc, 128), F32),
             pltpu.VMEM((8, 2, acc, 128), F32),
-            pltpu.VMEM((plan.own, C, 256), F32),
-            pltpu.VMEM((plan.nz, plan.zrows, 2 * W), BF),
-            pltpu.VMEM((plan.nz, plan.zrows, 2 * W), BF),
+            pltpu.VMEM((plan.wrows, 2 * W), BF),
+            *[pltpu.VMEM((lay.chunks * plan.pieces, plan.zrows, 2 * W), BF)] * 5,
             pltpu.VMEM((stages, C + 8, W), F32),
             pltpu.VMEM((stages, C + 8, W), F32),
-            dma((2,)),
-            dma((plan.nz,)),
-            dma((plan.nz,)),
+            dma((1 + lay.chunks,)),
+            *[dma((lay.chunks * plan.pieces,))] * 5,
             dma((stages,)),
             dma((stages,)),
             *Stream.scratch(min(4, plan.steps), 2 * plan.per, big.cells),
             *Stream.scratch(min(4, plan.steps), 2 * plan.per, big.cells),
             *Stream.scratch(min(3, plan.steps), 2 * plan.per, big.cells),
-            *Exchange.scratch(plan),
+            *Exchange.scratch(plan, lay),
         ],
         compiler_params=params(collective_id=2, has_side_effects=True),
         name="mode_backward",
@@ -1089,7 +1173,7 @@
       pick_all, move_all, move_lin, zero_lanes, part, kernel_all)
 
 
-def input_grads(plan, rank, part_big, part_small, modes, lin_sum):
+def input_grads(plan, rank, part_big, part_small, modes, lin_sum, weights):
     big, small = plan.big, plan.small
     per, steps = plan.wide_per, plan.wide_steps
     last = steps - 1
@@ -1098,9 +1182,18 @@
     for p in range(4):
         split[p * C : p * C + C, p, :C] = np.eye(C)
     split = split.reshape(W, 512)
-
-    def body(r, pb, ps, mb, ms, vb, eb, vs, es, lin, cut, db, ds, lin_out, bias_out):
+    blades = np.zeros((2, 2 * W, 4, 128), np.float32)
+    for odd in range(2):
+        for lane in range(W):
+            at = lane + 128 * odd if lane < 128 else 128 + 64 * odd + lane
+            blades[odd, at, lane // C, lane % C] = 1.0
+    blades = low(blades.reshape(2, 2 * W, 512))
+    lay = plan.by_modes
+
+    def body(r, pb, ps, mb, ms, vb, eb, vs, es, lin, cut, w_in, blade,
+             db, ds, lin_out, bias_out, w_out, w_held, w_sem):
         i = pl.program_id(0)
+        put = pltpu.make_async_copy(w_held, w_out, w_sem.at[0])
 
         @pl.when(i == 0)
         def _():
@@ -1111,12 +1204,26 @@
             for p in range(4):
                 lin_out[p] = v[:C, 128 * p : 128 * p + C]
                 bias_out[p : p + 1, :] = v[C : C + 1, 128 * p : 128 * p + C]
+            for c in range(lay.chunks):
+                rows = w_in[c * plan.wrows : (c + 1) * plan.wrows, :]
+                for odd in range(2):
+                    v = dot(rows, blade[odd])
+                    for j in range(lay.modes // 2):
+                        for p in range(4):
+                            w_held[lay.first_mode(c) + 2 * j + odd, p] = (
+                                v[j * C : j * C + C, 128 * p : 128 * p + C]
+                            )
+            put.start()
+
+        @pl.when(i == steps)
+        def _():
+            put.wait()
 
         def run(part, m, d, geo, inverse, spread, count):
             span = spread.shape[1]
             qs = []
             for pair in range(count):
-                qs += inverse_pair(geo, load_modes(plan, m, pair), inverse[...], 1.0)
+                qs += inverse_pair(geo, load_by_modes(plan, m, pair), inverse[...], 1.0)
             q = jnp.concatenate(qs, axis=0) * jnp.asarray(1.0 / geo.side, BF)
             for j in range(geo.cells // span):
                 v = dot(q[:, 128 * j : 128 * j + 128], spread[...])
@@ -1132,6 +1239,7 @@
         def _():
             run(ps, ms, ds, small, vs, es, plan.nsmall // 2)
 
+    extra = [lin_sum, split, weights, blades]
     tables = []
     specs = []
     for geo in (big, small):
@@ -1147,77 +1255,53 @@
             in_specs=[
                 big_field,
                 small_field,
-                pl.BlockSpec((plan.n, per * plan.own, 2 * W), lambda i, r: (0, wide(i, last), 0)),
-                pl.BlockSpec((plan.n, plan.block, 2 * W), lambda i, r: (0, plan.steps, 0)),
+                pl.BlockSpec(
+                    (plan.n, lay.chunks, per * lay.modes, 2 * W),
+                    lambda i, r: (0, 0, wide(i, last), 0),
+                ),
+                pl.BlockSpec(
+                    (plan.n, lay.chunks, plan.per * lay.modes, 2 * W),
+                    lambda i, r: (0, 0, plan.steps, 0),
+                ),
                 *specs,
-                const_spec(lin_sum.shape),
-                const_spec(split.shape),
+                *[const_spec(v.shape) for v in extra],
             ],
-            out_specs=[big_field, small_field, const_spec((4, C, C)), const_spec((4, C))],
+            out_specs=[big_field, small_field, const_spec((4, C, C)), const_spec((4, C)),
+                       ANYWHERE],
+            scratch_shapes=[
+                pltpu.VMEM((plan.own, 4, C, C), F32), pltpu.SemaphoreType.DMA((1,))
+            ],
         ),
         out_shape=[
             jax.ShapeDtypeStruct(part_big.shape, F32),
             jax.ShapeDtypeStruct(part_small.shape, F32),
             jax.ShapeDtypeStruct((4, C, C), F32),
             jax.ShapeDtypeStruct((4, C), F32),
+            jax.ShapeDtypeStruct((plan.own, 4, C, C), F32),
         ],
         compiler_params=params(),
         name="input_grads",
-    )(rank, part_big, part_small, modes, modes, *tables, lin_sum, split)
-
-
-def collect(plan, here, pieces):
-    pick = np.zeros((2, 2 * W, 4, 128), np.float32)
-    for odd in range(2):
-        for lane in range(W):
-            at = lane + 128 * odd if lane < 128 else 128 + 64 * odd + lane
-            pick[odd, at, lane // C, lane % C] = 1.0
-    pick = low(pick.reshape(2, 2 * W, 512))
-
-    def body(z, pick_ref, *refs):
-        pieces, out, rows = refs[: plan.nz], refs[plan.nz], refs[plan.nz + 1]
-        for d, piece in enumerate(pieces):
-            at = lax.rem(z[0] + plan.nz - d, plan.nz) * plan.zrows
-            rows[pl.ds(pl.multiple_of(at, 16), plan.zrows), :] = piece[...]
-        for odd in range(2):
-            v = dot(rows[: plan.wrows, :], pick_ref[odd])
-            for j in range(plan.own // 2):
-                for p in range(4):
-                    out[2 * j + odd, p] = v[j * C : j * C + C, 128 * p : 128 * p + C]
-
-    vmem = pl.BlockSpec(memory_space=pltpu.VMEM)
-    return pl.pallas_call(
-        body,
-        in_specs=[pl.BlockSpec(memory_space=pltpu.SMEM)] + [vmem] * (1 + plan.nz),
-        out_specs=vmem,
-        out_shape=jax.ShapeDtypeStruct((plan.own, 4, C, C), F32),
-        scratch_shapes=[pltpu.VMEM((plan.nz * plan.zrows, 2 * W), BF)],
-        compiler_params=params(),
-        name="collect",
-    )(here, pick, *pieces)
+    )(rank, part_big, part_small, modes, modes, *tables, *extra)
 
 
 def on_device(plan, x_big, x_small, spec_weight, lin_weight, lin_bias, grad_big, grad_small):
     rank = lax.axis_index("rows").reshape(1)
-    here = lax.axis_index("samples").reshape(1)
-    whole = (plan.n, plan.total, 2 * W)
+    width = 2 * W
     modes, kernel, spectrum = forward_kernel(plan, x_big, x_small, spec_weight)
     out_big, out_small, pre_big, pre_small, part, lin_grad, columns = cells_pass(
-        plan, rank, x_big, x_small, grad_big, grad_small, modes.reshape(whole), lin_weight,
-        lin_bias,
+        plan, rank, x_big, x_small, grad_big, grad_small, modes.reshape(plan.n, -1, width),
+        lin_weight, lin_bias,
     )
-    part_big, part_small, modes, weight_part, lin_sum = backward_kernel(
-        plan, part.reshape(plan.chips, 2, -1, 2 * W), pre_big, pre_small,
-        grad_big, grad_small, kernel, spectrum, lin_weight, lin_grad, columns,
+    lay = plan.by_modes
+    part_big, part_small, modes, weights, lin_sum = backward_kernel(
+        plan, part.reshape((plan.chips, 2) + part.shape[1:]), pre_big, pre_small,
+        grad_big, grad_small, kernel, spectrum.reshape(-1, plan.own, width), lin_weight,
+        lin_grad, columns,
     )
-    pieces = [weight_part]
-    for d in range(1, plan.nz):
-        pairs = [(z, (z + d) % plan.nz) for z in range(plan.nz)]
-        pieces.append(lax.ppermute(weight_part, "samples", pairs))
-    dx_big, dx_small, lin_weight_grad, lin_bias_grad = input_grads(
-        plan, rank, part_big, part_small, modes.reshape(whole), lin_sum
+    dx_big, dx_small, lin_weight_grad, lin_bias_grad, spec_grad = input_grads(
+        plan, rank, part_big, part_small, modes.reshape(plan.n, lay.chunks, -1, width),
+        lin_sum, weights,
     )
-    spec_grad = collect(plan, here, pieces)
     return out_big, out_small, dx_big, dx_small, spec_grad, lin_weight_grad, lin_bias_grad
 
 

time: 178 us -> 168 us (0.944)
  starting transfers between devices: 5.32 us -> 0 us
  Pallas kernels: 171 us -> 167 us
    ppermute x3 -> x0, starting transfers between devices: 5.32 us -> none  [on_device(): pieces.append(lax.ppermute(weight_part, 'samples', pairs))]
    pallas_call x1 -> x0, Pallas kernels: 3.98 us -> none  [collect(): pl.pallas_call(body, in_specs=[pl.BlockSpec(memory_space=pltpu.SMEM)] + [...]
  transfers between devices with their start and end apart: 3 -> 0, of which waited for: 0 -> 0; matrix products, arithmetic and copies ran while one was open for 0% -> 0% of each run, Pallas kernels for 15% -> 0%
where the time goes in v4:
time: 168 us
  Pallas kernels  167 us (99%)
    pallas_call x1, Pallas kernels, backward_kernel(): pl.pallas_call(kernel, grid=(plan.count,), in_specs=[ANYWHERE, plain_fiel...  51 us
    pallas_call x1, Pallas kernels, cells_pass(): pl.pallas_call(body, grid_spec=pltpu.PrefetchScalarGridSpec(num_scalar_pr...  44.7 us
    pallas_call x1, Pallas kernels, forward_kernel(): pl.pallas_call(kernel, grid=(last + 1,), in_specs=[ANYWHERE, plain_fields...  42.9 us
    pallas_call x1, Pallas kernels, input_grads(): pl.pallas_call(body, grid_spec=pltpu.PrefetchScalarGridSpec(num_scalar_pr...  28.4 us

profile of v4, /device:TPU:0, one launch (start us, length us, event | category | flops | bytes accessed | tf_op | source)
XLA Modules:
  0.0 167.8 jit_solution(13904546466432588200)
XLA Ops:
  0.6 42.9 %mode_forward.1 = (bf16[4,2,480,384]{3,2,1,0:T(8,128)(2,1)}, bf16[32,256,256]{2,1,0:T(8,128)(2,1)}, bf16[480,384]{1,0:T(8,128)(2,1)}) custom-call(bf16[28,4,48,2048]{3,2,1,0:T(8,128)(2,1)} %xb.1, bf16[2,4,48,512]{3,2,1,0:T(8,128)(2,1)} %xs.3, bf16[1024,256]{1,0:T(8,128)(2,1)} %constant.44.clone.fb, bf16[512,256]{1,0:T(8,128)(2,1)} %constant.45.clone.fs, ...), custom_call_target="tpu_custom_call" | custom-call | tf_op jit(solution)/shard_map/mode_forward/pallas_call | solution.py:670
  43.6 44.7 %cells.1 = (bf16[28,4,48,2048]{3,2,1,0:T(8,128)(2,1)}, bf16[2,4,48,512]{3,2,1,0:T(8,128)(2,1)}, bf16[28,4,48,2048]{3,2,1,0:T(8,128)(2,1)}, bf16[2,4,48,512]{3,2,...) custom-call(s32[1]{0:T(128)} %bitcast.r, ...), custom_call_target="tpu_custom_call" | custom-call | tf_op jit(solution)/shard_map/cells/pallas_call | solution.py:834
  88.3 51.0 %mode_backward.1 = (bf16[28,4,48,2048]{3,2,1,0:T(8,128)(2,1)}, bf16[2,4,48,512]{3,2,1,0:T(8,128)(2,1)}, bf16[4,2,480,384]{3,2,1,0:T(8,128)(2,1)}, bf16[768,384]{1,0:T(8,128)(2,1)}, f32[56,192]{1,0:T(8,128)}) custom-call(bf16[28,4,48,2048]{3,2,1,0:T(8,128)(2,1)} %get-tuple-element.30.pb, bf16[2,4,48,512]{3,2,1,0:T(8,128)(2,1)} %get-tuple-element.31.ps, ...), custom_call_target="tpu_custom_call" | custom-call | tf_op jit(solution)/shard_map/mode_backward/pallas_call | solution.py:1118
  139.3 28.4 %input_grads.1 = (f32[28,4,48,2048]{3,2,1,0:T(8,128)}, f32[2,4,48,512]{3,2,1,0:T(8,128)}, f32[4,48,48]{2,1,0:T(8,128)}, f32[4,48]{1,0:T(4,128)}, f32[32,4,48,48]{3,2,1,0:T(8,128)}) custom-call(s32[1]{0:T(128)} %bitcast.r, bf16[28,4,48,2048]{3,2,1,0:T(8,128)(2,1)} %get-tuple-element.37.pb, bf16[2,4,48,512]{3,2,1,0:T(8,128)(2,1)} %get-tuple-element.38.ps, ...), custom_call_target="tpu_custom_call" | custom-call | tf_op jit(solution)/shard_map/input_grads/pallas_call | solution.py:1250

commit v5 on v4

--- a/solution.py
+++ b/solution.py
@@ -203,7 +203,7 @@
         self.orders = (bits, bits[::-1])
         self.levels = len(bits)
         self.wrows = self.by_modes.modes // 2 * C
-        self.pieces = 2
+        self.pieces = 4
         self.zrows = self.wrows // self.pieces
         assert self.nz % 2 == 0 and self.zrows % 16 == 0
 
@@ -721,9 +721,9 @@
     per, steps = plan.wide_per, plan.wide_steps
     last = steps - 1
 
-    def body(r, xb, xs, gb, gs, m, ms, fb, sb, vb, eb, fs, ss, vs, es,
+    def body(r, xb, xs, gb, gs, m, m_next, ms, fb, sb, vb, eb, fs, ss, vs, es,
              place, rows_table, line, eye, lw, lb, ob, os_, pb, ps, z, lin_acc, y_acc,
-             kt, bias_ref):
+             kt, bias_ref, q_next):
         i = pl.program_id(0)
 
         @pl.when(i == 0)
@@ -737,16 +737,26 @@
             lin_acc[...] = jnp.zeros_like(lin_acc)
             y_acc[...] = jnp.zeros_like(y_acc)
 
-        def run(x, g, o, d, m, z, geo, first, second, inverse, spread, count):
+        def coefficients(geo, m, pair, inverse):
+            qs = inverse_pair(geo, load_modes(plan, m, pair), inverse[...], 0.5 / MX)
+            line = jnp.concatenate([bias_ref[...]] * (geo.qlanes // 128), axis=1)
+            return [q + line for q in qs]
+
+        def prepare(m):
+            for s, q in enumerate(coefficients(plan.big, m, 0, vb)):
+                q_next[s] = q
+
+        @pl.when(i == 0)
+        def _():
+            prepare(m)
+
+        def run(x, g, o, d, m, z, geo, first, second, inverse, spread, count, following=None):
             wide_cells = 2 * geo.side
             lane = lax.broadcasted_iota(jnp.int32, (W, 128), 1)
             held, groups = {}, {}
 
             def rows_back(pair):
-                qs = inverse_pair(geo, load_modes(plan, m, pair), inverse[...], 0.5 / MX)
-                line = jnp.concatenate([bias_ref[...]] * (geo.qlanes // 128), axis=1)
-                for s in range(2):
-                    held[2 * pair + s] = qs[s] + line
+                held[2 * pair], held[2 * pair + 1] = coefficients(geo, m, pair, inverse)
 
             def main(at, p):
                 lo = p * wide_cells
@@ -789,25 +799,39 @@
                 store_by_modes(plan, z, pair, forward_rows(groups[pair], second[...]))
 
             side = []
-            rows_back(0)
+            if following is None:
+                rows_back(0)
+            else:
+                for s in range(2):
+                    held[s] = q_next.at[s]
             for at in range(2 * count):
                 pair = at // 2
                 if at % 2 == 0 and pair + 1 < count:
                     side.append(lambda pair=pair: rows_back(pair + 1))
+                if at == 2 and following is not None:
+                    side.append(following)
+                done = 0
                 for p in range(geo.npairs):
                     main(at, p)
                     if side:
                         side.pop(0)()
-                side += [lambda at=at, k=k: weight_grad(at, k) for k in range(2)]
+                    if 2 * (p + 1) == geo.npairs:
+                        side.append(lambda at=at: weight_grad(at, 0))
+                    if at % 2 == 1 and (p + 1) * geo.ngroups // geo.npairs > done:
+                        side.append(lambda pair=pair, k=done: columns(pair, k))
+                        done += 1
+                if geo.npairs == 1:
+                    side.append(lambda at=at: weight_grad(at, 0))
+                side.append(lambda at=at: weight_grad(at, 1))
                 if at % 2 == 1:
-                    side += [lambda pair=pair, k=k: columns(pair, k) for k in range(geo.ngroups)]
                     side.append(lambda pair=pair: rows_out(pair))
             for task in side:
                 task()
 
         @pl.when(i < steps)
         def _():
-            run(xb, gb, ob, pb, m, z, plan.big, fb, sb, vb, eb, per)
+            run(xb, gb, ob, pb, m, z, plan.big, fb, sb, vb, eb, per,
+                lambda: prepare(m_next))
 
         @pl.when(i == steps)
         def _():
@@ -842,6 +866,9 @@
                 big_field,
                 small_field,
                 pl.BlockSpec((plan.n, rows, 2 * W), lambda i, r: (0, wide(i, last), 0)),
+                pl.BlockSpec(
+                    (plan.n, plan.own, 2 * W), lambda i, r: (0, wide(i + 1, last) * per, 0)
+                ),
                 pl.BlockSpec((plan.n, plan.block, 2 * W), lambda i, r: (0, plan.steps, 0)),
                 *specs,
                 *[const_spec(v.shape) for v in extra],
@@ -857,7 +884,11 @@
                 const_spec((W, W)),
                 const_spec((W, 128)),
             ],
-            scratch_shapes=[pltpu.VMEM((W, 2 * W), BF), pltpu.VMEM((W, 128), BF)],
+            scratch_shapes=[
+                pltpu.VMEM((W, 2 * W), BF),
+                pltpu.VMEM((W, 128), BF),
+                pltpu.VMEM((2, W, big.qlanes), BF),
+            ],
         ),
         out_shape=[
             jax.ShapeDtypeStruct(x_big.shape, BF),
@@ -872,7 +903,7 @@
         ],
         compiler_params=params(),
         name="cells",
-    )(rank, x_big, x_small, g_big, g_small, modes, modes, *tables, *extra)
+    )(rank, x_big, x_small, g_big, g_small, modes, modes, modes, *tables, *extra)
 
 
 def backward_kernel(plan, part, p_big, p_small, g_big, g_small, kernel_all, spectrum,
@@ -1078,6 +1109,7 @@
 
         def chunk_total(c):
             ex.finish_sum(c, 1.0 / MX)
+            weight_grad(c)
             ex.mix(c, ((1,), (1,)))
 
         last = plan.count - 1
@@ -1088,7 +1120,7 @@
             step = 2 + 2 * w
             items += [(step, task) for task in wave]
             for lag, task in enumerate((weight_grad, sum_weights, cross_weights)):
-                if 0 <= w - first - lag < lay.chunks:
+                if lag and 0 <= w - first - lag < lay.chunks:
                     at = len(items) if lag < 2 else len(items) - len(wave)
                     items.insert(at, (step, lambda task=task, c=w - first - lag: task(c)))
             if w >= 3 and z_bits + w -3 < stages:

time: 168 us -> 165 us (0.982)
  Pallas kernels: 167 us -> 164 us
where the time goes in v5:
time: 165 us
  Pallas kernels  164 us (99%)
    pallas_call x1, Pallas kernels, backward_kernel(): pl.pallas_call(kernel, grid=(plan.count,), in_specs=[ANYWHERE, plain_fiel...  49.8 us
    pallas_call x1, Pallas kernels, cells_pass(): pl.pallas_call(body, grid_spec=pltpu.PrefetchScalarGridSpec(num_scalar_pr...  43.1 us
    pallas_call x1, Pallas kernels, forward_kernel(): pl.pallas_call(kernel, grid=(last + 1,), in_specs=[ANYWHERE, plain_fields...  42.9 us
    pallas_call x1, Pallas kernels, input_grads(): pl.pallas_call(body, grid_spec=pltpu.PrefetchScalarGridSpec(num_scalar_pr...  28.4 us

profile of v5, /device:TPU:0, one launch (start us, length us, event | category | flops | bytes accessed | tf_op | source)
XLA Modules:
  0.0 165.1 jit_solution(13448828077451643763)
XLA Ops:
  0.6 42.9 %mode_forward.1 = (bf16[4,2,480,384]{3,2,1,0:T(8,128)(2,1)}, bf16[32,256,256]{2,1,0:T(8,128)(2,1)}, bf16[480,384]{1,0:T(8,128)(2,1)}) custom-call(bf16[28,4,48,2048]{3,2,1,0:T(8,128)(2,1)} %xb.1, bf16[2,4,48,512]{3,2,1,0:T(8,128)(2,1)} %xs.3, bf16[1024,256]{1,0:T(8,128)(2,1)} %constant.44.clone.fb, bf16[512,256]{1,0:T(8,128)(2,1)} %constant.45.clone.fs, ...), custom_call_target="tpu_custom_call" | custom-call | tf_op jit(solution)/shard_map/mode_forward/pallas_call | solution.py:670
  43.6 43.1 %cells.1 = (bf16[28,4,48,2048]{3,2,1,0:T(8,128)(2,1)}, bf16[2,4,48,512]{3,2,1,0:T(8,128)(2,1)}, bf16[28,4,48,2048]{3,2,1,0:T(8,128)(2,1)}, bf16[2,4,48,512]{3,2,...) custom-call(s32[1]{0:T(128)} %bitcast.r, ...), custom_call_target="tpu_custom_call" | custom-call | tf_op jit(solution)/shard_map/cells/pallas_call | solution.py:858
  86.7 49.8 %mode_backward.1 = (bf16[28,4,48,2048]{3,2,1,0:T(8,128)(2,1)}, bf16[2,4,48,512]{3,2,1,0:T(8,128)(2,1)}, bf16[4,2,480,384]{3,2,1,0:T(8,128)(2,1)}, bf16[768,384]{1,0:T(8,128)(2,1)}, f32[56,192]{1,0:T(8,128)}) custom-call(bf16[28,4,48,2048]{3,2,1,0:T(8,128)(2,1)} %get-tuple-element.30.pb, bf16[2,4,48,512]{3,2,1,0:T(8,128)(2,1)} %get-tuple-element.31.ps, ...), custom_call_target="tpu_custom_call" | custom-call | tf_op jit(solution)/shard_map/mode_backward/pallas_call | solution.py:1150
  136.5 28.4 %input_grads.1 = (f32[28,4,48,2048]{3,2,1,0:T(8,128)}, f32[2,4,48,512]{3,2,1,0:T(8,128)}, f32[4,48,48]{2,1,0:T(8,128)}, f32[4,48]{1,0:T(4,128)}, f32[32,4,48,48]{3,2,1,0:T(8,128)}) custom-call(s32[1]{0:T(128)} %bitcast.r, bf16[28,4,48,2048]{3,2,1,0:T(8,128)(2,1)} %get-tuple-element.37.pb, bf16[2,4,48,512]{3,2,1,0:T(8,128)(2,1)} %get-tuple-element.38.ps, ...), custom_call_target="tpu_custom_call" | custom-call | tf_op jit(solution)/shard_map/input_grads/pallas_call | solution.py:1282

commit v6 on v5

--- a/solution.py
+++ b/solution.py
@@ -203,7 +203,7 @@
         self.orders = (bits, bits[::-1])
         self.levels = len(bits)
         self.wrows = self.by_modes.modes // 2 * C
-        self.pieces = 4
+        self.pieces = 6
         self.zrows = self.wrows // self.pieces
         assert self.nz % 2 == 0 and self.zrows % 16 == 0
 
@@ -1117,7 +1117,7 @@
         waves = ex.waves(chunk_total)
         first = plan.levels - 1
         for w, wave in enumerate(waves):
-            step = 2 + 2 * w
+            step = (2, 3, 4, 6, 9, 12)[w] if w < 6 else last
             items += [(step, task) for task in wave]
             for lag, task in enumerate((weight_grad, sum_weights, cross_weights)):
                 if lag and 0 <= w - first - lag < lay.chunks:

time: 165 us -> 165 us (level)
  no operation moved by 1% of the time
where the time goes in v6:
time: 165 us; the launch traced here: 164 us
  Pallas kernels  164 us (99%)
    pallas_call x1, Pallas kernels, backward_kernel(): pl.pallas_call(kernel, grid=(plan.count,), in_specs=[ANYWHERE, plain_fiel...  49.1 us
    pallas_call x1, Pallas kernels, cells_pass(): pl.pallas_call(body, grid_spec=pltpu.PrefetchScalarGridSpec(num_scalar_pr...  43.1 us
    pallas_call x1, Pallas kernels, forward_kernel(): pl.pallas_call(kernel, grid=(last + 1,), in_specs=[ANYWHERE, plain_fields...  42.9 us
    pallas_call x1, Pallas kernels, input_grads(): pl.pallas_call(body, grid_spec=pltpu.PrefetchScalarGridSpec(num_scalar_pr...  28.4 us

profile of v6, /device:TPU:0, one launch (start us, length us, event | category | flops | bytes accessed | tf_op | source)
XLA Modules:
  0.0 164.4 jit_solution(13629766143425675809)
XLA Ops:
  0.6 42.9 %mode_forward.1 = (bf16[4,2,480,384]{3,2,1,0:T(8,128)(2,1)}, bf16[32,256,256]{2,1,0:T(8,128)(2,1)}, bf16[480,384]{1,0:T(8,128)(2,1)}) custom-call(bf16[28,4,48,2048]{3,2,1,0:T(8,128)(2,1)} %xb.1, bf16[2,4,48,512]{3,2,1,0:T(8,128)(2,1)} %xs.3, bf16[1024,256]{1,0:T(8,128)(2,1)} %constant.44.clone.fb, bf16[512,256]{1,0:T(8,128)(2,1)} %constant.45.clone.fs, ...), custom_call_target="tpu_custom_call" | custom-call | tf_op jit(solution)/shard_map/mode_forward/pallas_call | solution.py:670
  43.6 43.1 %cells.1 = (bf16[28,4,48,2048]{3,2,1,0:T(8,128)(2,1)}, bf16[2,4,48,512]{3,2,1,0:T(8,128)(2,1)}, bf16[28,4,48,2048]{3,2,1,0:T(8,128)(2,1)}, bf16[2,4,48,512]{3,2,...) custom-call(s32[1]{0:T(128)} %bitcast.r, ...), custom_call_target="tpu_custom_call" | custom-call | tf_op jit(solution)/shard_map/cells/pallas_call | solution.py:858
  86.7 49.1 %mode_backward.1 = (bf16[28,4,48,2048]{3,2,1,0:T(8,128)(2,1)}, bf16[2,4,48,512]{3,2,1,0:T(8,128)(2,1)}, bf16[4,2,480,384]{3,2,1,0:T(8,128)(2,1)}, bf16[768,384]{1,0:T(8,128)(2,1)}, f32[56,192]{1,0:T(8,128)}) custom-call(bf16[28,4,48,2048]{3,2,1,0:T(8,128)(2,1)} %get-tuple-element.30.pb, bf16[2,4,48,512]{3,2,1,0:T(8,128)(2,1)} %get-tuple-element.31.ps, ...), custom_call_target="tpu_custom_call" | custom-call | tf_op jit(solution)/shard_map/mode_backward/pallas_call | solution.py:1150
  135.9 28.4 %input_grads.1 = (f32[28,4,48,2048]{3,2,1,0:T(8,128)}, f32[2,4,48,512]{3,2,1,0:T(8,128)}, f32[4,48,48]{2,1,0:T(8,128)}, f32[4,48]{1,0:T(4,128)}, f32[32,4,48,48]{3,2,1,0:T(8,128)}) custom-call(s32[1]{0:T(128)} %bitcast.r, bf16[28,4,48,2048]{3,2,1,0:T(8,128)(2,1)} %get-tuple-element.37.pb, bf16[2,4,48,512]{3,2,1,0:T(8,128)(2,1)} %get-tuple-element.38.ps, ...), custom_call_target="tpu_custom_call" | custom-call | tf_op jit(solution)/shard_map/input_grads/pallas_call | solution.py:1282
